TPU v7x, 128 devices: a whole 4x4x4 slice. The times are simulated.
128 devices in a mesh: row: 16 (over x, y_lo, core), col: 8 (over y_hi, z).
Axes of the slice: x: 4, y: 4 (y_hi: 2, y_lo: 2; y = y_hi * 2 + y_lo), z: 4, core: 2. Of those that a mesh axis runs over, the one named last changes fastest.
Arguments:
- corr: float32 [2, 9216, 9216], P(None, 'row', 'col'), may hold values from -1.8 to 1.8, as said below
- bonds_down: float32 [96, 96], replicated, may hold values from 0.5 to 1.5
- bonds_across: float32 [96, 96], replicated, may hold values from 0.5 to 1.5
- repulsion: float32 [96, 96], replicated, may hold values from 1 to 4
Outputs:
- corr_next: float32 [2, 9216, 9216], P(None, 'row', 'col')
Inputs may be any that keep to these rules, and one draw needn't show every extreme that they name: `corr`: the real part's diagonal entries lie between 0 and 1.
All inputs are finite; a program needn't handle non-finite values.
Results may differ from a plain program's by a relative error of at most 0.00002.
Values sent between devices are 32-bit elements; how exact they have to be, the bound alone decides.
No kernel may reach another device: no remote copies, remote signals or barrier semaphores. Data moves between devices by JAX's collectives and lax.ppermute only.
A program may use at most 192 MiB of HBM per device.

v0:
```python
import functools

import jax
import jax.numpy as jnp
from jax import lax
from jax.experimental import pallas as pl
from jax.experimental.pallas import tpu as pltpu
from jax.sharding import PartitionSpec as P

PATCH = 24
SQUARE = PATCH * PATCH
COLUMNS = 2 * SQUARE
LANES = 128
TILES = COLUMNS // LANES
LATTICE = 4 * PATCH
TIME_STEP = 0.04
F32 = jnp.float32
VMEM_LIMIT = 8 * 1024 * 1024

DN_IN, UP_IN, RT_IN, LF_IN, DN_RIM, UP_RIM, RT_RIM, LF_RIM, ROW_U = range(9)
C_DN, C_UP, C_RT, C_LF, C_DN_RIM, C_UP_RIM, C_RT_E, C_RT_F, C_LF_E, C_LF_F, C_X_E, C_X_F, COL_U = range(13)


def iota(shape, dim):
    return lax.broadcasted_iota(jnp.int32, shape, dim)


def over24(x):
    return ((x.astype(F32) + 0.5) * (1.0 / PATCH)).astype(jnp.int32)


def on(mask):
    return jnp.where(mask, 1.0, 0.0).astype(F32)


def within(x, lo, hi):
    return on(x >= lo) * on(x <= hi)


def place():
    return lax.axis_index("row"), lax.axis_index("col")


def tile(t):
    return pl.ds(t * LANES, LANES)


def weights_kernel(down_ref, across_ref, rep_ref, roww, colw):
    row_id, col_id = place()
    side = (LATTICE, LATTICE)
    down = jnp.where(iota(side, 0) < LATTICE - 1, down_ref[...], 0.0)
    across = jnp.where(iota(side, 1) < LATTICE - 1, across_ref[...], 0.0)
    rep = rep_ref[...]
    dot = functools.partial(jnp.dot, precision=lax.Precision.HIGHEST, preferred_element_type=F32)

    s = iota((SQUARE, LATTICE), 0)
    lane = iota((SQUARE, LATTICE), 1)
    a = over24(s)
    b = s - PATCH * a
    ga = PATCH * (row_id // 4) + a
    gb = PATCH * (row_id % 4) + b

    def pick_rows(table, da, db):
        rows = dot(on(lane == ga + da), table)
        return jnp.sum(jnp.where(lane == gb + db, rows, 0.0), axis=1, keepdims=True)

    a1 = a[:, 0:1]
    b1 = b[:, 0:1]
    last = PATCH - 1
    dn = -TIME_STEP * pick_rows(down, 0, 0)
    up = -TIME_STEP * pick_rows(down, -1, 0)
    rt = -TIME_STEP * pick_rows(across, 0, 0)
    lf = -TIME_STEP * pick_rows(across, 0, -1)
    values = {
        DN_IN: dn * on(a1 < last), UP_IN: up * on(a1 > 0), RT_IN: rt * on(b1 < last), LF_IN: lf * on(b1 > 0),
        DN_RIM: dn * on(a1 == last), UP_RIM: up * on(a1 == 0), RT_RIM: rt * on(b1 == last), LF_RIM: lf * on(b1 == 0),
        ROW_U: TIME_STEP * pick_rows(rep, 0, 0),
    }
    for k, v in values.items():
        roww[k] = jnp.broadcast_to(v, (SQUARE, LANES))

    wide = (LATTICE, COLUMNS)
    j = iota(wide, 1)
    g = (j >= SQUARE).astype(jnp.int32)
    jj = j - SQUARE * g
    a = over24(jj)
    b = jj - PATCH * a
    sub = iota(wide, 0)
    parity = col_id % 2
    ga = PATCH * (col_id // 2) + a
    gb = PATCH * (2 * parity + g) + b

    def pick_cols(table, da, db):
        cols = dot(table, on(sub == gb + db))
        return jnp.sum(jnp.where(sub == ga + da, cols, 0.0), axis=0, keepdims=True)

    a = a[0:1]
    b = b[0:1]
    g = g[0:1]
    dn = TIME_STEP * pick_cols(down, 0, 0)
    up = TIME_STEP * pick_cols(down, -1, 0)
    rt = TIME_STEP * pick_cols(across, 0, 0)
    lf = TIME_STEP * pick_cols(across, 0, -1)
    tails0 = rt * on(b == last) * on(g == 0)
    heads1 = lf * on(b == 0) * on(g == 1)
    tails1 = rt * on(b == last) * on(g == 1)
    heads0 = lf * on(b == 0) * on(g == 0)
    even = on(jnp.full(a.shape, parity, jnp.int32) == 0)
    x_even = even * tails1
    x_odd = (1.0 - even) * heads0
    rt_e = within(a, 3, 18)
    lf_e = within(a, 5, 20)
    xe_e = within(a, 6, 21)
    xo_e = within(a, 2, 17)
    values = {
        C_DN: dn * on(a < last), C_UP: up * on(a > 0), C_RT: rt * on(b < last), C_LF: lf * on(b > 0),
        C_DN_RIM: dn * on(a == last), C_UP_RIM: up * on(a == 0),
        C_RT_E: tails0 * rt_e, C_RT_F: tails0 * (1.0 - rt_e),
        C_LF_E: heads1 * lf_e, C_LF_F: heads1 * (1.0 - lf_e),
        C_X_E: x_even * xe_e + x_odd * xo_e, C_X_F: x_even * (1.0 - xe_e) + x_odd * (1.0 - xo_e),
        COL_U: TIME_STEP * pick_cols(rep, 0, 0),
    }
    for k, v in values.items():
        colw[k] = jnp.broadcast_to(v, (8, COLUMNS))


STRIP = (PATCH, LANES)


def squeeze_cols(tiles, lane24, m1, m2, n0):
    e = jnp.where(lane24 == m1, tiles[1], jnp.where(lane24 == m2, tiles[2], tiles[3]))
    f = jnp.where(lane24 == n0, tiles[0], tiles[4])
    return e, f


def lane_maps(shape=STRIP):
    lane = iota(shape, 1)
    return lane, lane - PATCH * over24(lane)


def parities():
    row_id, col_id = place()
    return lax.rem(col_id // 2, 2) == 0, lax.rem(col_id, 2) == 0, lax.rem(row_id // 4, 2) == 0, lax.rem(row_id, 2) == 0


FOLDS = (((0, 24, 16), (16, 88, 8), (40, 96, 8)), ((48, 24, 16), (64, 88, 16)), ((80, 24, 8), (104, 32, 8), (112, 88, 16)))
QUARTER = SQUARE // 4


def pack_faces(src, face_a, face_b, side, down_a, down_b, across_a, across_b, diag):
    up_first, even, row_up_first, row_even = parities()
    base = jnp.where(even, 4 * LANES, 0)
    lane, lane24 = lane_maps()
    lane8 = lax.rem(lane, 8)
    m1 = jnp.where(even, 7, 16)
    m2 = jnp.where(even, 23, 8)
    n0 = jnp.where(even, 15, 0)
    v0 = jnp.where(even, 7, 0)
    low = lane < 64
    half = lax.rem(lane, 64)
    first_part = half < PATCH
    last_part = half >= 64 - PATCH

    def faces(rows):
        edge = [[src[p, rows, tile(t)] for t in (0, 4, 8)] for p in range(2)]
        top = [jnp.where(low, e[0], e[1]) for e in edge]
        bot = [jnp.where(low, e[1], e[2]) for e in edge]
        top = jnp.where(last_part, pltpu.roll(top[0], 40, 1), top[1])
        bot = jnp.where(first_part, pltpu.roll(bot[0], 88, 1), bot[1])
        return jnp.where(up_first, bot, top), jnp.where(up_first, top, bot)

    def squeezed(rows):
        out = []
        for p in range(2):
            tiles = [src[p, rows, pl.ds(pl.multiple_of(base + LANES * t, LANES), LANES)] for t in range(5)]
            out += squeeze_cols(tiles, lane24, m1, m2, n0)
        return out

    def step(k, carry):
        at = [pl.ds(pl.multiple_of(q * QUARTER + k * PATCH, 8), PATCH) for q in range(4)]
        whole = [faces(rows) for rows in at]
        for n, msg in enumerate((face_a, face_b)):
            turned = {d: pltpu.roll(whole[3][n], d, 1) for d in (24, 56, 72, 104)}
            for q in range(3):
                value = whole[q][n]
                for source, to, count in FOLDS[q]:
                    value = jnp.where(jnp.logical_and(lane >= to, lane < to + count), turned[(to - source) % LANES], value)
                msg[at[q], :] = value
        for h in range(2):
            msg = None
            for slot, v in enumerate(squeezed(at[h]) + squeezed(at[h + 2])):
                msg = v if slot == 0 else jnp.where(lane8 == lax.rem(v0 + slot, 8), pltpu.roll(v, slot, 1), msg)
            side[at[h], :] = msg
        return carry

    lax.fori_loop(0, PATCH // 4, step, 0)
    for p in range(2):
        for out, flip in ((down_a, row_up_first), (down_b, jnp.logical_not(row_up_first))):
            out[p] = src[p, pl.ds(pl.multiple_of(jnp.where(flip, SQUARE - PATCH, 0), 8), PATCH), :]
        for a in range(PATCH):
            left = src[p, a * PATCH : a * PATCH + 1, :]
            right = src[p, a * PATCH + PATCH - 1 : a * PATCH + PATCH, :]
            across_a[p, a : a + 1, :] = jnp.where(row_even, right, left)
            across_b[p, a : a + 1, :] = jnp.where(row_even, left, right)
    pack_diag(src, diag)


def pack_diag(src, diag):
    row_id, col_id = place()
    diag[...] = jnp.zeros(diag.shape, F32)

    @pl.when(row_id // 2 == col_id)
    def _():
        odd = row_id % 2
        lane = iota((8, LANES), 1) - iota((8, LANES), 0)
        for t in range(5):
            total = jnp.zeros((8, LANES), F32)
            first = t * LANES - 64 * odd
            for k in range(LANES // 8):
                row = first + 8 * k
                inside = jnp.logical_and(row >= 0, row < SQUARE)
                at = pl.multiple_of(jnp.clip(row, 0, SQUARE - 8), 8)
                value = src[0, pl.ds(at, 8), pl.ds(pl.multiple_of((4 * odd + t) * LANES, LANES), LANES)]
                total = total + jnp.where(jnp.logical_and(lane == 8 * k, inside), value, 0.0)
            diag[pl.ds(4 * odd + t, 1), :] = jnp.sum(total, axis=0, keepdims=True)


def hop_strip(src, q, a, roww, colw):
    sub = iota((8, LANES), 0)
    lane, lane24 = lane_maps((8, LANES))
    here = pl.multiple_of(a * PATCH, 8)
    above = pl.multiple_of(jnp.maximum(a - 1, 0) * PATCH, 8)
    below = pl.multiple_of(jnp.minimum(a + 1, PATCH - 1) * PATCH, 8)
    x = [[src[q, pl.ds(here + 8 * k, 8), tile(t)] for t in range(TILES)] for k in range(3)]
    out = [[None] * TILES for _ in range(3)]
    rw = [[roww[n, pl.ds(here + 8 * k, 8), :] for n in (DN_IN, UP_IN, RT_IN, LF_IN)] for k in range(3)]
    for t in range(TILES):
        fwd = [pltpu.roll(x[k][t], 1, 0) for k in range(3)]
        bwd = [pltpu.roll(x[k][t], 7, 0) for k in range(3)]
        for k in range(3):
            left = fwd[0] if k == 0 else jnp.where(sub == 0, fwd[k - 1], fwd[k])
            right = bwd[2] if k == 2 else jnp.where(sub == 7, bwd[k + 1], bwd[k])
            dn, up, rt, lf = rw[k]
            out[k][t] = (
                dn * src[q, pl.ds(below + 8 * k, 8), tile(t)]
                + up * src[q, pl.ds(above + 8 * k, 8), tile(t)]
                + rt * right
                + lf * left
            )
    for k in range(3):
        row = x[k]
        r1 = [pltpu.roll(v, 1, 1) for v in row]
        l1 = [pltpu.roll(v, LANES - 1, 1) for v in row]
        r24 = [pltpu.roll(v, PATCH, 1) for v in row]
        l24 = [pltpu.roll(v, LANES - PATCH, 1) for v in row]
        te, tf = [pltpu.roll(v, 41, 1) for v in squeeze_cols(row[0:5], lane24, 15, 7, 23)]
        he, hf = [pltpu.roll(v, 87, 1) for v in squeeze_cols(row[4:9], lane24, 8, 0, 16)]
        for t in range(TILES):
            w = lambda n: colw[n, :, tile(t)]
            minus_b = r1[t] if t == 0 else jnp.where(lane < 1, r1[t - 1], r1[t])
            plus_b = l1[t] if t == TILES - 1 else jnp.where(lane >= LANES - 1, l1[t + 1], l1[t])
            minus_a = r24[t] if t == 0 else jnp.where(lane < PATCH, r24[t - 1], r24[t])
            plus_a = l24[t] if t == TILES - 1 else jnp.where(lane >= LANES - PATCH, l24[t + 1], l24[t])
            acc = out[k][t] + w(C_DN) * plus_a + w(C_UP) * minus_a + w(C_RT) * plus_b + w(C_LF) * minus_b
            if t <= 3:
                acc = acc + w(C_RT_E) * he
            if t in (0, 3, 4):
                acc = acc + w(C_RT_F) * hf
            if 5 <= t <= 8:
                acc = acc + w(C_LF_E) * te
            if t in (4, 5, 8):
                acc = acc + w(C_LF_F) * tf
            out[k][t] = acc
    return out


def interior_kernel(final, first, last, *refs):
    y1, y, roww, colw, out = refs[-5:]

    def step(a, carry):
        here = pl.multiple_of(a * PATCH, 8)
        for p in range(2):
            hops = hop_strip(y1, 1 - p, a, roww, colw)
            for k in range(3):
                rows = pl.ds(here + 8 * k, 8)
                for t in range(TILES):
                    old = y1[p, rows, tile(t)]
                    if final:
                        old = old + y[p, rows, tile(t)]
                    new = old + hops[k][t] if p == 0 else old - hops[k][t]
                    out[p, rows, tile(t)] = 0.5 * new if final else new
        return carry

    lax.fori_loop(first, last, step, 0)


def unfolded(msg, at, lane):
    value = None
    for q in range(3):
        carrier = msg[pl.ds(pl.multiple_of(q * QUARTER + at, 8), 8), :]
        for source, to, count in FOLDS[q]:
            turned = pltpu.roll(carrier, (source - to) % LANES, 1)
            inside = jnp.logical_and(lane >= source, lane < source + count)
            value = turned if value is None else jnp.where(inside, turned, value)
    return value


def finish(scale, base, y, halos, roww, colw, out, e_row, e_col, chunk_done=None):
    face_a, face_b, side, down_a, down_b, across_a, across_b, col_diag, row_diag = halos
    row_id, col_id = place()
    up_first, even, row_up_first, row_even = parities()
    row_odd = lax.rem(row_id, 2)
    shift = jnp.where(even, 87, 41)
    lane = iota((8, LANES), 1)
    for t in range(5):
        strip = jnp.where(row_odd == 1, row_diag[4 + t : 5 + t, :], row_diag[t : t + 1, :])
        e_row[t * LANES : (t + 1) * LANES, :] = jnp.broadcast_to(strip, (LANES, LANES)).T
    for t in range(TILES):
        e_col[:, tile(t)] = col_diag[t : t + 1, :] * colw[COL_U, :, tile(t)]

    def strip(a, folded):
        here = pl.multiple_of(a * PATCH, 8)
        near = pl.ds(pl.multiple_of(8 * (a // 8), 8), 8)
        to_first = lax.rem(8 - lax.rem(a, 8), 8)
        to_last = 7 - lax.rem(a, 8)
        half = a // (PATCH // 2)
        for k in range(3):
            rows = pl.ds(here + 8 * k, 8)
            es = e_row[pl.ds(64 * row_odd + here + 8 * k, 8), :] * roww[ROW_U, rows, :]
            if folded:
                got = [unfolded(m, here - 3 * QUARTER + 8 * k, lane) for m in (face_a, face_b)]
            else:
                got = [m[rows, :] for m in (face_a, face_b)]
            lower = jnp.where(up_first, got[0], got[1])
            upper = jnp.where(up_first, got[1], got[0])
            lowers = (lower, pltpu.roll(lower, 40, 1))
            uppers = (upper, pltpu.roll(upper, 88, 1))
            packed = side[pl.ds(pl.multiple_of(here - half * (SQUARE // 2), 8) + 8 * k, 8), :]
            gaps = [es - e_col[:, tile(t)] for t in range(TILES)]
            for p in range(2):
                q = 1 - p
                se, sf = [pltpu.roll(packed, lax.rem(shift + LANES - (4 * half + 2 * q + n), LANES), 1) for n in range(2)]
                for t in range(TILES):
                    w = lambda n: colw[n, :, tile(t)]
                    acc = gaps[t] * y[q, rows, tile(t)]
                    if t in (0, 4):
                        acc = acc + w(C_UP_RIM) * uppers[q]
                    if t in (4, 8):
                        acc = acc + w(C_DN_RIM) * lowers[q]
                    if t != 4:
                        acc = acc + w(C_X_E) * se
                    if t in (0, 3, 4, 5, 8):
                        acc = acc + w(C_X_F) * sf
                    if k != 1:
                        pair = [m[q, near, tile(t)] for m in (across_a, across_b)]
                    if k == 0:
                        left = pltpu.roll(jnp.where(row_even, pair[1], pair[0]), to_first, 0)
                        acc = acc + roww[LF_RIM, rows, :] * left
                    if k == 2:
                        right = pltpu.roll(jnp.where(row_even, pair[0], pair[1]), to_last, 0)
                        acc = acc + roww[RT_RIM, rows, :] * right
                    if scale != 1.0:
                        acc = scale * acc
                    old = base[p, rows, tile(t)]
                    out[p, rows, tile(t)] = old + acc if p == 0 else old - acc

    def rim(a, weight, first, second):
        for p in range(2):
            for k in range(3):
                rows = pl.ds(a * PATCH + 8 * k, 8)
                w = roww[weight, rows, :] * (scale if p == 0 else -scale)
                for t in range(TILES):
                    pair = [m[1 - p, 8 * k : 8 * k + 8, tile(t)] for m in (first, second)]
                    out[p, rows, tile(t)] += w * jnp.where(row_up_first, pair[0], pair[1])

    fold = 3 * PATCH // 4
    lax.fori_loop(0, fold, lambda a, c: (strip(a, False), c)[1], 0)
    rim(0, UP_RIM, down_b, down_a)
    if chunk_done is not None:
        chunk_done(0, fold * PATCH)
    lax.fori_loop(fold, PATCH, lambda a, c: (strip(a, True), c)[1], 0)
    rim(PATCH - 1, DN_RIM, down_a, down_b)
    if chunk_done is not None:
        chunk_done(fold * PATCH, SQUARE)


def middle_kernel(base, y, *refs):
    halos, (roww, colw), (y1, *faces), (e_row, e_col) = refs[:9], refs[9:11], refs[11:20], refs[20:]
    finish(1.0, base, y, halos, roww, colw, y1, e_row, e_col)
    pack_faces(y1, *faces)


def last_kernel(base, y1, *refs):
    halos, (roww, colw), out_hbm, (e_row, e_col, out, sems) = refs[:9], refs[9:11], refs[11], refs[12:]
    copies = []

    def chunk_done(first, last):
        for p in range(2):
            rows = pl.ds(first, last - first)
            copies.append(pltpu.make_async_copy(out.at[p, rows], out_hbm.at[p, rows], sems.at[len(copies)]))
            copies[-1].start()

    finish(0.5, base, y1, halos, roww, colw, out, e_row, e_col, chunk_done)
    for c in copies:
        c.wait()


def on_chip(*shape):
    return pltpu.VMEM(shape, F32)


VM = pl.BlockSpec(memory_space=pltpu.VMEM)
STATE = (2, SQUARE, COLUMNS)
FACES = (((3 * QUARTER, LANES),) * 2 + ((SQUARE // 2, LANES),) + ((2, PATCH, COLUMNS),) * 4 + ((16, LANES),))


def call(kernel, args, out_shapes, scratch=(), flops=1000, out_specs=None, aliases=None):
    many = isinstance(out_shapes, (list, tuple))
    return pl.pallas_call(
        kernel,
        out_shape=out_shapes,
        in_specs=[VM] * len(args),
        out_specs=out_specs or ([VM] * len(out_shapes) if many else VM),
        scratch_shapes=list(scratch),
        input_output_aliases=aliases or {},
        compiler_params=pltpu.CompilerParams(vmem_limit_bytes=VMEM_LIMIT),
        cost_estimate=pl.CostEstimate(flops=flops, bytes_accessed=1000, transcendentals=0),
    )(*[pltpu.with_memory_space_constraint(x, pltpu.VMEM) for x in args])


def pairs(axis, linked):
    n = lax.axis_size(axis)
    found = [(i, j) for i in range(n) for j in range(i + 1, n) if linked(i, j)]
    return found + [(j, i) for i, j in found]


def traded(block, axis, linked):
    return lax.ppermute(block, axis, pairs(axis, linked))


def flipped(block, axis, bit):
    return traded(block, axis, lambda i, j: j == i ^ bit)


def tie(value, *after):
    def kernel(*refs):
        refs[-1][...] = refs[0][...]

    return call(kernel, (value, *after), on_chip(*value.shape), flops=0)


def exchange(faces, piece):
    face_a, face_b, side, down_a, down_b, across_a, across_b, diag = faces
    face_a = flipped(face_a, "col", 2)
    face_b = traded(face_b, "col", lambda i, j: j == i + 2 and (i // 2) % 2 == 1)
    side = flipped(side, "col", 1)
    down_a = flipped(down_a, "row", 4)
    down_b = traded(down_b, "row", lambda i, j: j == i + 4 and (i // 4) % 2 == 1)
    col_diag = diag + flipped(diag, "row", 4)
    row_diag = diag + flipped(diag, "col", 4)
    part = piece(0, None)
    col_diag = tie(col_diag, part)
    col_got = flipped(col_diag, "row", 8)
    part = piece(1, part, col_diag, row_diag)
    col_diag = tie(col_diag + col_got, part, side)
    col_got = flipped(col_diag, "row", 1)
    part = piece(2, part, col_diag)
    across_a = flipped(tie(across_a, part), "row", 1)
    across_b = traded(tie(across_b, part), "row", lambda i, j: j == i + 1 and i % 4 == 1)
    col_diag = tie(col_diag + col_got, part)
    col_diag = col_diag + flipped(col_diag, "row", 2)
    row_diag = tie(row_diag, face_a, face_b, part)
    row_got = flipped(row_diag, "col", 1)
    part = piece(3, part, row_diag)
    row_diag = row_diag + row_got
    row_diag = row_diag + flipped(row_diag, "col", 2)
    return part, (face_a, face_b, side, down_a, down_b, across_a, across_b, col_diag, row_diag)


PIECES = 4


def interior(final, y1, y, weights):
    def piece(n, part, *after):
        step = PATCH // PIECES
        kernel = functools.partial(interior_kernel, final, n * step, (n + 1) * step)
        args = (*after, y1, y, *weights)
        if n == 0:
            return call(kernel, args, on_chip(*STATE))
        return call(kernel, (part, *args), on_chip(*STATE), aliases={0: 0})

    return piece


def local(corr, bonds_down, bonds_across, repulsion):
    faces_out = [on_chip(*s) for s in FACES]
    e_scratch = [pltpu.VMEM((5 * LANES, LANES), F32), pltpu.VMEM((8, COLUMNS), F32)]
    weights = call(
        weights_kernel,
        (bonds_down, bonds_across, repulsion),
        [on_chip(9, SQUARE, LANES), on_chip(13, 8, COLUMNS)],
    )
    faces = call(pack_faces, (corr,), faces_out)
    part, halos = exchange(faces, interior(False, corr, corr, weights))
    y1, *faces = call(middle_kernel, (part, corr, *halos, *weights), [on_chip(*STATE), *faces_out], e_scratch)
    part, halos = exchange(faces, interior(True, y1, corr, weights))
    return call(
        last_kernel,
        (part, y1, *halos, *weights),
        jax.ShapeDtypeStruct(STATE, F32),
        [*e_scratch, pltpu.VMEM(STATE, F32), pltpu.SemaphoreType.DMA((4,))],
        out_specs=pl.BlockSpec(memory_space=pl.ANY),
    )


def solution(mesh):
    in_specs = (P(None, "row", "col"), P(), P(), P())
    out_specs = P(None, "row", "col")
    return jax.shard_map(local, mesh=mesh, in_specs=in_specs, out_specs=out_specs, check_vma=False)
```

profile of v0, /device:TPU:0, one launch (start us, length us, event | category | flops | bytes accessed | tf_op | source)
XLA Modules:
  0.0 100.8 jit_solution(4881592289035682476)
XLA Ops:
  0.0 2.5 %copy-done = f32[2,576,1152]{2,1,0:T(8,128)S(1)} copy-done((f32[2,576,1152]{2,1,0:T(8,128)S(1)}, f32[2,576,1152]{2,1,0:T(8,128)}, u32[]{:S(2)}) %copy-start) | copy-done | bytes 5308440
  4.2 3.2 %collective-permute-start.1 = (f32[16,128]{1,0:T(8,128)S(1)}, f32[16,128]{1,0:T(8,128)S(1)}, u32[]{:S(2)}, u32[]{:S(2)}) collective-permute-start(f32[16,128]{1,0:T(8,128)S(1)} %get-tuple-element.26), channel_id=1, source_target_pairs={{0,4},{1,5},{2,6},{3,7},{4,0},{5,1},{6,2},{7,3},{8,12},{9,13},{10,... | collective-permute-start | bytes 24584 | tf_op jit(solution)/shard_map/ppermute | solution.py:438
  10.7 3.6 %collective-permute-start.4 = (f32[432,128]{1,0:T(8,128)S(1)}, f32[432,128]{1,0:T(8,128)S(1)}, u32[]{:S(2)}, u32[]{:S(2)}) collective-permute-start(f32[432,128]{1,0:T(8,128)S(1)} %get-tuple-element.28), channel_id=1, source_target_pairs={{0,2},{1,3},{4,6},{5,7},{2,0},{3,1},{6,4},{7,5},{8,10},{9,11},{12,... | collective-permute-start | bytes 663560 | tf_op jit(solution)/shard_map/ppermute | solution.py:438
  17.4 3.0 %shard_map.46 = (f32[9,576,128]{2,1,0:T(8,128)S(1)}, f32[13,8,1152]{2,1,0:T(8,128)S(1)}) custom-call(f32[96,96]{1,0:T(8,128)S(1)} %copy-done.2, f32[96,96]{1,0:T(8,128)S(1)} %copy-done.3, f32[96,96]{1,0:T(8,128)S(1)} %copy-done.4), custom_call_target="tpu_custom_call" | custom-call | flops 1000 | bytes 1000 | tf_op jit(solution)/shard_map/pallas_call | solution.py:419
  20.4 2.2 %shard_map.47.refs_1_.refs_0_ = f32[2,576,1152]{2,1,0:T(8,128)S(1)} custom-call(f32[2,576,1152]{2,1,0:T(8,128)S(1)} %copy-done.1, f32[2,576,1152]{2,1,0:T(8,128)S(1)} %copy-done.1, f32[9,576,128]{2,1,0:T(8,128)S(1)} %get-tuple-element.24.refs_2_.refs_5_.refs_4_.refs_9_, f32[13,8,1152]{2,1,0:T(8,128)S(1)} %get-tuple-element.25.refs_3_.refs_6_.refs_5_.refs_10_), custom_call_target="tpu_custom_call" | custom-call | flops 1000 | bytes 1000 | tf_op jit(solution)/shard_map/pallas_call | solution.py:419
  22.6 2.8 %collective-permute-start.2 = (f32[16,128]{1,0:T(8,128)S(1)}, f32[16,128]{1,0:T(8,128)S(1)}, u32[]{:S(2)}, u32[]{:S(2)}) collective-permute-start(f32[16,128]{1,0:T(8,128)S(1)} %shard_map.49.refs_1_), channel_id=1, source_target_pairs={{0,64},{8,72},{16,80},{24,88},{32,96},{40,104},{48,112},{56,120},{... | collective-permute-start | bytes 24584 | tf_op jit(solution)/shard_map/ppermute | solution.py:438
  25.6 2.2 %shard_map.50.refs_1_.refs_0_ = f32[2,576,1152]{2,1,0:T(8,128)S(1)} custom-call(f32[2,576,1152]{2,1,0:T(8,128)S(1)} %shard_map.47.refs_1_.refs_0_, f32[16,128]{1,0:T(8,128)S(1)} %shard_map.49.refs_1_, f32[16,128]{1,0:T(8,128)S(1)} %get-tuple-element.45.refs_2_.refs_0_, f32[2,576,1152]{2,1,0:T(8,128)S(1)} %copy-done.1, ...), custom_call_target="tpu_custom_call", output_to_operand_aliasing={{}: (0, {})} | custom-call | flops 1000 | bytes 1000 | tf_op jit(solution)/shard_map/pallas_call | solution.py:419
  28.6 2.2 %shard_map.52.refs_3_.refs_0_.refs_1_ = f32[2,576,1152]{2,1,0:T(8,128)S(1)} custom-call(f32[2,576,1152]{2,1,0:T(8,128)S(1)} %shard_map.50.refs_1_.refs_0_, f32[16,128]{1,0:T(8,128)S(1)} %shard_map.51.refs_1_, f32[2,576,1152]{2,1,0:T(8,128)S(1)} %copy-done.1, f32[2,576,1152]{2,1,0:T(8,128)S(1)} %copy-done.1, ...), custom_call_target="tpu_custom_call", output_to_operand_aliasing={{}: (0, {})} | custom-call | flops 1000 | bytes 1000 | tf_op jit(solution)/shard_map/pallas_call | solution.py:419
  31.7 2.1 %collective-permute-start.10 = (f32[16,128]{1,0:T(8,128)S(1)}, f32[16,128]{1,0:T(8,128)S(1)}, u32[]{:S(2)}, u32[]{:S(2)}) collective-permute-start(f32[16,128]{1,0:T(8,128)S(1)} %shard_map.51.refs_1_), channel_id=1, source_target_pairs={{0,8},{16,24},{32,40},{48,56},{64,72},{80,88},{96,104},{112,120},{... | collective-permute-start | bytes 24584 | tf_op jit(solution)/shard_map/ppermute | solution.py:438
  34.6 3.6 %collective-permute-done.12 = f32[16,128]{1,0:T(8,128)S(1)} collective-permute-done((f32[16,128]{1,0:T(8,128)S(1)}, f32[16,128]{1,0:T(8,128)S(1)}, u32[]{:S(2)}, u32[]{:S(2)}) %collective-permute-start.12) | collective-permute-done | bytes 8224 | tf_op jit(solution)/shard_map/ppermute | solution.py:438
  41.9 5.6 %collective-permute-start.13 = (f32[16,128]{1,0:T(8,128)S(1)}, f32[16,128]{1,0:T(8,128)S(1)}, u32[]{:S(2)}, u32[]{:S(2)}) collective-permute-start(f32[16,128]{1,0:T(8,128)S(1)} %add.47), channel_id=1, source_target_pairs={{0,2},{1,3},{4,6},{5,7},{2,0},{3,1},{6,4},{7,5},{8,10},{9,11},{12,... | collective-permute-start | bytes 24584 | tf_op jit(solution)/shard_map/ppermute | solution.py:438
  47.6 2.2 %shard_map.54.base = f32[2,576,1152]{2,1,0:T(8,128)S(1)} custom-call(f32[2,576,1152]{2,1,0:T(8,128)S(1)} %shard_map.52.refs_3_.refs_0_.refs_1_, f32[16,128]{1,0:T(8,128)S(1)} %shard_map.53.refs_1_, f32[2,576,1152]{2,1,0:T(8,128)S(1)} %copy-done.1, f32[2,576,1152]{2,1,0:T(8,128)S(1)} %copy-done.1, ...), custom_call_target="tpu_custom_call", output_to_operand_aliasing={{}: (0, {})} | custom-call | flops 1000 | bytes 1000 | tf_op jit(solution)/shard_map/pallas_call | solution.py:419
  49.8 5.8 %shard_map.58 = (f32[2,576,1152]{2,1,0:T(8,128)S(1)}, f32[432,128]{1,0:T(8,128)S(1)}, f32[432,128]{1,0:T(8,128)S(1)}, f32[288,128]{1,0:T(8,128)S(1)}, f32[2,24,1...) custom-call(f32[2,576,1152]{2,1,0:T(8,128)S(1)} %shard_map.54.base, ...), custom_call_target="tpu_custom_call" | custom-call | flops 1000 | bytes 1000 | tf_op jit(solution)/shard_map/pallas_call | solution.py:419
  55.6 2.0 %collective-permute-start.15 = (f32[16,128]{1,0:T(8,128)S(1)}, f32[16,128]{1,0:T(8,128)S(1)}, u32[]{:S(2)}, u32[]{:S(2)}) collective-permute-start(f32[16,128]{1,0:T(8,128)S(1)} %get-tuple-element.35), channel_id=1, source_target_pairs={{0,4},{1,5},{2,6},{3,7},{4,0},{5,1},{6,2},{7,3},{8,12},{9,13},{10,... | collective-permute-start | bytes 24584 | tf_op jit(solution)/shard_map/ppermute | solution.py:438
  57.6 4.1 %collective-permute-start.14 = (f32[16,128]{1,0:T(8,128)S(1)}, f32[16,128]{1,0:T(8,128)S(1)}, u32[]{:S(2)}, u32[]{:S(2)}) collective-permute-start(f32[16,128]{1,0:T(8,128)S(1)} %get-tuple-element.35), channel_id=1, source_target_pairs={{0,32},{8,40},{16,48},{24,56},{64,96},{72,104},{80,112},{88,120},{... | collective-permute-start | bytes 24584 | tf_op jit(solution)/shard_map/ppermute | solution.py:438
  63.6 2.2 %shard_map.59.refs_1_.refs_0_ = f32[2,576,1152]{2,1,0:T(8,128)S(1)} custom-call(f32[2,576,1152]{2,1,0:T(8,128)S(1)} %get-tuple-element.34.refs_0_.refs_3_.refs_2_.y1, f32[2,576,1152]{2,1,0:T(8,128)S(1)} %copy-done.1, f32[9,576,128]{2,1,0:T(8,128)S(1)} %get-tuple-element.24.refs_2_.refs_5_.refs_4_.refs_9_, ...), custom_call_target="tpu_custom_call" | custom-call | flops 1000 | bytes 1000 | tf_op jit(solution)/shard_map/pallas_call | solution.py:419
  68.4 2.2 %shard_map.61.refs_1_.refs_0_ = f32[2,576,1152]{2,1,0:T(8,128)S(1)} custom-call(f32[2,576,1152]{2,1,0:T(8,128)S(1)} %shard_map.59.refs_1_.refs_0_, f32[16,128]{1,0:T(8,128)S(1)} %shard_map.60.refs_1_, f32[16,128]{1,0:T(8,128)S(1)} %get-tuple-element.43.refs_2_.refs_0_, ...), custom_call_target="tpu_custom_call", output_to_operand_aliasing={{}: (0, {})} | custom-call | flops 1000 | bytes 1000 | tf_op jit(solution)/shard_map/pallas_call | solution.py:419
  71.9 2.2 %shard_map.63.refs_3_.refs_0_.refs_1_ = f32[2,576,1152]{2,1,0:T(8,128)S(1)} custom-call(f32[2,576,1152]{2,1,0:T(8,128)S(1)} %shard_map.61.refs_1_.refs_0_, f32[16,128]{1,0:T(8,128)S(1)} %shard_map.62.refs_1_, f32[2,576,1152]{2,1,0:T(8,128)S(1)} %get-tuple-element.34.refs_0_.refs_3_.refs_2_.y1, ...), custom_call_target="tpu_custom_call", output_to_operand_aliasing={{}: (0, {})} | custom-call | flops 1000 | bytes 1000 | tf_op jit(solution)/shard_map/pallas_call | solution.py:419
  75.0 2.1 %collective-permute-start.24 = (f32[16,128]{1,0:T(8,128)S(1)}, f32[16,128]{1,0:T(8,128)S(1)}, u32[]{:S(2)}, u32[]{:S(2)}) collective-permute-start(f32[16,128]{1,0:T(8,128)S(1)} %shard_map.62.refs_1_), channel_id=1, source_target_pairs={{0,8},{16,24},{32,40},{48,56},{64,72},{80,88},{96,104},{112,120},{... | collective-permute-start | bytes 24584 | tf_op jit(solution)/shard_map/ppermute | solution.py:438
  78.6 3.0 %collective-permute-done.26 = f32[16,128]{1,0:T(8,128)S(1)} collective-permute-done((f32[16,128]{1,0:T(8,128)S(1)}, f32[16,128]{1,0:T(8,128)S(1)}, u32[]{:S(2)}, u32[]{:S(2)}) %collective-permute-start.26) | collective-permute-done | bytes 8224 | tf_op jit(solution)/shard_map/ppermute | solution.py:438
  83.3 2.0 %collective-permute-done.25 = f32[16,128]{1,0:T(8,128)S(1)} collective-permute-done((f32[16,128]{1,0:T(8,128)S(1)}, f32[16,128]{1,0:T(8,128)S(1)}, u32[]{:S(2)}, u32[]{:S(2)}) %collective-permute-start.25) | collective-permute-done | bytes 8224 | tf_op jit(solution)/shard_map/ppermute | solution.py:438
  85.3 7.6 %collective-permute-start.27 = (f32[16,128]{1,0:T(8,128)S(1)}, f32[16,128]{1,0:T(8,128)S(1)}, u32[]{:S(2)}, u32[]{:S(2)}) collective-permute-start(f32[16,128]{1,0:T(8,128)S(1)} %add.54), channel_id=1, source_target_pairs={{0,2},{1,3},{4,6},{5,7},{2,0},{3,1},{6,4},{7,5},{8,10},{9,11},{12,... | collective-permute-start | bytes 24584 | tf_op jit(solution)/shard_map/ppermute | solution.py:438
  92.9 2.2 %shard_map.65.base = f32[2,576,1152]{2,1,0:T(8,128)S(1)} custom-call(f32[2,576,1152]{2,1,0:T(8,128)S(1)} %shard_map.63.refs_3_.refs_0_.refs_1_, f32[16,128]{1,0:T(8,128)S(1)} %shard_map.64.refs_1_, f32[2,576,1152]{2,1,0:T(8,128)S(1)} %get-tuple-element.34.refs_0_.refs_3_.refs_2_.y1, f32[2,576,1152]{2,1,0:T(8,128)S(1)} %copy-done.1, ...), custom_call_target="tpu_custom_call", output_to_operand_aliasing={{}: (0, {})} | custom-call | flops 1000 | bytes 1000 | tf_op jit(solution)/shard_map/pallas_call | solution.py:419
  95.2 5.4 %shard_map.69 = f32[2,576,1152]{2,1,0:T(8,128)} custom-call(f32[2,576,1152]{2,1,0:T(8,128)S(1)} %shard_map.65.base, f32[2,576,1152]{2,1,0:T(8,128)S(1)} %get-tuple-element.34.refs_0_.refs_3_.refs_2_.y1, f32[432,128]{1,0:T(8,128)S(1)} %collective-permute-done.18.refs_1_.refs_0_, f32[432,128]{1,0:T(8,128)S(1)} %collective-permute-done.19.refs_2_.refs_1_, ...), custom_call_target="tpu_custom_call" | custom-call | flops 1000 | bytes 1000 | tf_op jit(solution)/shard_map/pallas_call | solution.py:419
  (78 shorter events, 24.2 us)
Async XLA Ops:
  4.2 18.4 %collective-permute-start.1 = (f32[16,128]{1,0:T(8,128)S(1)}, f32[16,128]{1,0:T(8,128)S(1)}, u32[]{:S(2)}, u32[]{:S(2)}) collective-permute-start(f32[16,128]{1,0:T(8,128)S(1)} %get-tuple-element.26), channel_id=1, source_target_pairs={{0,4},{1,5},{2,6},{3,7},{4,0},{5,1},{6,2},{7,3},{8,12},{9,13},{10,... | collective-permute-start | bytes 24584 | tf_op jit(solution)/shard_map/ppermute | solution.py:438
  7.3 15.2 %collective-permute-start = (f32[16,128]{1,0:T(8,128)S(1)}, f32[16,128]{1,0:T(8,128)S(1)}, u32[]{:S(2)}, u32[]{:S(2)}) collective-permute-start(f32[16,128]{1,0:T(8,128)S(1)} %get-tuple-element.26), channel_id=1, source_target_pairs={{0,32},{8,40},{16,48},{24,56},{64,96},{72,104},{80,112},{88,120},{... | collective-permute-start | bytes 24584 | tf_op jit(solution)/shard_map/ppermute | solution.py:438
  8.8 19.1 %collective-permute-start.3 = (f32[288,128]{1,0:T(8,128)S(1)}, f32[288,128]{1,0:T(8,128)S(1)}, u32[]{:S(2)}, u32[]{:S(2)}) collective-permute-start(f32[288,128]{1,0:T(8,128)S(1)} %get-tuple-element.27), channel_id=1, source_target_pairs={{0,1},{2,3},{4,5},{6,7},{1,0},{3,2},{5,4},{7,6},{8,9},{10,11},{12,... | collective-permute-start | bytes 442376 | tf_op jit(solution)/shard_map/ppermute | solution.py:438
  10.7 20.2 %collective-permute-start.4 = (f32[432,128]{1,0:T(8,128)S(1)}, f32[432,128]{1,0:T(8,128)S(1)}, u32[]{:S(2)}, u32[]{:S(2)}) collective-permute-start(f32[432,128]{1,0:T(8,128)S(1)} %get-tuple-element.28), channel_id=1, source_target_pairs={{0,2},{1,3},{4,6},{5,7},{2,0},{3,1},{6,4},{7,5},{8,10},{9,11},{12,... | collective-permute-start | bytes 663560 | tf_op jit(solution)/shard_map/ppermute | solution.py:438
  14.3 17.3 %collective-permute-start.5 = (f32[432,128]{1,0:T(8,128)S(1)}, f32[432,128]{1,0:T(8,128)S(1)}, u32[]{:S(2)}, u32[]{:S(2)}) collective-permute-start(f32[432,128]{1,0:T(8,128)S(1)} %get-tuple-element.29), channel_id=1, source_target_pairs={{2,4},{3,5},{4,2},{5,3},{10,12},{11,13},{12,10},{13,11},{18,20},{1... | collective-permute-start | bytes 663560 | tf_op jit(solution)/shard_map/ppermute | solution.py:438
  22.6 5.4 %collective-permute-start.2 = (f32[16,128]{1,0:T(8,128)S(1)}, f32[16,128]{1,0:T(8,128)S(1)}, u32[]{:S(2)}, u32[]{:S(2)}) collective-permute-start(f32[16,128]{1,0:T(8,128)S(1)} %shard_map.49.refs_1_), channel_id=1, source_target_pairs={{0,64},{8,72},{16,80},{24,88},{32,96},{40,104},{48,112},{56,120},{... | collective-permute-start | bytes 24584 | tf_op jit(solution)/shard_map/ppermute | solution.py:438
  25.4 24.4 %collective-permute-start.6 = (f32[2,24,1152]{2,1,0:T(8,128)S(1)}, f32[2,24,1152]{2,1,0:T(8,128)S(1)}, u32[]{:S(2)}, u32[]{:S(2)}) collective-permute-start(f32[2,24,1152]{2,1,0:T(8,128)S(1)} %get-tuple-element.30), channel_id=1, source_target_pairs={{0,32},{8,40},{16,48},{24,56},{64,96},{72,104},{80,112},{88,120},{... | collective-permute-start | bytes 663560 | tf_op jit(solution)/shard_map/ppermute | solution.py:438
  28.0 21.8 %collective-permute-start.7 = (f32[2,24,1152]{2,1,0:T(8,128)S(1)}, f32[2,24,1152]{2,1,0:T(8,128)S(1)}, u32[]{:S(2)}, u32[]{:S(2)}) collective-permute-start(f32[2,24,1152]{2,1,0:T(8,128)S(1)} %get-tuple-element.31), channel_id=1, source_target_pairs={{32,64},{40,72},{48,80},{56,88},{64,32},{72,40},{80,48},{88,56},{3... | collective-permute-start | bytes 663560 | tf_op jit(solution)/shard_map/ppermute | solution.py:438
  30.9 18.9 %collective-permute-start.8 = (f32[2,24,1152]{2,1,0:T(8,128)S(1)}, f32[2,24,1152]{2,1,0:T(8,128)S(1)}, u32[]{:S(2)}, u32[]{:S(2)}) collective-permute-start(f32[2,24,1152]{2,1,0:T(8,128)S(1)} %shard_map.55), channel_id=1, source_target_pairs={{0,8},{16,24},{32,40},{48,56},{64,72},{80,88},{96,104},{112,120},{... | collective-permute-start | bytes 663560 | tf_op jit(solution)/shard_map/ppermute | solution.py:438
  31.0 18.8 %collective-permute-start.9 = (f32[2,24,1152]{2,1,0:T(8,128)S(1)}, f32[2,24,1152]{2,1,0:T(8,128)S(1)}, u32[]{:S(2)}, u32[]{:S(2)}) collective-permute-start(f32[2,24,1152]{2,1,0:T(8,128)S(1)} %shard_map.56), channel_id=1, source_target_pairs={{8,16},{40,48},{72,80},{104,112},{16,8},{48,40},{80,72},{112,104},... | collective-permute-start | bytes 663560 | tf_op jit(solution)/shard_map/ppermute | solution.py:438
  34.6 3.7 %collective-permute-start.12 = (f32[16,128]{1,0:T(8,128)S(1)}, f32[16,128]{1,0:T(8,128)S(1)}, u32[]{:S(2)}, u32[]{:S(2)}) collective-permute-start(f32[16,128]{1,0:T(8,128)S(1)} %shard_map.53.refs_1_), channel_id=1, source_target_pairs={{0,1},{2,3},{4,5},{6,7},{1,0},{3,2},{5,4},{7,6},{8,9},{10,11},{12,... | collective-permute-start | bytes 24584 | tf_op jit(solution)/shard_map/ppermute | solution.py:438
  41.9 7.8 %collective-permute-start.13 = (f32[16,128]{1,0:T(8,128)S(1)}, f32[16,128]{1,0:T(8,128)S(1)}, u32[]{:S(2)}, u32[]{:S(2)}) collective-permute-start(f32[16,128]{1,0:T(8,128)S(1)} %add.47), channel_id=1, source_target_pairs={{0,2},{1,3},{4,6},{5,7},{2,0},{3,1},{6,4},{7,5},{8,10},{9,11},{12,... | collective-permute-start | bytes 24584 | tf_op jit(solution)/shard_map/ppermute | solution.py:438
  55.6 10.2 %collective-permute-start.15 = (f32[16,128]{1,0:T(8,128)S(1)}, f32[16,128]{1,0:T(8,128)S(1)}, u32[]{:S(2)}, u32[]{:S(2)}) collective-permute-start(f32[16,128]{1,0:T(8,128)S(1)} %get-tuple-element.35), channel_id=1, source_target_pairs={{0,4},{1,5},{2,6},{3,7},{4,0},{5,1},{6,2},{7,3},{8,12},{9,13},{10,... | collective-permute-start | bytes 24584 | tf_op jit(solution)/shard_map/ppermute | solution.py:438
  57.6 8.2 %collective-permute-start.14 = (f32[16,128]{1,0:T(8,128)S(1)}, f32[16,128]{1,0:T(8,128)S(1)}, u32[]{:S(2)}, u32[]{:S(2)}) collective-permute-start(f32[16,128]{1,0:T(8,128)S(1)} %get-tuple-element.35), channel_id=1, source_target_pairs={{0,32},{8,40},{16,48},{24,56},{64,96},{72,104},{80,112},{88,120},{... | collective-permute-start | bytes 24584 | tf_op jit(solution)/shard_map/ppermute | solution.py:438
  61.7 9.4 %collective-permute-start.17 = (f32[288,128]{1,0:T(8,128)S(1)}, f32[288,128]{1,0:T(8,128)S(1)}, u32[]{:S(2)}, u32[]{:S(2)}) collective-permute-start(f32[288,128]{1,0:T(8,128)S(1)} %get-tuple-element.36), channel_id=1, source_target_pairs={{0,1},{2,3},{4,5},{6,7},{1,0},{3,2},{5,4},{7,6},{8,9},{10,11},{12,... | collective-permute-start | bytes 442376 | tf_op jit(solution)/shard_map/ppermute | solution.py:438
  61.7 12.6 %collective-permute-start.18 = (f32[432,128]{1,0:T(8,128)S(1)}, f32[432,128]{1,0:T(8,128)S(1)}, u32[]{:S(2)}, u32[]{:S(2)}) collective-permute-start(f32[432,128]{1,0:T(8,128)S(1)} %get-tuple-element.37), channel_id=1, source_target_pairs={{0,2},{1,3},{4,6},{5,7},{2,0},{3,1},{6,4},{7,5},{8,10},{9,11},{12,... | collective-permute-start | bytes 663560 | tf_op jit(solution)/shard_map/ppermute | solution.py:438
  62.9 12.1 %collective-permute-start.19 = (f32[432,128]{1,0:T(8,128)S(1)}, f32[432,128]{1,0:T(8,128)S(1)}, u32[]{:S(2)}, u32[]{:S(2)}) collective-permute-start(f32[432,128]{1,0:T(8,128)S(1)} %get-tuple-element.38), channel_id=1, source_target_pairs={{2,4},{3,5},{4,2},{5,3},{10,12},{11,13},{12,10},{13,11},{18,20},{1... | collective-permute-start | bytes 663560 | tf_op jit(solution)/shard_map/ppermute | solution.py:438
  65.8 5.2 %collective-permute-start.16 = (f32[16,128]{1,0:T(8,128)S(1)}, f32[16,128]{1,0:T(8,128)S(1)}, u32[]{:S(2)}, u32[]{:S(2)}) collective-permute-start(f32[16,128]{1,0:T(8,128)S(1)} %shard_map.60.refs_1_), channel_id=1, source_target_pairs={{0,64},{8,72},{16,80},{24,88},{32,96},{40,104},{48,112},{56,120},{... | collective-permute-start | bytes 24584 | tf_op jit(solution)/shard_map/ppermute | solution.py:438
  66.9 28.2 %collective-permute-start.20 = (f32[2,24,1152]{2,1,0:T(8,128)S(1)}, f32[2,24,1152]{2,1,0:T(8,128)S(1)}, u32[]{:S(2)}, u32[]{:S(2)}) collective-permute-start(f32[2,24,1152]{2,1,0:T(8,128)S(1)} %get-tuple-element.39), channel_id=1, source_target_pairs={{0,32},{8,40},{16,48},{24,56},{64,96},{72,104},{80,112},{88,120},{... | collective-permute-start | bytes 663560 | tf_op jit(solution)/shard_map/ppermute | solution.py:438
  71.1 24.1 %collective-permute-start.21 = (f32[2,24,1152]{2,1,0:T(8,128)S(1)}, f32[2,24,1152]{2,1,0:T(8,128)S(1)}, u32[]{:S(2)}, u32[]{:S(2)}) collective-permute-start(f32[2,24,1152]{2,1,0:T(8,128)S(1)} %get-tuple-element.40), channel_id=1, source_target_pairs={{32,64},{40,72},{48,80},{56,88},{64,32},{72,40},{80,48},{88,56},{3... | collective-permute-start | bytes 663560 | tf_op jit(solution)/shard_map/ppermute | solution.py:438
  74.2 21.0 %collective-permute-start.22 = (f32[2,24,1152]{2,1,0:T(8,128)S(1)}, f32[2,24,1152]{2,1,0:T(8,128)S(1)}, u32[]{:S(2)}, u32[]{:S(2)}) collective-permute-start(f32[2,24,1152]{2,1,0:T(8,128)S(1)} %shard_map.66), channel_id=1, source_target_pairs={{0,8},{16,24},{32,40},{48,56},{64,72},{80,88},{96,104},{112,120},{... | collective-permute-start | bytes 663560 | tf_op jit(solution)/shard_map/ppermute | solution.py:438
  74.3 20.9 %collective-permute-start.23 = (f32[2,24,1152]{2,1,0:T(8,128)S(1)}, f32[2,24,1152]{2,1,0:T(8,128)S(1)}, u32[]{:S(2)}, u32[]{:S(2)}) collective-permute-start(f32[2,24,1152]{2,1,0:T(8,128)S(1)} %shard_map.67), channel_id=1, source_target_pairs={{8,16},{40,48},{72,80},{104,112},{16,8},{48,40},{80,72},{112,104},... | collective-permute-start | bytes 663560 | tf_op jit(solution)/shard_map/ppermute | solution.py:438
  78.0 3.7 %collective-permute-start.26 = (f32[16,128]{1,0:T(8,128)S(1)}, f32[16,128]{1,0:T(8,128)S(1)}, u32[]{:S(2)}, u32[]{:S(2)}) collective-permute-start(f32[16,128]{1,0:T(8,128)S(1)} %shard_map.64.refs_1_), channel_id=1, source_target_pairs={{0,1},{2,3},{4,5},{6,7},{1,0},{3,2},{5,4},{7,6},{8,9},{10,11},{12,... | collective-permute-start | bytes 24584 | tf_op jit(solution)/shard_map/ppermute | solution.py:438
  85.3 9.9 %collective-permute-start.27 = (f32[16,128]{1,0:T(8,128)S(1)}, f32[16,128]{1,0:T(8,128)S(1)}, u32[]{:S(2)}, u32[]{:S(2)}) collective-permute-start(f32[16,128]{1,0:T(8,128)S(1)} %add.54), channel_id=1, source_target_pairs={{0,2},{1,3},{4,6},{5,7},{2,0},{3,1},{6,4},{7,5},{8,10},{9,11},{12,... | collective-permute-start | bytes 24584 | tf_op jit(solution)/shard_map/ppermute | solution.py:438
  (9 other events, 35.9 us)
where the time goes:
time: 102 us; the launch traced here: 101 us
  starting transfers between devices  48.9 us (48%)
  Pallas kernels  33.4 us (33%)
  waiting for transfers between devices  13 us (13%)
  local copies, waits for them, and re-layouts  4.9 us (5%)
    ppermute x28, starting transfers between devices, traded(): return lax.ppermute(block, axis, pairs(axis, linked))  48.9 us
    pallas_call x24, Pallas kernels, call(): pl.pallas_call(kernel, out_shape=out_shapes, in_specs=[VM] * len(args), o...  33.4 us
    ppermute x28, waiting for transfers between devices, traded(): return lax.ppermute(block, axis, pairs(axis, linked))  13 us
    unnamed x10, local copies, waits for them, and re-layouts  4.9 us
  transfers between devices with their start and end apart: 28, of which 8 were waited for; matrix products, arithmetic and copies ran while one was open for 0% of the time, Pallas kernels for 20%

commit v1 on v0

--- a/solution.py
+++ b/solution.py
@@ -18,7 +18,7 @@
 VMEM_LIMIT = 8 * 1024 * 1024
 
 DN_IN, UP_IN, RT_IN, LF_IN, DN_RIM, UP_RIM, RT_RIM, LF_RIM, ROW_U = range(9)
-C_DN, C_UP, C_RT, C_LF, C_DN_RIM, C_UP_RIM, C_RT_E, C_RT_F, C_LF_E, C_LF_F, C_X_E, C_X_F, COL_U = range(13)
+C_DN, C_UP, C_RT, C_LF, C_DN_RIM, C_UP_RIM, C_RT_E, C_RT_F, C_LF_E, C_LF_F, C_X_E, C_X_F, COL_U, C_DN_ALL, C_UP_ALL, C_RT_ALL, C_LF_ALL = range(17)
 
 
 def iota(shape, dim):
@@ -45,12 +45,12 @@
     return pl.ds(t * LANES, LANES)
 
 
-def weights_kernel(down_ref, across_ref, rep_ref, roww, colw):
+def weights(bonds, roww, colw):
     row_id, col_id = place()
     side = (LATTICE, LATTICE)
-    down = jnp.where(iota(side, 0) < LATTICE - 1, down_ref[...], 0.0)
-    across = jnp.where(iota(side, 1) < LATTICE - 1, across_ref[...], 0.0)
-    rep = rep_ref[...]
+    down = jnp.where(iota(side, 0) < LATTICE - 1, bonds[0], 0.0)
+    across = jnp.where(iota(side, 1) < LATTICE - 1, bonds[1], 0.0)
+    rep = bonds[2]
     dot = functools.partial(jnp.dot, precision=lax.Precision.HIGHEST, preferred_element_type=F32)
 
     s = iota((SQUARE, LATTICE), 0)
@@ -119,6 +119,7 @@
         C_LF_E: heads1 * lf_e, C_LF_F: heads1 * (1.0 - lf_e),
         C_X_E: x_even * xe_e + x_odd * xo_e, C_X_F: x_even * (1.0 - xe_e) + x_odd * (1.0 - xo_e),
         COL_U: TIME_STEP * pick_cols(rep, 0, 0),
+        C_DN_ALL: dn, C_UP_ALL: up, C_RT_ALL: rt, C_LF_ALL: lf,
     }
     for k, v in values.items():
         colw[k] = jnp.broadcast_to(v, (8, COLUMNS))
@@ -147,7 +148,7 @@
 QUARTER = SQUARE // 4
 
 
-def pack_faces(src, face_a, face_b, side, down_a, down_b, across_a, across_b, diag):
+def pack_faces(src, face_a, face_b, side, down_a, down_b, across_a, across_b):
     up_first, even, row_up_first, row_even = parities()
     base = jnp.where(even, 4 * LANES, 0)
     lane, lane24 = lane_maps()
@@ -202,27 +203,78 @@
             right = src[p, a * PATCH + PATCH - 1 : a * PATCH + PATCH, :]
             across_a[p, a : a + 1, :] = jnp.where(row_even, right, left)
             across_b[p, a : a + 1, :] = jnp.where(row_even, left, right)
-    pack_diag(src, diag)
-
-
-def pack_diag(src, diag):
+
+
+SLOT = 24
+
+
+def pack_densities(src, colw, table, row_sums, slots):
     row_id, col_id = place()
-    diag[...] = jnp.zeros(diag.shape, F32)
-
-    @pl.when(row_id // 2 == col_id)
+    odd = lax.rem(row_id, 2)
+    across = lax.rem(row_id, 4) - 2 * lax.rem(col_id, 2)
+    along = row_id // 4 - col_id // 2
+    beside = jnp.logical_and(along == 0, jnp.logical_and(across >= -1, across <= 2))
+    over = jnp.logical_and(jnp.abs(along) == 1, jnp.logical_and(across >= 0, across <= 1))
+    table[...] = jnp.zeros(table.shape, F32)
+
+    @pl.when(jnp.logical_or(beside, over))
     def _():
-        odd = row_id % 2
-        lane = iota((8, LANES), 1) - iota((8, LANES), 0)
+        slots[...] = jnp.zeros(slots.shape, F32)
+        row_sums[...] = jnp.zeros(row_sums.shape, F32)
+        lane = iota((8, LANES), 1)
+        sub = iota((8, LANES), 0)
+        codes = []
+        for t in range(TILES):
+            j = lane + t * LANES
+            g = (j >= SQUARE).astype(jnp.int32)
+            a = over24(j - SQUARE * g)
+            b = j - SQUARE * g - PATCH * a
+            codes.append(100 * (PATCH * (col_id // 2) + a) + PATCH * (2 * lax.rem(col_id, 2) + g) + b)
+        first = 100 * PATCH * (row_id // 4) + PATCH * lax.rem(row_id, 4)
+
+        def step(a, sums):
+            sums = list(sums)
+            for k in range(3):
+                here = pl.multiple_of(a * PATCH + 8 * k, 8)
+                mine = first + 100 * a + 8 * k + sub
+                along_row = None
+                for t in range(TILES):
+                    apart = mine - codes[t]
+                    w = jnp.where(apart == 100, colw[C_DN_ALL, :, tile(t)], 0.0)
+                    w = jnp.where(apart == -100, colw[C_UP_ALL, :, tile(t)], w)
+                    w = jnp.where(apart == 1, colw[C_RT_ALL, :, tile(t)], w)
+                    w = jnp.where(apart == -1, colw[C_LF_ALL, :, tile(t)], w)
+                    flow = w * src[1, pl.ds(here, 8), tile(t)]
+                    sums[t] = sums[t] - flow + jnp.where(apart == 0, src[0, pl.ds(here, 8), tile(t)], 0.0)
+                    sums[TILES + t] = sums[TILES + t] + jnp.where(apart == 0, src[0, pl.ds(here, 8), tile(t)], 0.0)
+                    along_row = flow if along_row is None else along_row + flow
+                row_sums[pl.ds(64 * odd + here, 8), :] = along_row
+            return tuple(sums)
+
+        sums = lax.fori_loop(0, PATCH, step, (jnp.zeros((8, LANES), F32),) * (2 * TILES))
+        for t in range(TILES):
+            slots[0, t : t + 1, :] = jnp.sum(sums[TILES + t], axis=0, keepdims=True)
+            slots[0, TILES + t : TILES + t + 1, :] = jnp.sum(sums[t], axis=0, keepdims=True)
         for t in range(5):
-            total = jnp.zeros((8, LANES), F32)
-            first = t * LANES - 64 * odd
-            for k in range(LANES // 8):
-                row = first + 8 * k
-                inside = jnp.logical_and(row >= 0, row < SQUARE)
-                at = pl.multiple_of(jnp.clip(row, 0, SQUARE - 8), 8)
-                value = src[0, pl.ds(at, 8), pl.ds(pl.multiple_of((4 * odd + t) * LANES, LANES), LANES)]
-                total = total + jnp.where(jnp.logical_and(lane == 8 * k, inside), value, 0.0)
-            diag[pl.ds(4 * odd + t, 1), :] = jnp.sum(total, axis=0, keepdims=True)
+            got = jnp.sum(row_sums[t * LANES : (t + 1) * LANES, :].T, axis=0, keepdims=True)
+            slots[1, pl.ds(TILES + 4 * odd + t, 1), :] = got
+        table[pl.ds(pl.multiple_of(SLOT * col_id, 8), SLOT), :] = slots[0]
+        table[pl.ds(pl.multiple_of(SLOT * (row_id // 2), 8), SLOT), :] += slots[1]
+
+
+def first_kernel(corr, down, across, rep, y, roww, colw, *refs):
+    faces, table, (row_sums, slots, bonds, sems) = refs[:7], refs[7], refs[8:]
+    copies = [pltpu.make_async_copy(v, bonds.at[n], sems.at[n]) for n, v in enumerate((down, across, rep))]
+    copies += [pltpu.make_async_copy(corr.at[p], y.at[p], sems.at[3 + p]) for p in range(2)]
+    for c in copies:
+        c.start()
+    for c in copies[:3]:
+        c.wait()
+    weights(bonds, roww, colw)
+    for c in copies[3:]:
+        c.wait()
+    pack_faces(y, *faces)
+    pack_densities(y, colw, table, row_sums, slots)
 
 
 def hop_strip(src, q, a, roww, colw):
@@ -305,18 +357,22 @@
     return value
 
 
-def finish(scale, base, y, halos, roww, colw, out, e_row, e_col, chunk_done=None):
-    face_a, face_b, side, down_a, down_b, across_a, across_b, col_diag, row_diag = halos
+def finish(stage, base, y, halos, roww, colw, out, e_row, e_col, chunk_done=None):
+    face_a, face_b, side, down_a, down_b, across_a, across_b, table = halos
+    scale = 0.5 if stage else 1.0
     row_id, col_id = place()
     up_first, even, row_up_first, row_even = parities()
     row_odd = lax.rem(row_id, 2)
     shift = jnp.where(even, 87, 41)
     lane = iota((8, LANES), 1)
+    row_slot = table[pl.ds(pl.multiple_of(SLOT * (row_id // 2), 8), SLOT), :]
+    col_slot = table[pl.ds(pl.multiple_of(SLOT * col_id, 8), SLOT), :]
     for t in range(5):
-        strip = jnp.where(row_odd == 1, row_diag[4 + t : 5 + t, :], row_diag[t : t + 1, :])
+        u = stage * TILES + t
+        strip = jnp.where(row_odd == 1, row_slot[4 + u : 5 + u, :], row_slot[u : u + 1, :])
         e_row[t * LANES : (t + 1) * LANES, :] = jnp.broadcast_to(strip, (LANES, LANES)).T
     for t in range(TILES):
-        e_col[:, tile(t)] = col_diag[t : t + 1, :] * colw[COL_U, :, tile(t)]
+        e_col[:, tile(t)] = col_slot[stage * TILES + t : stage * TILES + t + 1, :] * colw[COL_U, :, tile(t)]
 
     def strip(a, folded):
         here = pl.multiple_of(a * PATCH, 8)
@@ -385,13 +441,13 @@
 
 
 def middle_kernel(base, y, *refs):
-    halos, (roww, colw), (y1, *faces), (e_row, e_col) = refs[:9], refs[9:11], refs[11:20], refs[20:]
-    finish(1.0, base, y, halos, roww, colw, y1, e_row, e_col)
+    halos, (roww, colw), (y1, *faces), (e_row, e_col) = refs[:8], refs[8:10], refs[10:18], refs[18:]
+    finish(0, base, y, halos, roww, colw, y1, e_row, e_col)
     pack_faces(y1, *faces)
 
 
 def last_kernel(base, y1, *refs):
-    halos, (roww, colw), out_hbm, (e_row, e_col, out, sems) = refs[:9], refs[9:11], refs[11], refs[12:]
+    halos, (roww, colw), out_hbm, (e_row, e_col, out, sems) = refs[:8], refs[8:10], refs[10], refs[11:]
     copies = []
 
     def chunk_done(first, last):
@@ -400,7 +456,7 @@
             copies.append(pltpu.make_async_copy(out.at[p, rows], out_hbm.at[p, rows], sems.at[len(copies)]))
             copies[-1].start()
 
-    finish(0.5, base, y1, halos, roww, colw, out, e_row, e_col, chunk_done)
+    finish(1, base, y1, halos, roww, colw, out, e_row, e_col, chunk_done)
     for c in copies:
         c.wait()
 
@@ -411,21 +467,22 @@
 
 VM = pl.BlockSpec(memory_space=pltpu.VMEM)
 STATE = (2, SQUARE, COLUMNS)
-FACES = (((3 * QUARTER, LANES),) * 2 + ((SQUARE // 2, LANES),) + ((2, PATCH, COLUMNS),) * 4 + ((16, LANES),))
-
-
-def call(kernel, args, out_shapes, scratch=(), flops=1000, out_specs=None, aliases=None):
+FACES = ((3 * QUARTER, LANES),) * 2 + ((SQUARE // 2, LANES),) + ((2, PATCH, COLUMNS),) * 4
+TABLE = (8 * SLOT, LANES)
+
+
+def call(kernel, args, out_shapes, scratch=(), out_specs=None, aliases=None, loads=False):
     many = isinstance(out_shapes, (list, tuple))
     return pl.pallas_call(
         kernel,
         out_shape=out_shapes,
-        in_specs=[VM] * len(args),
+        in_specs=[pl.BlockSpec(memory_space=pl.ANY) if loads else VM] * len(args),
         out_specs=out_specs or ([VM] * len(out_shapes) if many else VM),
         scratch_shapes=list(scratch),
         input_output_aliases=aliases or {},
         compiler_params=pltpu.CompilerParams(vmem_limit_bytes=VMEM_LIMIT),
-        cost_estimate=pl.CostEstimate(flops=flops, bytes_accessed=1000, transcendentals=0),
-    )(*[pltpu.with_memory_space_constraint(x, pltpu.VMEM) for x in args])
+        cost_estimate=pl.CostEstimate(flops=1000, bytes_accessed=1000, transcendentals=0),
+    )(*[pltpu.with_memory_space_constraint(x, pltpu.HBM if loads else pltpu.VMEM) for x in args])
 
 
 def pairs(axis, linked):
@@ -446,35 +503,89 @@
     def kernel(*refs):
         refs[-1][...] = refs[0][...]
 
-    return call(kernel, (value, *after), on_chip(*value.shape), flops=0)
-
-
-def exchange(faces, piece):
-    face_a, face_b, side, down_a, down_b, across_a, across_b, diag = faces
-    face_a = flipped(face_a, "col", 2)
-    face_b = traded(face_b, "col", lambda i, j: j == i + 2 and (i // 2) % 2 == 1)
-    side = flipped(side, "col", 1)
-    down_a = flipped(down_a, "row", 4)
-    down_b = traded(down_b, "row", lambda i, j: j == i + 4 and (i // 4) % 2 == 1)
-    col_diag = diag + flipped(diag, "row", 4)
-    row_diag = diag + flipped(diag, "col", 4)
+    return call(kernel, (value, *after), on_chip(*value.shape))
+
+
+def merged(value, got, *after):
+    def kernel(*refs):
+        refs[-1][...] = refs[0][...] + refs[1][...]
+
+    return call(kernel, (value, got, *after), on_chip(*value.shape))
+
+
+def swap_face_a(x):
+    return flipped(x, "col", 2)
+
+
+def swap_face_b(x):
+    return traded(x, "col", lambda i, j: j == i + 2 and (i // 2) % 2 == 1)
+
+
+def swap_side(x):
+    return flipped(x, "col", 1)
+
+
+def swap_down_a(x):
+    return flipped(x, "row", 4)
+
+
+def swap_down_b(x):
+    return traded(x, "row", lambda i, j: j == i + 4 and (i // 4) % 2 == 1)
+
+
+def swap_across_a(x):
+    return flipped(x, "row", 1)
+
+
+def swap_across_b(x):
+    return traded(x, "row", lambda i, j: j == i + 1 and i % 4 == 1)
+
+
+def swap_bits(x, row_bits, col_bits):
+    rows, cols = lax.axis_size("row"), lax.axis_size("col")
+    route = [(r * cols + c, (r ^ row_bits) * cols + (c ^ col_bits)) for r in range(rows) for c in range(cols)]
+    return lax.ppermute(x, ("row", "col"), route)
+
+
+def first_exchange(faces, table, piece):
+    face_a, face_b, side, down_a, down_b, across_a, across_b = faces
+    face_a, face_b = swap_face_a(face_a), swap_face_b(face_b)
+    got = flipped(table, "row", 4)
     part = piece(0, None)
-    col_diag = tie(col_diag, part)
-    col_got = flipped(col_diag, "row", 8)
-    part = piece(1, part, col_diag, row_diag)
-    col_diag = tie(col_diag + col_got, part, side)
-    col_got = flipped(col_diag, "row", 1)
-    part = piece(2, part, col_diag)
-    across_a = flipped(tie(across_a, part), "row", 1)
-    across_b = traded(tie(across_b, part), "row", lambda i, j: j == i + 1 and i % 4 == 1)
-    col_diag = tie(col_diag + col_got, part)
-    col_diag = col_diag + flipped(col_diag, "row", 2)
-    row_diag = tie(row_diag, face_a, face_b, part)
-    row_got = flipped(row_diag, "col", 1)
-    part = piece(3, part, row_diag)
-    row_diag = row_diag + row_got
-    row_diag = row_diag + flipped(row_diag, "col", 2)
-    return part, (face_a, face_b, side, down_a, down_b, across_a, across_b, col_diag, row_diag)
+    table = merged(table, got, part)
+    got = flipped(table, "row", 12)
+    side = swap_side(tie(side, table))
+    down_a = swap_down_a(tie(down_a, table))
+    part = piece(1, part, table)
+    table = merged(table, got, part)
+    got = flipped(table, "row", 1)
+    down_b = swap_down_b(tie(down_b, table))
+    part = piece(2, part, table)
+    table = merged(table, got, part, side, face_a, face_b)
+    got = flipped(table, "row", 2)
+    across_a = swap_across_a(tie(across_a, table))
+    across_b = swap_across_b(tie(across_b, table))
+    part = piece(3, part, table)
+    table = merged(table, got, part, down_a)
+    table = merged(table, swap_bits(table, 2, 4), down_b)
+    table = merged(table, flipped(table, "col", 1), across_a)
+    table = merged(table, flipped(table, "col", 3), across_b)
+    return part, (face_a, face_b, side, down_a, down_b, across_a, across_b, table)
+
+
+def second_exchange(faces, table, piece):
+    face_a, face_b, side, down_a, down_b, across_a, across_b = faces
+    face_a, face_b = swap_face_a(face_a), swap_face_b(face_b)
+    part = piece(0, None)
+    side = swap_side(tie(side, part))
+    down_a = swap_down_a(tie(down_a, part))
+    down_b = swap_down_b(tie(down_b, part))
+    part = piece(1, part)
+    part = piece(2, part)
+    across_a = swap_across_a(tie(across_a, part))
+    across_b = swap_across_b(tie(across_b, part))
+    part = piece(3, part, side, down_a, down_b)
+    return part, (face_a, face_b, side, down_a, down_b, across_a, across_b, table)
 
 
 PIECES = 4
@@ -495,15 +606,22 @@
 def local(corr, bonds_down, bonds_across, repulsion):
     faces_out = [on_chip(*s) for s in FACES]
     e_scratch = [pltpu.VMEM((5 * LANES, LANES), F32), pltpu.VMEM((8, COLUMNS), F32)]
-    weights = call(
-        weights_kernel,
-        (bonds_down, bonds_across, repulsion),
-        [on_chip(9, SQUARE, LANES), on_chip(13, 8, COLUMNS)],
+    y, roww, colw, *faces, table = call(
+        first_kernel,
+        (corr, bonds_down, bonds_across, repulsion),
+        [on_chip(*STATE), on_chip(9, SQUARE, LANES), on_chip(17, 8, COLUMNS), *faces_out, on_chip(*TABLE)],
+        [
+            pltpu.VMEM((5 * LANES, LANES), F32),
+            pltpu.VMEM((2, SLOT, LANES), F32),
+            pltpu.VMEM((3, LATTICE, LATTICE), F32),
+            pltpu.SemaphoreType.DMA((5,)),
+        ],
+        loads=True,
     )
-    faces = call(pack_faces, (corr,), faces_out)
-    part, halos = exchange(faces, interior(False, corr, corr, weights))
-    y1, *faces = call(middle_kernel, (part, corr, *halos, *weights), [on_chip(*STATE), *faces_out], e_scratch)
-    part, halos = exchange(faces, interior(True, y1, corr, weights))
+    weights = (roww, colw)
+    part, halos = first_exchange(faces, table, interior(False, y, y, weights))
+    y1, *faces = call(middle_kernel, (part, y, *halos, *weights), [on_chip(*STATE), *faces_out], e_scratch)
+    part, halos = second_exchange(faces, halos[-1], interior(True, y1, y, weights))
     return call(
         last_kernel,
         (part, y1, *halos, *weights),

time: 102 us -> 87.8 us (0.86)
  the two profiles are of different devices: /device:TPU:0 before, /device:TPU:19 now
where the time goes in v1:
time: 87.8 us; the launch traced here: 87.6 us
  starting transfers between devices  42.1 us (48%)
  Pallas kernels  35.9 us (41%)
  waiting for transfers between devices  9.18 us (10%)
    ppermute x20, starting transfers between devices, traded(): return lax.ppermute(block, axis, pairs(axis, linked))  42 us
    pallas_call x28, Pallas kernels, call(): pl.pallas_call(kernel, out_shape=out_shapes, in_specs=[pl.BlockSpec(memor...  35.9 us
    ppermute x20, waiting for transfers between devices, traded(): return lax.ppermute(block, axis, pairs(axis, linked))  9.18 us
  transfers between devices with their start and end apart: 21, of which 4 were waited for; matrix products, arithmetic and copies ran while one was open for 0% of the time, Pallas kernels for 18%

profile of v1, /device:TPU:19, one launch (start us, length us, event | category | flops | bytes accessed | tf_op | source)
XLA Modules:
  0.0 87.6 jit_solution(11887746712357472003)
XLA Ops:
  0.0 7.2 %shard_map.46 = (f32[2,576,1152]{2,1,0:T(8,128)S(1)}, f32[9,576,128]{2,1,0:T(8,128)S(1)}, f32[17,8,1152]{2,1,0:T(8,128)S(1)}, f32[432,128]{1,0:T(8,128)S(1)}, f3...) custom-call(f32[2,576,1152]{2,1,0:T(8,128)} %corr.1, ...), custom_call_target="tpu_custom_call" | custom-call | flops 1000 | bytes 1000 | tf_op jit(solution)/shard_map/pallas_call | solution.py:476
  7.3 2.0 %collective-permute-start.4 = (f32[432,128]{1,0:T(8,128)S(1)}, f32[432,128]{1,0:T(8,128)S(1)}, u32[]{:S(2)}, u32[]{:S(2)}) collective-permute-start(f32[432,128]{1,0:T(8,128)S(1)} %get-tuple-element.29), channel_id=1, source_target_pairs={{0,2},{1,3},{4,6},{5,7},{2,0},{3,1},{6,4},{7,5},{8,10},{9,11},{12,... | collective-permute-start | bytes 663560 | tf_op jit(solution)/shard_map/ppermute | solution.py:495
  9.2 3.5 %collective-permute-start.5 = (f32[432,128]{1,0:T(8,128)S(1)}, f32[432,128]{1,0:T(8,128)S(1)}, u32[]{:S(2)}, u32[]{:S(2)}) collective-permute-start(f32[432,128]{1,0:T(8,128)S(1)} %get-tuple-element.30), channel_id=1, source_target_pairs={{2,4},{3,5},{4,2},{5,3},{10,12},{11,13},{12,10},{13,11},{18,20},{1... | collective-permute-start | bytes 663560 | tf_op jit(solution)/shard_map/ppermute | solution.py:495
  12.8 2.2 %shard_map.47.refs_2_.refs_0_ = f32[2,576,1152]{2,1,0:T(8,128)S(1)} custom-call(f32[2,576,1152]{2,1,0:T(8,128)S(1)} %get-tuple-element.24.refs_0_.refs_1_.refs_2_.refs_3_.y.refs_5_, f32[2,576,1152]{2,1,0:T(8,128)S(1)} %get-tuple-element.24.refs_0_.refs_1_.refs_2_.refs_3_.y.refs_5_, ...), custom_call_target="tpu_custom_call" | custom-call | flops 1000 | bytes 1000 | tf_op jit(solution)/shard_map/pallas_call | solution.py:476
  15.0 2.2 %collective-permute-start.1 = (f32[192,128]{1,0:T(8,128)S(1)}, f32[192,128]{1,0:T(8,128)S(1)}, u32[]{:S(2)}, u32[]{:S(2)}) collective-permute-start(f32[192,128]{1,0:T(8,128)S(1)} %shard_map.48.refs_1_.refs_0_), channel_id=1, source_target_pairs={{0,96},{8,104},{16,112},{24,120},{32,64},{40,72},{48,80},{56,88},{... | collective-permute-start | bytes 294920 | tf_op jit(solution)/shard_map/ppermute | solution.py:495
  18.8 2.2 %shard_map.49.refs_2_.refs_0_ = f32[2,576,1152]{2,1,0:T(8,128)S(1)} custom-call(f32[2,576,1152]{2,1,0:T(8,128)S(1)} %shard_map.47.refs_2_.refs_0_, f32[192,128]{1,0:T(8,128)S(1)} %shard_map.48.refs_1_.refs_0_, f32[2,576,1152]{2,1,0:T(8,128)S(1)} %get-tuple-element.24.refs_0_.refs_1_.refs_2_.refs_3_.y.refs_5_, ...), custom_call_target="tpu_custom_call", output_to_operand_aliasing={{}: (0, {})} | custom-call | flops 1000 | bytes 1000 | tf_op jit(solution)/shard_map/pallas_call | solution.py:476
  22.6 2.4 %collective-permute-start.7 = (f32[2,24,1152]{2,1,0:T(8,128)S(1)}, f32[2,24,1152]{2,1,0:T(8,128)S(1)}, u32[]{:S(2)}, u32[]{:S(2)}) collective-permute-start(f32[2,24,1152]{2,1,0:T(8,128)S(1)} %shard_map.56), channel_id=1, source_target_pairs={{32,64},{40,72},{48,80},{56,88},{64,32},{72,40},{80,48},{88,56},{3... | collective-permute-start | bytes 663560 | tf_op jit(solution)/shard_map/ppermute | solution.py:495
  25.1 2.2 %shard_map.51.refs_2_.refs_0_ = f32[2,576,1152]{2,1,0:T(8,128)S(1)} custom-call(f32[2,576,1152]{2,1,0:T(8,128)S(1)} %shard_map.49.refs_2_.refs_0_, f32[192,128]{1,0:T(8,128)S(1)} %shard_map.50.refs_1_.refs_0_, f32[2,576,1152]{2,1,0:T(8,128)S(1)} %get-tuple-element.24.refs_0_.refs_1_.refs_2_.refs_3_.y.refs_5_, ...), custom_call_target="tpu_custom_call", output_to_operand_aliasing={{}: (0, {})} | custom-call | flops 1000 | bytes 1000 | tf_op jit(solution)/shard_map/pallas_call | solution.py:476
  27.3 3.0 %collective-permute-start.10 = (f32[192,128]{1,0:T(8,128)S(1)}, f32[192,128]{1,0:T(8,128)S(1)}, u32[]{:S(2)}, u32[]{:S(2)}) collective-permute-start(f32[192,128]{1,0:T(8,128)S(1)} %shard_map.53.refs_1_.refs_0_), channel_id=1, source_target_pairs={{0,16},{8,24},{32,48},{40,56},{64,80},{72,88},{96,112},{104,120},{... | collective-permute-start | bytes 294920 | tf_op jit(solution)/shard_map/ppermute | solution.py:495
  31.0 2.2 %shard_map.54.refs_2_.base = f32[2,576,1152]{2,1,0:T(8,128)S(1)} custom-call(f32[2,576,1152]{2,1,0:T(8,128)S(1)} %shard_map.51.refs_2_.refs_0_, f32[192,128]{1,0:T(8,128)S(1)} %shard_map.53.refs_1_.refs_0_, f32[2,576,1152]{2,1,0:T(8,128)S(1)} %get-tuple-element.24.refs_0_.refs_1_.refs_2_.refs_3_.y.refs_5_, ...), custom_call_target="tpu_custom_call", output_to_operand_aliasing={{}: (0, {})} | custom-call | flops 1000 | bytes 1000 | tf_op jit(solution)/shard_map/pallas_call | solution.py:476
  33.4 4.1 %collective-permute-start.9 = (f32[2,24,1152]{2,1,0:T(8,128)S(1)}, f32[2,24,1152]{2,1,0:T(8,128)S(1)}, u32[]{:S(2)}, u32[]{:S(2)}) collective-permute-start(f32[2,24,1152]{2,1,0:T(8,128)S(1)} %shard_map.58), channel_id=1, source_target_pairs={{8,16},{40,48},{72,80},{104,112},{16,8},{48,40},{80,72},{112,104},... | collective-permute-start | bytes 663560 | tf_op jit(solution)/shard_map/ppermute | solution.py:495
  37.8 3.3 %collective-permute-done.12.refs_1_ = f32[192,128]{1,0:T(8,128)S(1)} collective-permute-done((f32[192,128]{1,0:T(8,128)S(1)}, f32[192,128]{1,0:T(8,128)S(1)}, u32[]{:S(2)}, u32[]{:S(2)}) %collective-permute-start.12) | collective-permute-done | bytes 98336 | tf_op jit(solution)/shard_map/ppermute | solution.py:495
  41.1 5.0 %collective-permute-start.13 = (f32[192,128]{1,0:T(8,128)S(1)}, f32[192,128]{1,0:T(8,128)S(1)}, u32[]{:S(2)}, u32[]{:S(2)}) collective-permute-start(f32[192,128]{1,0:T(8,128)S(1)} %shard_map.61.refs_0_), channel_id=1, source_target_pairs={{0,3},{1,2},{4,7},{5,6},{3,0},{2,1},{7,4},{6,5},{8,11},{9,10},{12,... | collective-permute-start | bytes 294920 | tf_op jit(solution)/shard_map/ppermute | solution.py:495
  46.1 2.7 %collective-permute-done.13.refs_1_ = f32[192,128]{1,0:T(8,128)S(1)} collective-permute-done((f32[192,128]{1,0:T(8,128)S(1)}, f32[192,128]{1,0:T(8,128)S(1)}, u32[]{:S(2)}, u32[]{:S(2)}) %collective-permute-start.13) | collective-permute-done | bytes 98336 | tf_op jit(solution)/shard_map/ppermute | solution.py:495
  48.8 5.6 %shard_map.63 = (f32[2,576,1152]{2,1,0:T(8,128)S(1)}, f32[432,128]{1,0:T(8,128)S(1)}, f32[432,128]{1,0:T(8,128)S(1)}, f32[288,128]{1,0:T(8,128)S(1)}, f32[2,24,1...) custom-call(f32[2,576,1152]{2,1,0:T(8,128)S(1)} %shard_map.54.refs_2_.ba, ...), custom_call_target="tpu_custom_call" | custom-call | flops 1000 | bytes 1000 | tf_op jit(solution)/shard_map/pallas_call | solution.py:476
  54.3 2.2 %shard_map.64.refs_0_.refs_1_ = f32[2,576,1152]{2,1,0:T(8,128)S(1)} custom-call(f32[2,576,1152]{2,1,0:T(8,128)S(1)} %get-tuple-element.35.refs_0_.refs_1_.refs_4_.y1, f32[2,576,1152]{2,1,0:T(8,128)S(1)} %get-tuple-element.24.refs_0_.refs_1_.refs_2_.refs_3_.y.refs_5_, f32[9,576,128]{2,1,0:T(8,128)S(1)} %get-tuple-element.25.refs_2_.refs_4_.refs_8_.refs_3_.refs_6_, ...), custom_call_target="tpu_custom_call" | custom-call | flops 1000 | bytes 1000 | tf_op jit(solution)/shard_map/pallas_call | solution.py:476
  56.8 2.2 %shard_map.65.refs_0_ = f32[2,576,1152]{2,1,0:T(8,128)S(1)} custom-call(f32[2,576,1152]{2,1,0:T(8,128)S(1)} %shard_map.64.refs_0_.refs_1_, f32[2,576,1152]{2,1,0:T(8,128)S(1)} %get-tuple-element.35.refs_0_.refs_1_.refs_4_.y1, f32[2,576,1152]{2,1,0:T(8,128)S(1)} %get-tuple-element.24.refs_0_.refs_1_.refs_2_.refs_3_.y.refs_5_, ...), custom_call_target="tpu_custom_call", output_to_operand_aliasing={{}: (0, {})} | custom-call | flops 1000 | bytes 1000 | tf_op jit(solution)/shard_map/pallas_call | solution.py:476
  59.1 3.2 %collective-permute-start.16 = (f32[2,24,1152]{2,1,0:T(8,128)S(1)}, f32[2,24,1152]{2,1,0:T(8,128)S(1)}, u32[]{:S(2)}, u32[]{:S(2)}) collective-permute-start(f32[2,24,1152]{2,1,0:T(8,128)S(1)} %shard_map.69), channel_id=1, source_target_pairs={{32,64},{40,72},{48,80},{56,88},{64,32},{72,40},{80,48},{88,56},{3... | collective-permute-start | bytes 663560 | tf_op jit(solution)/shard_map/ppermute | solution.py:495
  62.2 3.9 %collective-permute-start.17 = (f32[432,128]{1,0:T(8,128)S(1)}, f32[432,128]{1,0:T(8,128)S(1)}, u32[]{:S(2)}, u32[]{:S(2)}) collective-permute-start(f32[432,128]{1,0:T(8,128)S(1)} %get-tuple-element.39), channel_id=1, source_target_pairs={{0,2},{1,3},{4,6},{5,7},{2,0},{3,1},{6,4},{7,5},{8,10},{9,11},{12,... | collective-permute-start | bytes 663560 | tf_op jit(solution)/shard_map/ppermute | solution.py:495
  68.1 2.2 %shard_map.66.refs_0_.refs_1_ = f32[2,576,1152]{2,1,0:T(8,128)S(1)} custom-call(f32[2,576,1152]{2,1,0:T(8,128)S(1)} %shard_map.65.refs_0_, f32[2,576,1152]{2,1,0:T(8,128)S(1)} %get-tuple-element.35.refs_0_.refs_1_.refs_4_.y1, f32[2,576,1152]{2,1,0:T(8,128)S(1)} %get-tuple-element.24.refs_0_.refs_1_.refs_2_.refs_3_.y.refs_5_, ...), custom_call_target="tpu_custom_call", output_to_operand_aliasing={{}: (0, {})} | custom-call | flops 1000 | bytes 1000 | tf_op jit(solution)/shard_map/pallas_call | solution.py:476
  70.4 4.5 %collective-permute-start.19 = (f32[2,24,1152]{2,1,0:T(8,128)S(1)}, f32[2,24,1152]{2,1,0:T(8,128)S(1)}, u32[]{:S(2)}, u32[]{:S(2)}) collective-permute-start(f32[2,24,1152]{2,1,0:T(8,128)S(1)} %shard_map.71), channel_id=1, source_target_pairs={{0,8},{16,24},{32,40},{48,56},{64,72},{80,88},{96,104},{112,120},{... | collective-permute-start | bytes 663560 | tf_op jit(solution)/shard_map/ppermute | solution.py:495
  76.8 2.2 %shard_map.70.base = f32[2,576,1152]{2,1,0:T(8,128)S(1)} custom-call(f32[2,576,1152]{2,1,0:T(8,128)S(1)} %shard_map.66.refs_0_.refs_1_, f32[288,128]{1,0:T(8,128)S(1)} %collective-permute-done.14.refs_1_.refs_2_, f32[2,24,1152]{2,1,0:T(8,128)S(1)} %collective-permute-done.15.refs_2_.refs_3_, ...), custom_call_target="tpu_custom_call", output_to_operand_aliasing={{}: (0, {})} | custom-call | flops 1000 | bytes 1000 | tf_op jit(solution)/shard_map/pallas_call | solution.py:476
  79.1 3.1 %collective-permute-done.20.refs_6_ = f32[2,24,1152]{2,1,0:T(8,128)S(1)} collective-permute-done((f32[2,24,1152]{2,1,0:T(8,128)S(1)}, f32[2,24,1152]{2,1,0:T(8,128)S(1)}, u32[]{:S(2)}, u32[]{:S(2)}) %collective-permute-start.20) | collective-permute-done | bytes 221216 | tf_op jit(solution)/shard_map/ppermute | solution.py:495
  82.1 5.4 %shard_map.73 = f32[2,576,1152]{2,1,0:T(8,128)} custom-call(f32[2,576,1152]{2,1,0:T(8,128)S(1)} %shard_map.70.base, f32[2,576,1152]{2,1,0:T(8,128)S(1)} %get-tuple-element.35.refs_0_.refs_1_.refs_4_.y1, f32[432,128]{1,0:T(8,128)S(1)} %collective-permute-done.17.refs_0_, f32[432,128]{1,0:T(8,128)S(1)} %collective-permute-done.18.refs_1_, ...), custom_call_target="tpu_custom_call" | custom-call | flops 1000 | bytes 1000 | tf_op jit(solution)/shard_map/pallas_call | solution.py:476
  (46 shorter events, 8.7 us)
Async XLA Ops:
  7.2 7.8 %collective-permute-start = (f32[192,128]{1,0:T(8,128)S(1)}, f32[192,128]{1,0:T(8,128)S(1)}, u32[]{:S(2)}, u32[]{:S(2)}) collective-permute-start(f32[192,128]{1,0:T(8,128)S(1)} %get-tuple-element.27.refs_0_), channel_id=1, source_target_pairs={{0,32},{8,40},{16,48},{24,56},{64,96},{72,104},{80,112},{88,120},{... | collective-permute-start | bytes 294920 | tf_op jit(solution)/shard_map/ppermute | solution.py:495
  7.3 15.4 %collective-permute-start.4 = (f32[432,128]{1,0:T(8,128)S(1)}, f32[432,128]{1,0:T(8,128)S(1)}, u32[]{:S(2)}, u32[]{:S(2)}) collective-permute-start(f32[432,128]{1,0:T(8,128)S(1)} %get-tuple-element.29), channel_id=1, source_target_pairs={{0,2},{1,3},{4,6},{5,7},{2,0},{3,1},{6,4},{7,5},{8,10},{9,11},{12,... | collective-permute-start | bytes 663560 | tf_op jit(solution)/shard_map/ppermute | solution.py:495
  9.2 18.0 %collective-permute-start.5 = (f32[432,128]{1,0:T(8,128)S(1)}, f32[432,128]{1,0:T(8,128)S(1)}, u32[]{:S(2)}, u32[]{:S(2)}) collective-permute-start(f32[432,128]{1,0:T(8,128)S(1)} %get-tuple-element.30), channel_id=1, source_target_pairs={{2,4},{3,5},{4,2},{5,3},{10,12},{11,13},{12,10},{13,11},{18,20},{1... | collective-permute-start | bytes 663560 | tf_op jit(solution)/shard_map/ppermute | solution.py:495
  15.0 6.0 %collective-permute-start.1 = (f32[192,128]{1,0:T(8,128)S(1)}, f32[192,128]{1,0:T(8,128)S(1)}, u32[]{:S(2)}, u32[]{:S(2)}) collective-permute-start(f32[192,128]{1,0:T(8,128)S(1)} %shard_map.48.refs_1_.refs_0_), channel_id=1, source_target_pairs={{0,96},{8,104},{16,112},{24,120},{32,64},{40,72},{48,80},{56,88},{... | collective-permute-start | bytes 294920 | tf_op jit(solution)/shard_map/ppermute | solution.py:495
  17.2 10.1 %collective-permute-start.3 = (f32[288,128]{1,0:T(8,128)S(1)}, f32[288,128]{1,0:T(8,128)S(1)}, u32[]{:S(2)}, u32[]{:S(2)}) collective-permute-start(f32[288,128]{1,0:T(8,128)S(1)} %shard_map.52), channel_id=1, source_target_pairs={{0,1},{2,3},{4,5},{6,7},{1,0},{3,2},{5,4},{7,6},{8,9},{10,11},{12,... | collective-permute-start | bytes 442376 | tf_op jit(solution)/shard_map/ppermute | solution.py:495
  18.0 15.2 %collective-permute-start.6 = (f32[2,24,1152]{2,1,0:T(8,128)S(1)}, f32[2,24,1152]{2,1,0:T(8,128)S(1)}, u32[]{:S(2)}, u32[]{:S(2)}) collective-permute-start(f32[2,24,1152]{2,1,0:T(8,128)S(1)} %shard_map.55), channel_id=1, source_target_pairs={{0,32},{8,40},{16,48},{24,56},{64,96},{72,104},{80,112},{88,120},{... | collective-permute-start | bytes 663560 | tf_op jit(solution)/shard_map/ppermute | solution.py:495
  21.0 6.3 %collective-permute-start.2 = (f32[192,128]{1,0:T(8,128)S(1)}, f32[192,128]{1,0:T(8,128)S(1)}, u32[]{:S(2)}, u32[]{:S(2)}) collective-permute-start(f32[192,128]{1,0:T(8,128)S(1)} %shard_map.50.refs_1_.refs_0_), channel_id=1, source_target_pairs={{0,8},{16,24},{32,40},{48,56},{64,72},{80,88},{96,104},{112,120},{... | collective-permute-start | bytes 294920 | tf_op jit(solution)/shard_map/ppermute | solution.py:495
  22.6 14.8 %collective-permute-start.7 = (f32[2,24,1152]{2,1,0:T(8,128)S(1)}, f32[2,24,1152]{2,1,0:T(8,128)S(1)}, u32[]{:S(2)}, u32[]{:S(2)}) collective-permute-start(f32[2,24,1152]{2,1,0:T(8,128)S(1)} %shard_map.56), channel_id=1, source_target_pairs={{32,64},{40,72},{48,80},{56,88},{64,32},{72,40},{80,48},{88,56},{3... | collective-permute-start | bytes 663560 | tf_op jit(solution)/shard_map/ppermute | solution.py:495
  27.3 6.0 %collective-permute-start.10 = (f32[192,128]{1,0:T(8,128)S(1)}, f32[192,128]{1,0:T(8,128)S(1)}, u32[]{:S(2)}, u32[]{:S(2)}) collective-permute-start(f32[192,128]{1,0:T(8,128)S(1)} %shard_map.53.refs_1_.refs_0_), channel_id=1, source_target_pairs={{0,16},{8,24},{32,48},{40,56},{64,80},{72,88},{96,112},{104,120},{... | collective-permute-start | bytes 294920 | tf_op jit(solution)/shard_map/ppermute | solution.py:495
  30.4 7.4 %collective-permute-start.8 = (f32[2,24,1152]{2,1,0:T(8,128)S(1)}, f32[2,24,1152]{2,1,0:T(8,128)S(1)}, u32[]{:S(2)}, u32[]{:S(2)}) collective-permute-start(f32[2,24,1152]{2,1,0:T(8,128)S(1)} %shard_map.57), channel_id=1, source_target_pairs={{0,8},{16,24},{32,40},{48,56},{64,72},{80,88},{96,104},{112,120},{... | collective-permute-start | bytes 663560 | tf_op jit(solution)/shard_map/ppermute | solution.py:495
  33.3 4.2 %collective-permute-start.11 = (f32[192,128]{1,0:T(8,128)S(1)}, f32[192,128]{1,0:T(8,128)S(1)}, u32[]{:S(2)}, u32[]{:S(2)}) collective-permute-start(f32[192,128]{1,0:T(8,128)S(1)} %shard_map.59.refs_0_), channel_id=1, source_target_pairs={{0,20},{1,21},{2,22},{3,23},{4,16},{5,17},{6,18},{7,19},{8,28},{9,... | collective-permute-start | bytes 294920 | tf_op jit(solution)/shard_map/ppermute | solution.py:547
  33.4 12.6 %collective-permute-start.9 = (f32[2,24,1152]{2,1,0:T(8,128)S(1)}, f32[2,24,1152]{2,1,0:T(8,128)S(1)}, u32[]{:S(2)}, u32[]{:S(2)}) collective-permute-start(f32[2,24,1152]{2,1,0:T(8,128)S(1)} %shard_map.58), channel_id=1, source_target_pairs={{8,16},{40,48},{72,80},{104,112},{16,8},{48,40},{80,72},{112,104},... | collective-permute-start | bytes 663560 | tf_op jit(solution)/shard_map/ppermute | solution.py:495
  37.5 3.5 %collective-permute-start.12 = (f32[192,128]{1,0:T(8,128)S(1)}, f32[192,128]{1,0:T(8,128)S(1)}, u32[]{:S(2)}, u32[]{:S(2)}) collective-permute-start(f32[192,128]{1,0:T(8,128)S(1)} %shard_map.60.refs_0_), channel_id=1, source_target_pairs={{0,1},{2,3},{4,5},{6,7},{1,0},{3,2},{5,4},{7,6},{8,9},{10,11},{12,... | collective-permute-start | bytes 294920 | tf_op jit(solution)/shard_map/ppermute | solution.py:495
  41.1 7.7 %collective-permute-start.13 = (f32[192,128]{1,0:T(8,128)S(1)}, f32[192,128]{1,0:T(8,128)S(1)}, u32[]{:S(2)}, u32[]{:S(2)}) collective-permute-start(f32[192,128]{1,0:T(8,128)S(1)} %shard_map.61.refs_0_), channel_id=1, source_target_pairs={{0,3},{1,2},{4,7},{5,6},{3,0},{2,1},{7,4},{6,5},{8,11},{9,10},{12,... | collective-permute-start | bytes 294920 | tf_op jit(solution)/shard_map/ppermute | solution.py:495
  56.6 18.3 %collective-permute-start.15 = (f32[2,24,1152]{2,1,0:T(8,128)S(1)}, f32[2,24,1152]{2,1,0:T(8,128)S(1)}, u32[]{:S(2)}, u32[]{:S(2)}) collective-permute-start(f32[2,24,1152]{2,1,0:T(8,128)S(1)} %shard_map.68), channel_id=1, source_target_pairs={{0,32},{8,40},{16,48},{24,56},{64,96},{72,104},{80,112},{88,120},{... | collective-permute-start | bytes 663560 | tf_op jit(solution)/shard_map/ppermute | solution.py:495
  56.7 13.6 %collective-permute-start.14 = (f32[288,128]{1,0:T(8,128)S(1)}, f32[288,128]{1,0:T(8,128)S(1)}, u32[]{:S(2)}, u32[]{:S(2)}) collective-permute-start(f32[288,128]{1,0:T(8,128)S(1)} %shard_map.67), channel_id=1, source_target_pairs={{0,1},{2,3},{4,5},{6,7},{1,0},{3,2},{5,4},{7,6},{8,9},{10,11},{12,... | collective-permute-start | bytes 442376 | tf_op jit(solution)/shard_map/ppermute | solution.py:495
  59.1 17.8 %collective-permute-start.16 = (f32[2,24,1152]{2,1,0:T(8,128)S(1)}, f32[2,24,1152]{2,1,0:T(8,128)S(1)}, u32[]{:S(2)}, u32[]{:S(2)}) collective-permute-start(f32[2,24,1152]{2,1,0:T(8,128)S(1)} %shard_map.69), channel_id=1, source_target_pairs={{32,64},{40,72},{48,80},{56,88},{64,32},{72,40},{80,48},{88,56},{3... | collective-permute-start | bytes 663560 | tf_op jit(solution)/shard_map/ppermute | solution.py:495
  62.2 16.8 %collective-permute-start.17 = (f32[432,128]{1,0:T(8,128)S(1)}, f32[432,128]{1,0:T(8,128)S(1)}, u32[]{:S(2)}, u32[]{:S(2)}) collective-permute-start(f32[432,128]{1,0:T(8,128)S(1)} %get-tuple-element.39), channel_id=1, source_target_pairs={{0,2},{1,3},{4,6},{5,7},{2,0},{3,1},{6,4},{7,5},{8,10},{9,11},{12,... | collective-permute-start | bytes 663560 | tf_op jit(solution)/shard_map/ppermute | solution.py:495
  66.2 12.9 %collective-permute-start.18 = (f32[432,128]{1,0:T(8,128)S(1)}, f32[432,128]{1,0:T(8,128)S(1)}, u32[]{:S(2)}, u32[]{:S(2)}) collective-permute-start(f32[432,128]{1,0:T(8,128)S(1)} %get-tuple-element.40), channel_id=1, source_target_pairs={{2,4},{3,5},{4,2},{5,3},{10,12},{11,13},{12,10},{13,11},{18,20},{1... | collective-permute-start | bytes 663560 | tf_op jit(solution)/shard_map/ppermute | solution.py:495
  70.4 8.7 %collective-permute-start.19 = (f32[2,24,1152]{2,1,0:T(8,128)S(1)}, f32[2,24,1152]{2,1,0:T(8,128)S(1)}, u32[]{:S(2)}, u32[]{:S(2)}) collective-permute-start(f32[2,24,1152]{2,1,0:T(8,128)S(1)} %shard_map.71), channel_id=1, source_target_pairs={{0,8},{16,24},{32,40},{48,56},{64,72},{80,88},{96,104},{112,120},{... | collective-permute-start | bytes 663560 | tf_op jit(solution)/shard_map/ppermute | solution.py:495
  74.9 7.2 %collective-permute-start.20 = (f32[2,24,1152]{2,1,0:T(8,128)S(1)}, f32[2,24,1152]{2,1,0:T(8,128)S(1)}, u32[]{:S(2)}, u32[]{:S(2)}) collective-permute-start(f32[2,24,1152]{2,1,0:T(8,128)S(1)} %shard_map.72), channel_id=1, source_target_pairs={{8,16},{40,48},{72,80},{104,112},{16,8},{48,40},{80,72},{112,104},... | collective-permute-start | bytes 663560 | tf_op jit(solution)/shard_map/ppermute | solution.py:495

commit v2 on v1

--- a/solution.py
+++ b/solution.py
@@ -45,14 +45,18 @@
     return pl.ds(t * LANES, LANES)
 
 
-def weights(bonds, roww, colw):
-    row_id, col_id = place()
+def tables(bonds):
     side = (LATTICE, LATTICE)
     down = jnp.where(iota(side, 0) < LATTICE - 1, bonds[0], 0.0)
     across = jnp.where(iota(side, 1) < LATTICE - 1, bonds[1], 0.0)
     rep = bonds[2]
     dot = functools.partial(jnp.dot, precision=lax.Precision.HIGHEST, preferred_element_type=F32)
-
+    return down, across, rep, dot
+
+
+def row_weights_kernel(bonds, roww):
+    row_id, _ = place()
+    down, across, rep, dot = tables(bonds)
     s = iota((SQUARE, LATTICE), 0)
     lane = iota((SQUARE, LATTICE), 1)
     a = over24(s)
@@ -79,6 +83,11 @@
     for k, v in values.items():
         roww[k] = jnp.broadcast_to(v, (SQUARE, LANES))
 
+
+def col_weights(bonds, colw):
+    _, col_id = place()
+    down, across, rep, dot = tables(bonds)
+    last = PATCH - 1
     wide = (LATTICE, COLUMNS)
     j = iota(wide, 1)
     g = (j >= SQUARE).astype(jnp.int32)
@@ -148,7 +157,7 @@
 QUARTER = SQUARE // 4
 
 
-def pack_faces(src, face_a, face_b, side, down_a, down_b, across_a, across_b):
+def pack_faces(src, face_a, face_b, side, down_a, down_b, across_a, across_b, ready=None):
     up_first, even, row_up_first, row_even = parities()
     base = jnp.where(even, 4 * LANES, 0)
     lane, lane24 = lane_maps()
@@ -194,7 +203,13 @@
             side[at[h], :] = msg
         return carry
 
-    lax.fori_loop(0, PATCH // 4, step, 0)
+    steps = PATCH // 4
+    if ready is None:
+        lax.fori_loop(0, steps, step, 0)
+    else:
+        for i in range(CHUNKS):
+            ready(i)
+            lax.fori_loop(i * steps // CHUNKS, (i + 1) * steps // CHUNKS, step, 0)
     for p in range(2):
         for out, flip in ((down_a, row_up_first), (down_b, jnp.logical_not(row_up_first))):
             out[p] = src[p, pl.ds(pl.multiple_of(jnp.where(flip, SQUARE - PATCH, 0), 8), PATCH), :]
@@ -208,7 +223,7 @@
 SLOT = 24
 
 
-def pack_densities(src, colw, table, row_sums, slots):
+def pack_densities(src, colw, table, row_sums, slots, sums, codes):
     row_id, col_id = place()
     odd = lax.rem(row_id, 2)
     across = lax.rem(row_id, 4) - 2 * lax.rem(col_id, 2)
@@ -221,40 +236,56 @@
     def _():
         slots[...] = jnp.zeros(slots.shape, F32)
         row_sums[...] = jnp.zeros(row_sums.shape, F32)
+        sums[...] = jnp.zeros(sums.shape, F32)
         lane = iota((8, LANES), 1)
         sub = iota((8, LANES), 0)
-        codes = []
         for t in range(TILES):
             j = lane + t * LANES
             g = (j >= SQUARE).astype(jnp.int32)
             a = over24(j - SQUARE * g)
             b = j - SQUARE * g - PATCH * a
-            codes.append(100 * (PATCH * (col_id // 2) + a) + PATCH * (2 * lax.rem(col_id, 2) + g) + b)
+            codes[t] = 100 * (PATCH * (col_id // 2) + a) + PATCH * (2 * lax.rem(col_id, 2) + g) + b
         first = 100 * PATCH * (row_id // 4) + PATCH * lax.rem(row_id, 4)
 
-        def step(a, sums):
-            sums = list(sums)
+        def share(a, tiles):
+            along_rows = [jnp.zeros((8, LANES), F32) for _ in range(3)]
+            for t in tiles:
+                cols = pl.ds(pl.multiple_of(t * LANES, LANES), LANES)
+                now = middle = jnp.zeros((8, LANES), F32)
+                for k in range(3):
+                    rows = pl.ds(pl.multiple_of(a * PATCH + 8 * k, 8), 8)
+                    apart = first + 100 * a + 8 * k + sub - codes[t]
+                    w = jnp.where(apart == 100, colw[C_DN_ALL, :, cols], 0.0)
+                    w = jnp.where(apart == -100, colw[C_UP_ALL, :, cols], w)
+                    w = jnp.where(apart == 1, colw[C_RT_ALL, :, cols], w)
+                    w = jnp.where(apart == -1, colw[C_LF_ALL, :, cols], w)
+                    flow = w * src[1, rows, cols]
+                    own = jnp.where(apart == 0, src[0, rows, cols], 0.0)
+                    now = now + own
+                    middle = middle + own - flow
+                    along_rows[k] = along_rows[k] + flow
+                sums[0, t] += now
+                sums[1, t] += middle
             for k in range(3):
-                here = pl.multiple_of(a * PATCH + 8 * k, 8)
-                mine = first + 100 * a + 8 * k + sub
-                along_row = None
-                for t in range(TILES):
-                    apart = mine - codes[t]
-                    w = jnp.where(apart == 100, colw[C_DN_ALL, :, tile(t)], 0.0)
-                    w = jnp.where(apart == -100, colw[C_UP_ALL, :, tile(t)], w)
-                    w = jnp.where(apart == 1, colw[C_RT_ALL, :, tile(t)], w)
-                    w = jnp.where(apart == -1, colw[C_LF_ALL, :, tile(t)], w)
-                    flow = w * src[1, pl.ds(here, 8), tile(t)]
-                    sums[t] = sums[t] - flow + jnp.where(apart == 0, src[0, pl.ds(here, 8), tile(t)], 0.0)
-                    sums[TILES + t] = sums[TILES + t] + jnp.where(apart == 0, src[0, pl.ds(here, 8), tile(t)], 0.0)
-                    along_row = flow if along_row is None else along_row + flow
-                row_sums[pl.ds(64 * odd + here, 8), :] = along_row
-            return tuple(sums)
-
-        sums = lax.fori_loop(0, PATCH, step, (jnp.zeros((8, LANES), F32),) * (2 * TILES))
+                row_sums[pl.ds(pl.multiple_of(64 * odd + a * PATCH + 8 * k, 8), 8), :] = along_rows[k]
+
+        @pl.when(beside)
+        def _():
+            def step(a, carry):
+                starts = [jnp.clip(SQUARE * g + PATCH * (a - 1), 0, (TILES - 2) * LANES) // LANES for g in range(2)]
+                share(a, [start + d for start in starts for d in range(2)])
+                return carry
+
+            lax.fori_loop(0, PATCH, step, 0)
+
+        @pl.when(over)
+        def _():
+            start = jnp.where(along == 1, 4, 0)
+            share(jnp.where(along == 1, 0, PATCH - 1), [start, start + 4])
+
         for t in range(TILES):
-            slots[0, t : t + 1, :] = jnp.sum(sums[TILES + t], axis=0, keepdims=True)
-            slots[0, TILES + t : TILES + t + 1, :] = jnp.sum(sums[t], axis=0, keepdims=True)
+            slots[0, t : t + 1, :] = jnp.sum(sums[0, t], axis=0, keepdims=True)
+            slots[0, TILES + t : TILES + t + 1, :] = jnp.sum(sums[1, t], axis=0, keepdims=True)
         for t in range(5):
             got = jnp.sum(row_sums[t * LANES : (t + 1) * LANES, :].T, axis=0, keepdims=True)
             slots[1, pl.ds(TILES + 4 * odd + t, 1), :] = got
@@ -262,88 +293,101 @@
         table[pl.ds(pl.multiple_of(SLOT * (row_id // 2), 8), SLOT), :] += slots[1]
 
 
-def first_kernel(corr, down, across, rep, y, roww, colw, *refs):
-    faces, table, (row_sums, slots, bonds, sems) = refs[:7], refs[7], refs[8:]
-    copies = [pltpu.make_async_copy(v, bonds.at[n], sems.at[n]) for n, v in enumerate((down, across, rep))]
-    copies += [pltpu.make_async_copy(corr.at[p], y.at[p], sems.at[3 + p]) for p in range(2)]
-    for c in copies:
+CHUNKS = 3
+
+
+def first_kernel(corr, down, across, rep, y, bonds, colw, *refs):
+    faces, table, (*scratch, sems) = refs[:7], refs[7], refs[8:]
+    tables_in = [pltpu.make_async_copy(v, bonds.at[n], sems.at[n]) for n, v in enumerate((down, across, rep))]
+    step = QUARTER // CHUNKS
+    chunks = []
+    for i in range(CHUNKS):
+        chunks.append([])
+        for q in range(4):
+            for p in range(2):
+                rows = pl.ds(q * QUARTER + i * step, step)
+                sem = sems.at[3 + (i * 4 + q) * 2 + p]
+                chunks[-1].append(pltpu.make_async_copy(corr.at[p, rows], y.at[p, rows], sem))
+    for c in sum([tables_in, *chunks], []):
         c.start()
-    for c in copies[:3]:
+    for c in tables_in:
         c.wait()
-    weights(bonds, roww, colw)
-    for c in copies[3:]:
-        c.wait()
-    pack_faces(y, *faces)
-    pack_densities(y, colw, table, row_sums, slots)
-
-
-def hop_strip(src, q, a, roww, colw):
+    col_weights(bonds, colw)
+
+    def ready(i):
+        for c in chunks[i]:
+            c.wait()
+
+    pack_faces(y, *faces, ready=ready)
+    pack_densities(y, colw, table, *scratch)
+
+
+def interior_kernel(final, first, last, *refs):
+    y1, y, roww, colw, out = refs[-5:]
     sub = iota((8, LANES), 0)
     lane, lane24 = lane_maps((8, LANES))
-    here = pl.multiple_of(a * PATCH, 8)
-    above = pl.multiple_of(jnp.maximum(a - 1, 0) * PATCH, 8)
-    below = pl.multiple_of(jnp.minimum(a + 1, PATCH - 1) * PATCH, 8)
-    x = [[src[q, pl.ds(here + 8 * k, 8), tile(t)] for t in range(TILES)] for k in range(3)]
-    out = [[None] * TILES for _ in range(3)]
-    rw = [[roww[n, pl.ds(here + 8 * k, 8), :] for n in (DN_IN, UP_IN, RT_IN, LF_IN)] for k in range(3)]
-    for t in range(TILES):
-        fwd = [pltpu.roll(x[k][t], 1, 0) for k in range(3)]
-        bwd = [pltpu.roll(x[k][t], 7, 0) for k in range(3)]
-        for k in range(3):
-            left = fwd[0] if k == 0 else jnp.where(sub == 0, fwd[k - 1], fwd[k])
-            right = bwd[2] if k == 2 else jnp.where(sub == 7, bwd[k + 1], bwd[k])
-            dn, up, rt, lf = rw[k]
-            out[k][t] = (
-                dn * src[q, pl.ds(below + 8 * k, 8), tile(t)]
-                + up * src[q, pl.ds(above + 8 * k, 8), tile(t)]
-                + rt * right
-                + lf * left
-            )
-    for k in range(3):
-        row = x[k]
-        r1 = [pltpu.roll(v, 1, 1) for v in row]
-        l1 = [pltpu.roll(v, LANES - 1, 1) for v in row]
-        r24 = [pltpu.roll(v, PATCH, 1) for v in row]
-        l24 = [pltpu.roll(v, LANES - PATCH, 1) for v in row]
-        te, tf = [pltpu.roll(v, 41, 1) for v in squeeze_cols(row[0:5], lane24, 15, 7, 23)]
-        he, hf = [pltpu.roll(v, 87, 1) for v in squeeze_cols(row[4:9], lane24, 8, 0, 16)]
+    three = range(3)
+
+    def strip(a, p):
+        q = 1 - p
+        here = pl.multiple_of(a * PATCH, 8)
+        above = pl.multiple_of(jnp.maximum(a - 1, 0) * PATCH, 8)
+        below = pl.multiple_of(jnp.minimum(a + 1, PATCH - 1) * PATCH, 8)
+
+        def at(t, k, start=here):
+            return y1[q, pl.ds(start + 8 * k, 8), tile(t)]
+
+        def side(t0, m1, m2, n0, shift):
+            pairs = [squeeze_cols([at(t0 + t, k) for t in range(5)], lane24, m1, m2, n0) for k in three]
+            return [[pltpu.roll(v, shift, 1) for v in pair] for pair in pairs]
+
+        def turned(t):
+            x = [at(t, k) for k in three]
+            return [[pltpu.roll(v, n, 1) for v in x] for n in (1, PATCH, LANES - 1, LANES - PATCH)]
+
+        heads = side(4, 8, 0, 16, 87)
+        tails = None
+        before, now = None, turned(0)
         for t in range(TILES):
+            later = turned(t + 1) if t < TILES - 1 else None
+            if t == 4:
+                tails = side(0, 15, 7, 23, 41)
+            x = [at(t, k) for k in three]
+            fwd = [pltpu.roll(v, 1, 0) for v in x]
+            bwd = [pltpu.roll(v, 7, 0) for v in x]
             w = lambda n: colw[n, :, tile(t)]
-            minus_b = r1[t] if t == 0 else jnp.where(lane < 1, r1[t - 1], r1[t])
-            plus_b = l1[t] if t == TILES - 1 else jnp.where(lane >= LANES - 1, l1[t + 1], l1[t])
-            minus_a = r24[t] if t == 0 else jnp.where(lane < PATCH, r24[t - 1], r24[t])
-            plus_a = l24[t] if t == TILES - 1 else jnp.where(lane >= LANES - PATCH, l24[t + 1], l24[t])
-            acc = out[k][t] + w(C_DN) * plus_a + w(C_UP) * minus_a + w(C_RT) * plus_b + w(C_LF) * minus_b
-            if t <= 3:
-                acc = acc + w(C_RT_E) * he
-            if t in (0, 3, 4):
-                acc = acc + w(C_RT_F) * hf
-            if 5 <= t <= 8:
-                acc = acc + w(C_LF_E) * te
-            if t in (4, 5, 8):
-                acc = acc + w(C_LF_F) * tf
-            out[k][t] = acc
-    return out
-
-
-def interior_kernel(final, first, last, *refs):
-    y1, y, roww, colw, out = refs[-5:]
+            for k in three:
+                rows = pl.ds(here + 8 * k, 8)
+                rw = lambda n: roww[n, rows, :]
+                left = fwd[0] if k == 0 else jnp.where(sub == 0, fwd[k - 1], fwd[k])
+                right = bwd[2] if k == 2 else jnp.where(sub == 7, bwd[k + 1], bwd[k])
+                minus_b = now[0][k] if t == 0 else jnp.where(lane < 1, before[0][k], now[0][k])
+                minus_a = now[1][k] if t == 0 else jnp.where(lane < PATCH, before[1][k], now[1][k])
+                plus_b = now[2][k] if later is None else jnp.where(lane >= LANES - 1, later[2][k], now[2][k])
+                plus_a = now[3][k] if later is None else jnp.where(lane >= LANES - PATCH, later[3][k], now[3][k])
+                acc = rw(DN_IN) * at(t, k, below) + rw(UP_IN) * at(t, k, above) + rw(RT_IN) * right + rw(LF_IN) * left
+                acc = acc + w(C_DN) * plus_a + w(C_UP) * minus_a + w(C_RT) * plus_b + w(C_LF) * minus_b
+                if t <= 3:
+                    acc = acc + w(C_RT_E) * heads[k][0]
+                if t in (0, 3, 4):
+                    acc = acc + w(C_RT_F) * heads[k][1]
+                if 5 <= t <= 8:
+                    acc = acc + w(C_LF_E) * tails[k][0]
+                if t in (4, 5, 8):
+                    acc = acc + w(C_LF_F) * tails[k][1]
+                old = y1[p, rows, tile(t)]
+                if final:
+                    old = old + y[p, rows, tile(t)]
+                new = old + acc if p == 0 else old - acc
+                out[p, rows, tile(t)] = 0.5 * new if final else new
+            before, now = now, later
 
     def step(a, carry):
-        here = pl.multiple_of(a * PATCH, 8)
         for p in range(2):
-            hops = hop_strip(y1, 1 - p, a, roww, colw)
-            for k in range(3):
-                rows = pl.ds(here + 8 * k, 8)
-                for t in range(TILES):
-                    old = y1[p, rows, tile(t)]
-                    if final:
-                        old = old + y[p, rows, tile(t)]
-                    new = old + hops[k][t] if p == 0 else old - hops[k][t]
-                    out[p, rows, tile(t)] = 0.5 * new if final else new
+            strip(a, p)
         return carry
 
-    lax.fori_loop(first, last, step, 0)
+    lax.fori_loop(first, last, step, 0, unroll=next(n for n in (4, 3, 2, 1) if (last - first) % n == 0))
 
 
 def unfolded(msg, at, lane):
@@ -430,14 +474,15 @@
                     out[p, rows, tile(t)] += w * jnp.where(row_up_first, pair[0], pair[1])
 
     fold = 3 * PATCH // 4
-    lax.fori_loop(0, fold, lambda a, c: (strip(a, False), c)[1], 0)
-    rim(0, UP_RIM, down_b, down_a)
-    if chunk_done is not None:
-        chunk_done(0, fold * PATCH)
-    lax.fori_loop(fold, PATCH, lambda a, c: (strip(a, True), c)[1], 0)
-    rim(PATCH - 1, DN_RIM, down_a, down_b)
-    if chunk_done is not None:
-        chunk_done(fold * PATCH, SQUARE)
+    stops = (0, fold, PATCH) if chunk_done is None else (0, fold // 3, 2 * fold // 3, fold, PATCH - 2, PATCH)
+    for start, stop in zip(stops, stops[1:]):
+        lax.fori_loop(start, stop, lambda a, c, f=start >= fold: (strip(a, f), c)[1], 0, unroll=2)
+        if start == 0:
+            rim(0, UP_RIM, down_b, down_a)
+        if stop == PATCH:
+            rim(PATCH - 1, DN_RIM, down_a, down_b)
+        if chunk_done is not None:
+            chunk_done(start * PATCH, stop * PATCH)
 
 
 def middle_kernel(base, y, *refs):
@@ -547,29 +592,26 @@
     return lax.ppermute(x, ("row", "col"), route)
 
 
-def first_exchange(faces, table, piece):
+def first_exchange(faces, table, first_work, piece):
     face_a, face_b, side, down_a, down_b, across_a, across_b = faces
     face_a, face_b = swap_face_a(face_a), swap_face_b(face_b)
-    got = flipped(table, "row", 4)
-    part = piece(0, None)
-    table = merged(table, got, part)
-    got = flipped(table, "row", 12)
+    table = merged(table, flipped(table, "row", 4), first_work)
     side = swap_side(tie(side, table))
+    part = piece(0, None, table)
+    table = merged(table, flipped(table, "row", 12), part)
     down_a = swap_down_a(tie(down_a, table))
+    table = merged(table, flipped(table, "row", 1), face_a, face_b)
+    down_b = swap_down_b(tie(down_b, table))
     part = piece(1, part, table)
-    table = merged(table, got, part)
-    got = flipped(table, "row", 1)
-    down_b = swap_down_b(tie(down_b, table))
+    table = merged(table, flipped(table, "row", 2), part, side)
+    across_a = swap_across_a(tie(across_a, table))
     part = piece(2, part, table)
-    table = merged(table, got, part, side, face_a, face_b)
-    got = flipped(table, "row", 2)
-    across_a = swap_across_a(tie(across_a, table))
+    table = merged(table, swap_bits(table, 2, 4), part, down_a)
     across_b = swap_across_b(tie(across_b, table))
     part = piece(3, part, table)
-    table = merged(table, got, part, down_a)
-    table = merged(table, swap_bits(table, 2, 4), down_b)
-    table = merged(table, flipped(table, "col", 1), across_a)
-    table = merged(table, flipped(table, "col", 3), across_b)
+    table = merged(table, flipped(table, "col", 1), part, down_b)
+    part = piece(4, part, table)
+    table = merged(table, flipped(table, "col", 3), part, across_a)
     return part, (face_a, face_b, side, down_a, down_b, across_a, across_b, table)
 
 
@@ -582,19 +624,17 @@
     down_b = swap_down_b(tie(down_b, part))
     part = piece(1, part)
     part = piece(2, part)
+    part = piece(3, part)
     across_a = swap_across_a(tie(across_a, part))
     across_b = swap_across_b(tie(across_b, part))
-    part = piece(3, part, side, down_a, down_b)
+    part = piece(4, part)
+    part = piece(5, part, face_a, face_b)
     return part, (face_a, face_b, side, down_a, down_b, across_a, across_b, table)
 
 
-PIECES = 4
-
-
-def interior(final, y1, y, weights):
+def interior(final, y1, y, weights, stops):
     def piece(n, part, *after):
-        step = PATCH // PIECES
-        kernel = functools.partial(interior_kernel, final, n * step, (n + 1) * step)
+        kernel = functools.partial(interior_kernel, final, stops[n], stops[n + 1])
         args = (*after, y1, y, *weights)
         if n == 0:
             return call(kernel, args, on_chip(*STATE))
@@ -606,27 +646,28 @@
 def local(corr, bonds_down, bonds_across, repulsion):
     faces_out = [on_chip(*s) for s in FACES]
     e_scratch = [pltpu.VMEM((5 * LANES, LANES), F32), pltpu.VMEM((8, COLUMNS), F32)]
-    y, roww, colw, *faces, table = call(
+    y, bonds, colw, *faces, table = call(
         first_kernel,
         (corr, bonds_down, bonds_across, repulsion),
-        [on_chip(*STATE), on_chip(9, SQUARE, LANES), on_chip(17, 8, COLUMNS), *faces_out, on_chip(*TABLE)],
+        [on_chip(*STATE), on_chip(3, LATTICE, LATTICE), on_chip(17, 8, COLUMNS), *faces_out, on_chip(*TABLE)],
         [
             pltpu.VMEM((5 * LANES, LANES), F32),
             pltpu.VMEM((2, SLOT, LANES), F32),
-            pltpu.VMEM((3, LATTICE, LATTICE), F32),
-            pltpu.SemaphoreType.DMA((5,)),
+            pltpu.VMEM((2, TILES, 8, LANES), F32),
+            pltpu.VMEM((TILES, 8, LANES), jnp.int32),
+            pltpu.SemaphoreType.DMA((3 + 8 * CHUNKS,)),
         ],
         loads=True,
     )
-    weights = (roww, colw)
-    part, halos = first_exchange(faces, table, interior(False, y, y, weights))
+    weights = (call(row_weights_kernel, (bonds,), on_chip(9, SQUARE, LANES)), colw)
+    part, halos = first_exchange(faces, table, weights[0], interior(False, y, y, weights, (0, 8, 10, 14, 18, 24)))
     y1, *faces = call(middle_kernel, (part, y, *halos, *weights), [on_chip(*STATE), *faces_out], e_scratch)
-    part, halos = second_exchange(faces, halos[-1], interior(True, y1, y, weights))
+    part, halos = second_exchange(faces, halos[-1], interior(True, y1, y, weights, (0, 4, 8, 12, 16, 20, 24)))
     return call(
         last_kernel,
         (part, y1, *halos, *weights),
         jax.ShapeDtypeStruct(STATE, F32),
-        [*e_scratch, pltpu.VMEM(STATE, F32), pltpu.SemaphoreType.DMA((4,))],
+        [*e_scratch, pltpu.VMEM(STATE, F32), pltpu.SemaphoreType.DMA((10,))],
         out_specs=pl.BlockSpec(memory_space=pl.ANY),
     )
 

time: 87.8 us -> 79.5 us (0.905)
  the two profiles are of different devices: /device:TPU:19 before, /device:TPU:26 now
where the time goes in v2:
time: 79.5 us; the launch traced here: 79.3 us
  starting transfers between devices  36.4 us (46%)
  Pallas kernels  29.4 us (37%)
  waiting for transfers between devices  13 us (16%)
    ppermute x20, starting transfers between devices, traded(): return lax.ppermute(block, axis, pairs(axis, linked))  36.3 us
    pallas_call x32, Pallas kernels, call(): pl.pallas_call(kernel, out_shape=out_shapes, in_specs=[pl.BlockSpec(memor...  29.4 us
    ppermute x20, waiting for transfers between devices, traded(): return lax.ppermute(block, axis, pairs(axis, linked))  8.43 us
    ppermute x1, waiting for transfers between devices, swap_bits(): return lax.ppermute(x, ('row', 'col'), route)  4.54 us
  transfers between devices with their start and end apart: 21, of which 5 were waited for; matrix products, arithmetic and copies ran while one was open for 0% of the time, Pallas kernels for 20%

profile of v2, /device:TPU:26, one launch (start us, length us, event | category | flops | bytes accessed | tf_op | source)
XLA Modules:
  0.0 79.3 jit_solution(16303267849895053197)
XLA Ops:
  0.0 4.4 %shard_map.46 = (f32[2,576,1152]{2,1,0:T(8,128)S(1)}, f32[3,96,96]{2,1,0:T(8,128)S(1)}, f32[17,8,1152]{2,1,0:T(8,128)S(1)}, f32[432,128]{1,0:T(8,128)S(1)}, f32[...) custom-call(f32[2,576,1152]{2,1,0:T(8,128)} %corr.1, ...), custom_call_target="tpu_custom_call" | custom-call | flops 1000 | bytes 1000 | tf_op jit(solution)/shard_map/pallas_call | solution.py:521
  5.0 3.9 %collective-permute-start.3 = (f32[432,128]{1,0:T(8,128)S(1)}, f32[432,128]{1,0:T(8,128)S(1)}, u32[]{:S(2)}, u32[]{:S(2)}) collective-permute-start(f32[432,128]{1,0:T(8,128)S(1)} %get-tuple-element.28), channel_id=1, source_target_pairs={{0,2},{1,3},{4,6},{5,7},{2,0},{3,1},{6,4},{7,5},{8,10},{9,11},{12,... | collective-permute-start | bytes 663560 | tf_op jit(solution)/shard_map/ppermute | solution.py:540
  8.9 3.4 %collective-permute-start.4 = (f32[432,128]{1,0:T(8,128)S(1)}, f32[432,128]{1,0:T(8,128)S(1)}, u32[]{:S(2)}, u32[]{:S(2)}) collective-permute-start(f32[432,128]{1,0:T(8,128)S(1)} %get-tuple-element.29), channel_id=1, source_target_pairs={{2,4},{3,5},{4,2},{5,3},{10,12},{11,13},{12,10},{13,11},{18,20},{1... | collective-permute-start | bytes 663560 | tf_op jit(solution)/shard_map/ppermute | solution.py:540
  12.3 1.4 %shard_map.47.refs_2_.refs_3_.refs_4_.refs_8_.refs_5_ = f32[9,576,128]{2,1,0:T(8,128)S(1)} custom-call(f32[3,96,96]{2,1,0:T(8,128)S(1)} %get-tuple-element.25.bonds), custom_call_target="tpu_custom_call" | custom-call | flops 1000 | bytes 1000 | tf_op jit(solution)/shard_map/pallas_call | solution.py:521
  13.8 1.9 %collective-permute-start.1 = (f32[192,128]{1,0:T(8,128)S(1)}, f32[192,128]{1,0:T(8,128)S(1)}, u32[]{:S(2)}, u32[]{:S(2)}) collective-permute-start(f32[192,128]{1,0:T(8,128)S(1)} %shard_map.48.refs_0_.refs_1_), channel_id=1, source_target_pairs={{0,96},{8,104},{16,112},{24,120},{32,64},{40,72},{48,80},{56,88},{... | collective-permute-start | bytes 294920 | tf_op jit(solution)/shard_map/ppermute | solution.py:540
  15.7 2.4 %shard_map.49.refs_2_.refs_0_ = f32[2,576,1152]{2,1,0:T(8,128)S(1)} custom-call(f32[192,128]{1,0:T(8,128)S(1)} %shard_map.48.refs_0_.refs_1_, f32[2,576,1152]{2,1,0:T(8,128)S(1)} %get-tuple-element.26.refs_1_.refs_2_.refs_3_.y.refs_4_, f32[2,576,1152]{2,1,0:T(8,128)S(1)} %get-tuple-element.26.refs_1_.refs_2_.refs_3_.y.refs_4_, ...), custom_call_target="tpu_custom_call" | custom-call | flops 1000 | bytes 1000 | tf_op jit(solution)/shard_map/pallas_call | solution.py:521
  18.6 2.0 %collective-permute-start.6 = (f32[288,128]{1,0:T(8,128)S(1)}, f32[288,128]{1,0:T(8,128)S(1)}, u32[]{:S(2)}, u32[]{:S(2)}) collective-permute-start(f32[288,128]{1,0:T(8,128)S(1)} %shard_map.53), channel_id=1, source_target_pairs={{0,1},{2,3},{4,5},{6,7},{1,0},{3,2},{5,4},{7,6},{8,9},{10,11},{12,... | collective-permute-start | bytes 442376 | tf_op jit(solution)/shard_map/ppermute | solution.py:540
  20.6 2.2 %collective-permute-start.8 = (f32[2,24,1152]{2,1,0:T(8,128)S(1)}, f32[2,24,1152]{2,1,0:T(8,128)S(1)}, u32[]{:S(2)}, u32[]{:S(2)}) collective-permute-start(f32[2,24,1152]{2,1,0:T(8,128)S(1)} %shard_map.56), channel_id=1, source_target_pairs={{0,32},{8,40},{16,48},{24,56},{64,96},{72,104},{80,112},{88,120},{... | collective-permute-start | bytes 663560 | tf_op jit(solution)/shard_map/ppermute | solution.py:540
  23.6 4.5 %collective-permute-start.10 = (f32[2,24,1152]{2,1,0:T(8,128)S(1)}, f32[2,24,1152]{2,1,0:T(8,128)S(1)}, u32[]{:S(2)}, u32[]{:S(2)}) collective-permute-start(f32[2,24,1152]{2,1,0:T(8,128)S(1)} %shard_map.59), channel_id=1, source_target_pairs={{32,64},{40,72},{48,80},{56,88},{64,32},{72,40},{80,48},{88,56},{3... | collective-permute-start | bytes 663560 | tf_op jit(solution)/shard_map/ppermute | solution.py:540
  29.5 4.5 %collective-permute-done.7.refs_1_ = f32[192,128]{1,0:T(8,128)S(1)} collective-permute-done((f32[192,128]{1,0:T(8,128)S(1)}, f32[192,128]{1,0:T(8,128)S(1)}, u32[]{:S(2)}, u32[]{:S(2)}) %collective-permute-start.7) | collective-permute-done | bytes 98336 | tf_op jit(solution)/shard_map/ppermute | solution.py:592
  34.1 1.9 %collective-permute-start.12 = (f32[2,24,1152]{2,1,0:T(8,128)S(1)}, f32[2,24,1152]{2,1,0:T(8,128)S(1)}, u32[]{:S(2)}, u32[]{:S(2)}) collective-permute-start(f32[2,24,1152]{2,1,0:T(8,128)S(1)} %shard_map.63), channel_id=1, source_target_pairs={{8,16},{40,48},{72,80},{104,112},{16,8},{48,40},{80,72},{112,104},... | collective-permute-start | bytes 663560 | tf_op jit(solution)/shard_map/ppermute | solution.py:540
  38.3 2.4 %collective-permute-done.9.refs_1_ = f32[192,128]{1,0:T(8,128)S(1)} collective-permute-done((f32[192,128]{1,0:T(8,128)S(1)}, f32[192,128]{1,0:T(8,128)S(1)}, u32[]{:S(2)}, u32[]{:S(2)}) %collective-permute-start.9) | collective-permute-done | bytes 98336 | tf_op jit(solution)/shard_map/ppermute | solution.py:540
  41.9 1.8 %shard_map.61.refs_2_.base = f32[2,576,1152]{2,1,0:T(8,128)S(1)} custom-call(f32[2,576,1152]{2,1,0:T(8,128)S(1)} %shard_map.58.refs_2_.refs_0_, f32[192,128]{1,0:T(8,128)S(1)} %shard_map.60.refs_1_.refs_0_, f32[2,576,1152]{2,1,0:T(8,128)S(1)} %get-tuple-element.26.refs_1_.refs_2_.refs_3_.y.refs_4_, ...), custom_call_target="tpu_custom_call", output_to_operand_aliasing={{}: (0, {})} | custom-call | flops 1000 | bytes 1000 | tf_op jit(solution)/shard_map/pallas_call | solution.py:521
  43.7 3.1 %collective-permute-done.13.refs_1_ = f32[192,128]{1,0:T(8,128)S(1)} collective-permute-done((f32[192,128]{1,0:T(8,128)S(1)}, f32[192,128]{1,0:T(8,128)S(1)}, u32[]{:S(2)}, u32[]{:S(2)}) %collective-permute-start.13) | collective-permute-done | bytes 98336 | tf_op jit(solution)/shard_map/ppermute | solution.py:540
  46.9 4.8 %shard_map.65 = (f32[2,576,1152]{2,1,0:T(8,128)S(1)}, f32[432,128]{1,0:T(8,128)S(1)}, f32[432,128]{1,0:T(8,128)S(1)}, f32[288,128]{1,0:T(8,128)S(1)}, f32[2,24,1...) custom-call(f32[2,576,1152]{2,1,0:T(8,128)S(1)} %shard_map.61.refs_2_.ba, ...), custom_call_target="tpu_custom_call" | custom-call | flops 1000 | bytes 1000 | tf_op jit(solution)/shard_map/pallas_call | solution.py:521
  52.4 4.6 %collective-permute-start.15 = (f32[432,128]{1,0:T(8,128)S(1)}, f32[432,128]{1,0:T(8,128)S(1)}, u32[]{:S(2)}, u32[]{:S(2)}) collective-permute-start(f32[432,128]{1,0:T(8,128)S(1)} %get-tuple-element.37), channel_id=1, source_target_pairs={{2,4},{3,5},{4,2},{5,3},{10,12},{11,13},{12,10},{13,11},{18,20},{1... | collective-permute-start | bytes 663560 | tf_op jit(solution)/shard_map/ppermute | solution.py:540
  58.3 1.2 %shard_map.67.refs_0_ = f32[2,576,1152]{2,1,0:T(8,128)S(1)} custom-call(f32[2,576,1152]{2,1,0:T(8,128)S(1)} %shard_map.66.refs_0_.refs_1_, f32[2,576,1152]{2,1,0:T(8,128)S(1)} %get-tuple-element.35.refs_0_.refs_1_.refs_3_.y1, f32[2,576,1152]{2,1,0:T(8,128)S(1)} %get-tuple-element.26.refs_1_.refs_2_.refs_3_.y.refs_4_, ...), custom_call_target="tpu_custom_call", output_to_operand_aliasing={{}: (0, {})} | custom-call | flops 1000 | bytes 1000 | tf_op jit(solution)/shard_map/pallas_call | solution.py:521
  59.5 1.2 %shard_map.68.refs_0_ = f32[2,576,1152]{2,1,0:T(8,128)S(1)} custom-call(f32[2,576,1152]{2,1,0:T(8,128)S(1)} %shard_map.67.refs_0_, f32[2,576,1152]{2,1,0:T(8,128)S(1)} %get-tuple-element.35.refs_0_.refs_1_.refs_3_.y1, f32[2,576,1152]{2,1,0:T(8,128)S(1)} %get-tuple-element.26.refs_1_.refs_2_.refs_3_.y.refs_4_, ...), custom_call_target="tpu_custom_call", output_to_operand_aliasing={{}: (0, {})} | custom-call | flops 1000 | bytes 1000 | tf_op jit(solution)/shard_map/pallas_call | solution.py:521
  61.2 1.2 %shard_map.69.refs_0_.refs_1_ = f32[2,576,1152]{2,1,0:T(8,128)S(1)} custom-call(f32[2,576,1152]{2,1,0:T(8,128)S(1)} %shard_map.68.refs_0_, f32[2,576,1152]{2,1,0:T(8,128)S(1)} %get-tuple-element.35.refs_0_.refs_1_.refs_3_.y1, f32[2,576,1152]{2,1,0:T(8,128)S(1)} %get-tuple-element.26.refs_1_.refs_2_.refs_3_.y.refs_4_, ...), custom_call_target="tpu_custom_call", output_to_operand_aliasing={{}: (0, {})} | custom-call | flops 1000 | bytes 1000 | tf_op jit(solution)/shard_map/pallas_call | solution.py:521
  62.5 3.2 %collective-permute-start.20 = (f32[2,24,1152]{2,1,0:T(8,128)S(1)}, f32[2,24,1152]{2,1,0:T(8,128)S(1)}, u32[]{:S(2)}, u32[]{:S(2)}) collective-permute-start(f32[2,24,1152]{2,1,0:T(8,128)S(1)} %shard_map.76), channel_id=1, source_target_pairs={{8,16},{40,48},{72,80},{104,112},{16,8},{48,40},{80,72},{112,104},... | collective-permute-start | bytes 663560 | tf_op jit(solution)/shard_map/ppermute | solution.py:540
  65.8 3.8 %collective-permute-start.18 = (f32[2,24,1152]{2,1,0:T(8,128)S(1)}, f32[2,24,1152]{2,1,0:T(8,128)S(1)}, u32[]{:S(2)}, u32[]{:S(2)}) collective-permute-start(f32[2,24,1152]{2,1,0:T(8,128)S(1)} %shard_map.74), channel_id=1, source_target_pairs={{32,64},{40,72},{48,80},{56,88},{64,32},{72,40},{80,48},{88,56},{3... | collective-permute-start | bytes 663560 | tf_op jit(solution)/shard_map/ppermute | solution.py:540
  70.0 1.2 %shard_map.70.refs_0_ = f32[2,576,1152]{2,1,0:T(8,128)S(1)} custom-call(f32[2,576,1152]{2,1,0:T(8,128)S(1)} %shard_map.69.refs_0_.refs_1_, f32[2,576,1152]{2,1,0:T(8,128)S(1)} %get-tuple-element.35.refs_0_.refs_1_.refs_3_.y1, f32[2,576,1152]{2,1,0:T(8,128)S(1)} %get-tuple-element.26.refs_1_.refs_2_.refs_3_.y.refs_4_, ...), custom_call_target="tpu_custom_call", output_to_operand_aliasing={{}: (0, {})} | custom-call | flops 1000 | bytes 1000 | tf_op jit(solution)/shard_map/pallas_call | solution.py:521
  72.3 2.5 %collective-permute-done.16.refs_2_ = f32[288,128]{1,0:T(8,128)S(1)} collective-permute-done((f32[288,128]{1,0:T(8,128)S(1)}, f32[288,128]{1,0:T(8,128)S(1)}, u32[]{:S(2)}, u32[]{:S(2)}) %collective-permute-start.16) | collective-permute-done | bytes 147488 | tf_op jit(solution)/shard_map/ppermute | solution.py:540
  74.8 4.3 %shard_map.77 = f32[2,576,1152]{2,1,0:T(8,128)} custom-call(f32[2,576,1152]{2,1,0:T(8,128)S(1)} %shard_map.71.base, f32[2,576,1152]{2,1,0:T(8,128)S(1)} %get-tuple-element.35.refs_0_.refs_1_.refs_3_.y1, f32[432,128]{1,0:T(8,128)S(1)} %collective-permute-done.14.refs_1_.refs_0_, f32[432,128]{1,0:T(8,128)S(1)} %collective-permute-done.15.refs_2_.refs_1_, ...), custom_call_target="tpu_custom_call" | custom-call | flops 1000 | bytes 1000 | tf_op jit(solution)/shard_map/pallas_call | solution.py:521
  (50 shorter events, 10.9 us)
Async XLA Ops:
  4.4 9.4 %collective-permute-start = (f32[192,128]{1,0:T(8,128)S(1)}, f32[192,128]{1,0:T(8,128)S(1)}, u32[]{:S(2)}, u32[]{:S(2)}) collective-permute-start(f32[192,128]{1,0:T(8,128)S(1)} %get-tuple-element.24.refs_0_), channel_id=1, source_target_pairs={{0,32},{8,40},{16,48},{24,56},{64,96},{72,104},{80,112},{88,120},{... | collective-permute-start | bytes 294920 | tf_op jit(solution)/shard_map/ppermute | solution.py:540
  5.0 17.9 %collective-permute-start.3 = (f32[432,128]{1,0:T(8,128)S(1)}, f32[432,128]{1,0:T(8,128)S(1)}, u32[]{:S(2)}, u32[]{:S(2)}) collective-permute-start(f32[432,128]{1,0:T(8,128)S(1)} %get-tuple-element.28), channel_id=1, source_target_pairs={{0,2},{1,3},{4,6},{5,7},{2,0},{3,1},{6,4},{7,5},{8,10},{9,11},{12,... | collective-permute-start | bytes 663560 | tf_op jit(solution)/shard_map/ppermute | solution.py:540
  8.9 14.0 %collective-permute-start.4 = (f32[432,128]{1,0:T(8,128)S(1)}, f32[432,128]{1,0:T(8,128)S(1)}, u32[]{:S(2)}, u32[]{:S(2)}) collective-permute-start(f32[432,128]{1,0:T(8,128)S(1)} %get-tuple-element.29), channel_id=1, source_target_pairs={{2,4},{3,5},{4,2},{5,3},{10,12},{11,13},{12,10},{13,11},{18,20},{1... | collective-permute-start | bytes 663560 | tf_op jit(solution)/shard_map/ppermute | solution.py:540
  13.8 4.7 %collective-permute-start.1 = (f32[192,128]{1,0:T(8,128)S(1)}, f32[192,128]{1,0:T(8,128)S(1)}, u32[]{:S(2)}, u32[]{:S(2)}) collective-permute-start(f32[192,128]{1,0:T(8,128)S(1)} %shard_map.48.refs_0_.refs_1_), channel_id=1, source_target_pairs={{0,96},{8,104},{16,112},{24,120},{32,64},{40,72},{48,80},{56,88},{... | collective-permute-start | bytes 294920 | tf_op jit(solution)/shard_map/ppermute | solution.py:540
  18.5 4.4 %collective-permute-start.2 = (f32[192,128]{1,0:T(8,128)S(1)}, f32[192,128]{1,0:T(8,128)S(1)}, u32[]{:S(2)}, u32[]{:S(2)}) collective-permute-start(f32[192,128]{1,0:T(8,128)S(1)} %shard_map.50.refs_0_.refs_1_), channel_id=1, source_target_pairs={{0,8},{16,24},{32,40},{48,56},{64,72},{80,88},{96,104},{112,120},{... | collective-permute-start | bytes 294920 | tf_op jit(solution)/shard_map/ppermute | solution.py:540
  18.6 9.5 %collective-permute-start.6 = (f32[288,128]{1,0:T(8,128)S(1)}, f32[288,128]{1,0:T(8,128)S(1)}, u32[]{:S(2)}, u32[]{:S(2)}) collective-permute-start(f32[288,128]{1,0:T(8,128)S(1)} %shard_map.53), channel_id=1, source_target_pairs={{0,1},{2,3},{4,5},{6,7},{1,0},{3,2},{5,4},{7,6},{8,9},{10,11},{12,... | collective-permute-start | bytes 442376 | tf_op jit(solution)/shard_map/ppermute | solution.py:540
  20.6 8.9 %collective-permute-start.8 = (f32[2,24,1152]{2,1,0:T(8,128)S(1)}, f32[2,24,1152]{2,1,0:T(8,128)S(1)}, u32[]{:S(2)}, u32[]{:S(2)}) collective-permute-start(f32[2,24,1152]{2,1,0:T(8,128)S(1)} %shard_map.56), channel_id=1, source_target_pairs={{0,32},{8,40},{16,48},{24,56},{64,96},{72,104},{80,112},{88,120},{... | collective-permute-start | bytes 663560 | tf_op jit(solution)/shard_map/ppermute | solution.py:540
  22.9 5.2 %collective-permute-start.5 = (f32[192,128]{1,0:T(8,128)S(1)}, f32[192,128]{1,0:T(8,128)S(1)}, u32[]{:S(2)}, u32[]{:S(2)}) collective-permute-start(f32[192,128]{1,0:T(8,128)S(1)} %shard_map.51.refs_1_.refs_0_), channel_id=1, source_target_pairs={{0,16},{8,24},{32,48},{40,56},{64,80},{72,88},{96,112},{104,120},{... | collective-permute-start | bytes 294920 | tf_op jit(solution)/shard_map/ppermute | solution.py:540
  23.6 14.7 %collective-permute-start.10 = (f32[2,24,1152]{2,1,0:T(8,128)S(1)}, f32[2,24,1152]{2,1,0:T(8,128)S(1)}, u32[]{:S(2)}, u32[]{:S(2)}) collective-permute-start(f32[2,24,1152]{2,1,0:T(8,128)S(1)} %shard_map.59), channel_id=1, source_target_pairs={{32,64},{40,72},{48,80},{56,88},{64,32},{72,40},{80,48},{88,56},{3... | collective-permute-start | bytes 663560 | tf_op jit(solution)/shard_map/ppermute | solution.py:540
  28.2 5.9 %collective-permute-start.7 = (f32[192,128]{1,0:T(8,128)S(1)}, f32[192,128]{1,0:T(8,128)S(1)}, u32[]{:S(2)}, u32[]{:S(2)}) collective-permute-start(f32[192,128]{1,0:T(8,128)S(1)} %shard_map.54.refs_1_.refs_0_), channel_id=1, source_target_pairs={{0,20},{1,21},{2,22},{3,23},{4,16},{5,17},{6,18},{7,19},{8,28},{9,... | collective-permute-start | bytes 294920 | tf_op jit(solution)/shard_map/ppermute | solution.py:592
  29.4 14.3 %collective-permute-start.11 = (f32[2,24,1152]{2,1,0:T(8,128)S(1)}, f32[2,24,1152]{2,1,0:T(8,128)S(1)}, u32[]{:S(2)}, u32[]{:S(2)}) collective-permute-start(f32[2,24,1152]{2,1,0:T(8,128)S(1)} %shard_map.62), channel_id=1, source_target_pairs={{0,8},{16,24},{32,40},{48,56},{64,72},{80,88},{96,104},{112,120},{... | collective-permute-start | bytes 663560 | tf_op jit(solution)/shard_map/ppermute | solution.py:540
  34.1 12.7 %collective-permute-start.12 = (f32[2,24,1152]{2,1,0:T(8,128)S(1)}, f32[2,24,1152]{2,1,0:T(8,128)S(1)}, u32[]{:S(2)}, u32[]{:S(2)}) collective-permute-start(f32[2,24,1152]{2,1,0:T(8,128)S(1)} %shard_map.63), channel_id=1, source_target_pairs={{8,16},{40,48},{72,80},{104,112},{16,8},{48,40},{80,72},{112,104},... | collective-permute-start | bytes 663560 | tf_op jit(solution)/shard_map/ppermute | solution.py:540
  36.0 4.7 %collective-permute-start.9 = (f32[192,128]{1,0:T(8,128)S(1)}, f32[192,128]{1,0:T(8,128)S(1)}, u32[]{:S(2)}, u32[]{:S(2)}) collective-permute-start(f32[192,128]{1,0:T(8,128)S(1)} %shard_map.57.refs_1_.refs_0_), channel_id=1, source_target_pairs={{0,1},{2,3},{4,5},{6,7},{1,0},{3,2},{5,4},{7,6},{8,9},{10,11},{12,... | collective-permute-start | bytes 294920 | tf_op jit(solution)/shard_map/ppermute | solution.py:540
  40.8 6.1 %collective-permute-start.13 = (f32[192,128]{1,0:T(8,128)S(1)}, f32[192,128]{1,0:T(8,128)S(1)}, u32[]{:S(2)}, u32[]{:S(2)}) collective-permute-start(f32[192,128]{1,0:T(8,128)S(1)} %shard_map.60.refs_1_.refs_0_), channel_id=1, source_target_pairs={{0,3},{1,2},{4,7},{5,6},{3,0},{2,1},{7,4},{6,5},{8,11},{9,10},{12,... | collective-permute-start | bytes 294920 | tf_op jit(solution)/shard_map/ppermute | solution.py:540
  51.7 14.1 %collective-permute-start.14 = (f32[432,128]{1,0:T(8,128)S(1)}, f32[432,128]{1,0:T(8,128)S(1)}, u32[]{:S(2)}, u32[]{:S(2)}) collective-permute-start(f32[432,128]{1,0:T(8,128)S(1)} %get-tuple-element.36), channel_id=1, source_target_pairs={{0,2},{1,3},{4,6},{5,7},{2,0},{3,1},{6,4},{7,5},{8,10},{9,11},{12,... | collective-permute-start | bytes 663560 | tf_op jit(solution)/shard_map/ppermute | solution.py:540
  52.4 17.1 %collective-permute-start.15 = (f32[432,128]{1,0:T(8,128)S(1)}, f32[432,128]{1,0:T(8,128)S(1)}, u32[]{:S(2)}, u32[]{:S(2)}) collective-permute-start(f32[432,128]{1,0:T(8,128)S(1)} %get-tuple-element.37), channel_id=1, source_target_pairs={{2,4},{3,5},{4,2},{5,3},{10,12},{11,13},{12,10},{13,11},{18,20},{1... | collective-permute-start | bytes 663560 | tf_op jit(solution)/shard_map/ppermute | solution.py:540
  60.7 14.1 %collective-permute-start.17 = (f32[2,24,1152]{2,1,0:T(8,128)S(1)}, f32[2,24,1152]{2,1,0:T(8,128)S(1)}, u32[]{:S(2)}, u32[]{:S(2)}) collective-permute-start(f32[2,24,1152]{2,1,0:T(8,128)S(1)} %shard_map.73), channel_id=1, source_target_pairs={{0,32},{8,40},{16,48},{24,56},{64,96},{72,104},{80,112},{88,120},{... | collective-permute-start | bytes 663560 | tf_op jit(solution)/shard_map/ppermute | solution.py:540
  62.4 12.4 %collective-permute-start.19 = (f32[2,24,1152]{2,1,0:T(8,128)S(1)}, f32[2,24,1152]{2,1,0:T(8,128)S(1)}, u32[]{:S(2)}, u32[]{:S(2)}) collective-permute-start(f32[2,24,1152]{2,1,0:T(8,128)S(1)} %shard_map.75), channel_id=1, source_target_pairs={{0,8},{16,24},{32,40},{48,56},{64,72},{80,88},{96,104},{112,120},{... | collective-permute-start | bytes 663560 | tf_op jit(solution)/shard_map/ppermute | solution.py:540
  62.5 12.3 %collective-permute-start.20 = (f32[2,24,1152]{2,1,0:T(8,128)S(1)}, f32[2,24,1152]{2,1,0:T(8,128)S(1)}, u32[]{:S(2)}, u32[]{:S(2)}) collective-permute-start(f32[2,24,1152]{2,1,0:T(8,128)S(1)} %shard_map.76), channel_id=1, source_target_pairs={{8,16},{40,48},{72,80},{104,112},{16,8},{48,40},{80,72},{112,104},... | collective-permute-start | bytes 663560 | tf_op jit(solution)/shard_map/ppermute | solution.py:540
  65.8 9.0 %collective-permute-start.18 = (f32[2,24,1152]{2,1,0:T(8,128)S(1)}, f32[2,24,1152]{2,1,0:T(8,128)S(1)}, u32[]{:S(2)}, u32[]{:S(2)}) collective-permute-start(f32[2,24,1152]{2,1,0:T(8,128)S(1)} %shard_map.74), channel_id=1, source_target_pairs={{32,64},{40,72},{48,80},{56,88},{64,32},{72,40},{80,48},{88,56},{3... | collective-permute-start | bytes 663560 | tf_op jit(solution)/shard_map/ppermute | solution.py:540
  69.6 5.2 %collective-permute-start.16 = (f32[288,128]{1,0:T(8,128)S(1)}, f32[288,128]{1,0:T(8,128)S(1)}, u32[]{:S(2)}, u32[]{:S(2)}) collective-permute-start(f32[288,128]{1,0:T(8,128)S(1)} %shard_map.72), channel_id=1, source_target_pairs={{0,1},{2,3},{4,5},{6,7},{1,0},{3,2},{5,4},{7,6},{8,9},{10,11},{12,... | collective-permute-start | bytes 442376 | tf_op jit(solution)/shard_map/ppermute | solution.py:540

commit v3 on v2

--- a/solution.py
+++ b/solution.py
@@ -223,18 +223,17 @@
 SLOT = 24
 
 
-def pack_densities(src, colw, table, row_sums, slots, sums, codes):
+def pack_densities(src, colw, slots, row_sums, sums, codes):
     row_id, col_id = place()
     odd = lax.rem(row_id, 2)
     across = lax.rem(row_id, 4) - 2 * lax.rem(col_id, 2)
     along = row_id // 4 - col_id // 2
     beside = jnp.logical_and(along == 0, jnp.logical_and(across >= -1, across <= 2))
     over = jnp.logical_and(jnp.abs(along) == 1, jnp.logical_and(across >= 0, across <= 1))
-    table[...] = jnp.zeros(table.shape, F32)
+    slots[...] = jnp.zeros(slots.shape, F32)
 
     @pl.when(jnp.logical_or(beside, over))
     def _():
-        slots[...] = jnp.zeros(slots.shape, F32)
         row_sums[...] = jnp.zeros(row_sums.shape, F32)
         sums[...] = jnp.zeros(sums.shape, F32)
         lane = iota((8, LANES), 1)
@@ -284,13 +283,11 @@
             share(jnp.where(along == 1, 0, PATCH - 1), [start, start + 4])
 
         for t in range(TILES):
-            slots[0, t : t + 1, :] = jnp.sum(sums[0, t], axis=0, keepdims=True)
-            slots[0, TILES + t : TILES + t + 1, :] = jnp.sum(sums[1, t], axis=0, keepdims=True)
+            slots[t : t + 1, :] = jnp.sum(sums[0, t], axis=0, keepdims=True)
+            slots[TILES + t : TILES + t + 1, :] = jnp.sum(sums[1, t], axis=0, keepdims=True)
         for t in range(5):
             got = jnp.sum(row_sums[t * LANES : (t + 1) * LANES, :].T, axis=0, keepdims=True)
-            slots[1, pl.ds(TILES + 4 * odd + t, 1), :] = got
-        table[pl.ds(pl.multiple_of(SLOT * col_id, 8), SLOT), :] = slots[0]
-        table[pl.ds(pl.multiple_of(SLOT * (row_id // 2), 8), SLOT), :] += slots[1]
+            slots[pl.ds(SLOT + TILES + 4 * odd + t, 1), :] = got
 
 
 CHUNKS = 3
@@ -409,8 +406,7 @@
     row_odd = lax.rem(row_id, 2)
     shift = jnp.where(even, 87, 41)
     lane = iota((8, LANES), 1)
-    row_slot = table[pl.ds(pl.multiple_of(SLOT * (row_id // 2), 8), SLOT), :]
-    col_slot = table[pl.ds(pl.multiple_of(SLOT * col_id, 8), SLOT), :]
+    col_slot, row_slot = table[0:SLOT, :], table[SLOT : 2 * SLOT, :]
     for t in range(5):
         u = stage * TILES + t
         strip = jnp.where(row_odd == 1, row_slot[4 + u : 5 + u, :], row_slot[u : u + 1, :])
@@ -513,7 +509,6 @@
 VM = pl.BlockSpec(memory_space=pltpu.VMEM)
 STATE = (2, SQUARE, COLUMNS)
 FACES = ((3 * QUARTER, LANES),) * 2 + ((SQUARE // 2, LANES),) + ((2, PATCH, COLUMNS),) * 4
-TABLE = (8 * SLOT, LANES)
 
 
 def call(kernel, args, out_shapes, scratch=(), out_specs=None, aliases=None, loads=False):
@@ -551,19 +546,92 @@
     return call(kernel, (value, *after), on_chip(*value.shape))
 
 
-def merged(value, got, *after):
-    def kernel(*refs):
-        refs[-1][...] = refs[0][...] + refs[1][...]
-
-    return call(kernel, (value, got, *after), on_chip(*value.shape))
+def rows_of(*slots):
+    return on_chip(sum(slots) * SLOT, LANES)
+
+
+def slot(n):
+    return pl.ds(pl.multiple_of(SLOT * n, 8), SLOT)
+
+
+def grow(known, got, *after):
+    rows = known.shape[0]
+
+    def kernel(known, got, *refs):
+        out = refs[-1]
+        out[0:SLOT, :] = known[0:SLOT, :] + got[0:SLOT, :]
+        out[SLOT:rows, :] = known[SLOT:rows, :]
+        out[rows : 2 * rows - SLOT, :] = got[SLOT:rows, :]
+
+    return call(kernel, (known, got, *after), on_chip(2 * rows - SLOT, LANES))
+
+
+def added(known, got, *after):
+    def kernel(known, got, *refs):
+        refs[-1][...] = known[...] + got[...]
+
+    return call(kernel, (known, got, *after), on_chip(*known.shape))
+
+
+def halve_all(known, got, *after):
+    def kernel(known, got, *refs):
+        keep, send, table = refs[-3:]
+        row_id, col_id = place()
+        mine = row_id // 2
+        for n, bits in enumerate((0, 2, 6, 4)):
+            rows = slice(SLOT * (n + 1), SLOT * (n + 2))
+            table[slot(mine ^ bits), :] = known[rows, :]
+            table[slot(mine ^ 1 ^ bits), :] = got[rows, :]
+        table[slot(col_id), :] += known[0:SLOT, :] + got[0:SLOT, :]
+        half = col_id // 4
+        for n in range(4):
+            keep[SLOT * n : SLOT * (n + 1), :] = table[slot(4 * half + n), :]
+            send[SLOT * n : SLOT * (n + 1), :] = table[slot(4 * (1 - half) + n), :]
+        keep[4 * SLOT :, :] = table[slot(mine), :]
+        send[4 * SLOT :, :] = table[slot(mine ^ 1), :]
+
+    scratch = [pltpu.VMEM((8 * SLOT, LANES), F32)]
+    return call(kernel, (known, got, *after), [rows_of(5), rows_of(5)], scratch)
+
+
+def halve_four(known, got, *after):
+    def kernel(known, got, *refs):
+        keep, send, total = refs[-3:]
+        z = lax.rem(place()[1], 4)
+        total[...] = known[...] + got[...]
+        for out, bits in ((keep, (0, 3)), (send, (1, 2))):
+            for n in range(2):
+                out[SLOT * n : SLOT * (n + 1), :] = total[slot(z ^ bits[n]), :]
+            out[2 * SLOT :, :] = total[4 * SLOT :, :]
+
+    return call(kernel, (known, got, *after), [rows_of(3), rows_of(3)], [pltpu.VMEM((5 * SLOT, LANES), F32)])
+
+
+def halve_two(known, got, *after):
+    def kernel(known, got, *refs):
+        keep, send = refs[-2:]
+        total = known[...] + got[...]
+        keep[0:SLOT, :] = total[0:SLOT]
+        send[0:SLOT, :] = total[SLOT : 2 * SLOT]
+        keep[SLOT:, :] = total[2 * SLOT :]
+        send[SLOT:, :] = total[2 * SLOT :]
+
+    return call(kernel, (known, got, *after), [rows_of(2), rows_of(2)])
 
 
 def swap_face_a(x):
     return flipped(x, "col", 2)
 
 
+def swapped(x, partner):
+    rows, cols = lax.axis_size("row"), lax.axis_size("col")
+    places = [(r, c) for r in range(rows) for c in range(cols)]
+    route = [(r * cols + c, partner(r, c)[0] * cols + partner(r, c)[1]) for r, c in places]
+    return lax.ppermute(x, ("row", "col"), route)
+
+
 def swap_face_b(x):
-    return traded(x, "col", lambda i, j: j == i + 2 and (i // 2) % 2 == 1)
+    return swapped(x, lambda r, c: (r, c ^ 6) if c // 2 in (1, 2) else (r ^ 1, c))
 
 
 def swap_side(x):
@@ -575,7 +643,7 @@
 
 
 def swap_down_b(x):
-    return traded(x, "row", lambda i, j: j == i + 4 and (i // 4) % 2 == 1)
+    return flipped(x, "row", 12)
 
 
 def swap_across_a(x):
@@ -583,52 +651,51 @@
 
 
 def swap_across_b(x):
-    return traded(x, "row", lambda i, j: j == i + 1 and i % 4 == 1)
+    return swapped(x, lambda r, c: (r ^ 3, c) if r % 4 in (1, 2) else (r ^ 4, c))
 
 
 def swap_bits(x, row_bits, col_bits):
-    rows, cols = lax.axis_size("row"), lax.axis_size("col")
-    route = [(r * cols + c, (r ^ row_bits) * cols + (c ^ col_bits)) for r in range(rows) for c in range(cols)]
-    return lax.ppermute(x, ("row", "col"), route)
-
-
-def first_exchange(faces, table, first_work, piece):
+    return swapped(x, lambda r, c: (r ^ row_bits, c ^ col_bits))
+
+
+def first_exchange(faces, share, first_work, piece):
     face_a, face_b, side, down_a, down_b, across_a, across_b = faces
-    face_a, face_b = swap_face_a(face_a), swap_face_b(face_b)
-    table = merged(table, flipped(table, "row", 4), first_work)
-    side = swap_side(tie(side, table))
-    part = piece(0, None, table)
-    table = merged(table, flipped(table, "row", 12), part)
-    down_a = swap_down_a(tie(down_a, table))
-    table = merged(table, flipped(table, "row", 1), face_a, face_b)
-    down_b = swap_down_b(tie(down_b, table))
-    part = piece(1, part, table)
-    table = merged(table, flipped(table, "row", 2), part, side)
-    across_a = swap_across_a(tie(across_a, table))
-    part = piece(2, part, table)
-    table = merged(table, swap_bits(table, 2, 4), part, down_a)
-    across_b = swap_across_b(tie(across_b, table))
-    part = piece(3, part, table)
-    table = merged(table, flipped(table, "col", 1), part, down_b)
-    part = piece(4, part, table)
-    table = merged(table, flipped(table, "col", 3), part, across_a)
+    side = swap_side(side)
+    face_b = swap_face_b(face_b)
+    face_a = swap_face_a(face_a)
+    known = grow(share, flipped(share, "row", 4), first_work)
+    part = piece(0, None, known)
+    known = grow(known, flipped(known, "row", 12), part)
+    down_a = swap_down_a(tie(down_a, known))
+    known = added(known, flipped(known, "row", 1), side)
+    down_b = swap_down_b(tie(down_b, known))
+    known, send = halve_all(known, flipped(known, "row", 2), face_a, face_b)
+    across_b = swap_across_b(tie(across_b, known))
+    part = piece(1, part, known)
+    known, send = halve_four(known, swap_bits(send, 2, 4), part, down_a, down_b)
+    across_a = swap_across_a(tie(across_a, known))
+    part = piece(2, part, known)
+    known, send = halve_two(known, flipped(send, "col", 1), part, across_b)
+    part = piece(3, part, known)
+    table = added(known, flipped(send, "col", 3), part, across_a)
     return part, (face_a, face_b, side, down_a, down_b, across_a, across_b, table)
 
 
 def second_exchange(faces, table, piece):
     face_a, face_b, side, down_a, down_b, across_a, across_b = faces
-    face_a, face_b = swap_face_a(face_a), swap_face_b(face_b)
+    face_b = swap_face_b(face_b)
+    face_a = swap_face_a(face_a)
+    across_a = swap_across_a(across_a)
+    across_b = swap_across_b(across_b)
+    side = swap_side(side)
     part = piece(0, None)
-    side = swap_side(tie(side, part))
     down_a = swap_down_a(tie(down_a, part))
+    part = piece(1, part, across_a)
     down_b = swap_down_b(tie(down_b, part))
-    part = piece(1, part)
-    part = piece(2, part)
+    part = piece(2, part, side)
     part = piece(3, part)
-    across_a = swap_across_a(tie(across_a, part))
-    across_b = swap_across_b(tie(across_b, part))
     part = piece(4, part)
-    part = piece(5, part, face_a, face_b)
+    part = piece(5, part)
     return part, (face_a, face_b, side, down_a, down_b, across_a, across_b, table)
 
 
@@ -646,13 +713,12 @@
 def local(corr, bonds_down, bonds_across, repulsion):
     faces_out = [on_chip(*s) for s in FACES]
     e_scratch = [pltpu.VMEM((5 * LANES, LANES), F32), pltpu.VMEM((8, COLUMNS), F32)]
-    y, bonds, colw, *faces, table = call(
+    y, bonds, colw, *faces, share = call(
         first_kernel,
         (corr, bonds_down, bonds_across, repulsion),
-        [on_chip(*STATE), on_chip(3, LATTICE, LATTICE), on_chip(17, 8, COLUMNS), *faces_out, on_chip(*TABLE)],
+        [on_chip(*STATE), on_chip(3, LATTICE, LATTICE), on_chip(17, 8, COLUMNS), *faces_out, on_chip(2 * SLOT, LANES)],
         [
             pltpu.VMEM((5 * LANES, LANES), F32),
-            pltpu.VMEM((2, SLOT, LANES), F32),
             pltpu.VMEM((2, TILES, 8, LANES), F32),
             pltpu.VMEM((TILES, 8, LANES), jnp.int32),
             pltpu.SemaphoreType.DMA((3 + 8 * CHUNKS,)),
@@ -660,7 +726,7 @@
         loads=True,
     )
     weights = (call(row_weights_kernel, (bonds,), on_chip(9, SQUARE, LANES)), colw)
-    part, halos = first_exchange(faces, table, weights[0], interior(False, y, y, weights, (0, 8, 10, 14, 18, 24)))
+    part, halos = first_exchange(faces, share, weights[0], interior(False, y, y, weights, (0, 8, 12, 18, 24)))
     y1, *faces = call(middle_kernel, (part, y, *halos, *weights), [on_chip(*STATE), *faces_out], e_scratch)
     part, halos = second_exchange(faces, halos[-1], interior(True, y1, y, weights, (0, 4, 8, 12, 16, 20, 24)))
     return call(

time: 79.5 us -> 69.9 us (0.88)
  the two profiles are of different devices: /device:TPU:26 before, /device:TPU:0 now
where the time goes in v3:
time: 69.9 us; the launch traced here: 69.8 us
  starting transfers between devices  31.9 us (46%)
  Pallas kernels  30.7 us (44%)
  waiting for transfers between devices  6.76 us (10%)
    pallas_call x27, Pallas kernels, call(): pl.pallas_call(kernel, out_shape=out_shapes, in_specs=[pl.BlockSpec(memor...  30.7 us
    ppermute x16, starting transfers between devices, traded(): return lax.ppermute(block, axis, pairs(axis, linked))  26.3 us
    ppermute x16, waiting for transfers between devices, traded(): return lax.ppermute(block, axis, pairs(axis, linked))  5.82 us
    ppermute x5, starting transfers between devices, swapped(): return lax.ppermute(x, ('row', 'col'), route)  5.52 us
  transfers between devices with their start and end apart: 21, of which 5 were waited for; matrix products, arithmetic and copies ran while one was open for 0% of the time, Pallas kernels for 23%

profile of v3, /device:TPU:0, one launch (start us, length us, event | category | flops | bytes accessed | tf_op | source)
XLA Modules:
  0.0 69.8 jit_solution(2178370778384612134)
XLA Ops:
  0.0 5.6 %shard_map.46 = (f32[2,576,1152]{2,1,0:T(8,128)S(1)}, f32[3,96,96]{2,1,0:T(8,128)S(1)}, f32[17,8,1152]{2,1,0:T(8,128)S(1)}, f32[432,128]{1,0:T(8,128)S(1)}, f32[...) custom-call(f32[2,576,1152]{2,1,0:T(8,128)} %corr.1, ...), custom_call_target="tpu_custom_call" | custom-call | flops 1000 | bytes 1000 | tf_op jit(solution)/shard_map/pallas_call | solution.py:516
  6.5 1.5 %collective-permute-start = (f32[48,128]{1,0:T(8,128)S(1)}, f32[48,128]{1,0:T(8,128)S(1)}, u32[]{:S(2)}, u32[]{:S(2)}) collective-permute-start(f32[48,128]{1,0:T(8,128)S(1)} %get-tuple-element.30.known), channel_id=1, source_target_pairs={{0,32},{8,40},{16,48},{24,56},{64,96},{72,104},{80,112},{88,120},{... | collective-permute-start | bytes 73736 | tf_op jit(solution)/shard_map/ppermute | solution.py:535
  8.0 1.4 %shard_map.47.refs_0_.refs_3_.refs_4_.refs_8_.refs_2_ = f32[9,576,128]{2,1,0:T(8,128)S(1)} custom-call(f32[3,96,96]{2,1,0:T(8,128)S(1)} %get-tuple-element.31.bonds), custom_call_target="tpu_custom_call" | custom-call | flops 1000 | bytes 1000 | tf_op jit(solution)/shard_map/pallas_call | solution.py:516
  10.3 2.7 %collective-permute-start.1 = (f32[72,128]{1,0:T(8,128)S(1)}, f32[72,128]{1,0:T(8,128)S(1)}, u32[]{:S(2)}, u32[]{:S(2)}) collective-permute-start(f32[72,128]{1,0:T(8,128)S(1)} %shard_map.48.refs_0_.known), channel_id=1, source_target_pairs={{0,96},{8,104},{16,112},{24,120},{32,64},{40,72},{48,80},{56,88},{... | collective-permute-start | bytes 110600 | tf_op jit(solution)/shard_map/ppermute | solution.py:535
  13.1 3.6 %collective-permute-start.5 = (f32[432,128]{1,0:T(8,128)S(1)}, f32[432,128]{1,0:T(8,128)S(1)}, u32[]{:S(2)}, u32[]{:S(2)}) collective-permute-start(f32[432,128]{1,0:T(8,128)S(1)} %get-tuple-element.35), channel_id=1, source_target_pairs={{0,2},{1,3},{4,6},{5,7},{2,0},{3,1},{6,4},{7,5},{8,10},{9,11},{12,... | collective-permute-start | bytes 663560 | tf_op jit(solution)/shard_map/ppermute | solution.py:535
  16.6 2.4 %shard_map.49.refs_0_ = f32[2,576,1152]{2,1,0:T(8,128)S(1)} custom-call(f32[72,128]{1,0:T(8,128)S(1)} %shard_map.48.refs_0_.known, f32[2,576,1152]{2,1,0:T(8,128)S(1)} %get-tuple-element.32.refs_1_.refs_2_.refs_3_.y, f32[2,576,1152]{2,1,0:T(8,128)S(1)} %get-tuple-element.32.refs_1_.refs_2_.refs_3_.y, ...), custom_call_target="tpu_custom_call" | custom-call | flops 1000 | bytes 1000 | tf_op jit(solution)/shard_map/pallas_call | solution.py:516
  21.3 2.7 %collective-permute-start.4 = (f32[120,128]{1,0:T(8,128)S(1)}, f32[120,128]{1,0:T(8,128)S(1)}, u32[]{:S(2)}, u32[]{:S(2)}) collective-permute-start(f32[120,128]{1,0:T(8,128)S(1)} %shard_map.51.known.refs_1_), channel_id=1, source_target_pairs={{0,16},{8,24},{32,48},{40,56},{64,80},{72,88},{96,112},{104,120},{... | collective-permute-start | bytes 184328 | tf_op jit(solution)/shard_map/ppermute | solution.py:535
  24.0 2.2 %collective-permute-done.4.got = f32[120,128]{1,0:T(8,128)S(1)} collective-permute-done((f32[120,128]{1,0:T(8,128)S(1)}, f32[120,128]{1,0:T(8,128)S(1)}, u32[]{:S(2)}, u32[]{:S(2)}) %collective-permute-start.4) | collective-permute-done | bytes 61472 | tf_op jit(solution)/shard_map/ppermute | solution.py:535
  26.3 4.5 %collective-permute-start.7 = (f32[120,128]{1,0:T(8,128)S(1)}, f32[120,128]{1,0:T(8,128)S(1)}, u32[]{:S(2)}, u32[]{:S(2)}) collective-permute-start(f32[120,128]{1,0:T(8,128)S(1)} %get-tuple-element.38), channel_id=1, source_target_pairs={{0,20},{1,21},{2,22},{3,23},{4,16},{5,17},{6,18},{7,19},{8,28},{9,... | collective-permute-start | bytes 184328 | tf_op jit(solution)/shard_map/ppermute | solution.py:630
  33.2 1.8 %shard_map.57.refs_0_ = f32[2,576,1152]{2,1,0:T(8,128)S(1)} custom-call(f32[2,576,1152]{2,1,0:T(8,128)S(1)} %shard_map.53.refs_0_, f32[72,128]{1,0:T(8,128)S(1)} %get-tuple-element.41.refs_1_.known, f32[2,576,1152]{2,1,0:T(8,128)S(1)} %get-tuple-element.32.refs_1_.refs_2_.refs_3_.y, ...), custom_call_target="tpu_custom_call", output_to_operand_aliasing={{}: (0, {})} | custom-call | flops 1000 | bytes 1000 | tf_op jit(solution)/shard_map/pallas_call | solution.py:516
  35.1 2.1 %collective-permute-done.10.got = f32[72,128]{1,0:T(8,128)S(1)} collective-permute-done((f32[72,128]{1,0:T(8,128)S(1)}, f32[72,128]{1,0:T(8,128)S(1)}, u32[]{:S(2)}, u32[]{:S(2)}) %collective-permute-start.10) | collective-permute-done | bytes 36896 | tf_op jit(solution)/shard_map/ppermute | solution.py:535
  37.2 4.0 %collective-permute-start.13 = (f32[48,128]{1,0:T(8,128)S(1)}, f32[48,128]{1,0:T(8,128)S(1)}, u32[]{:S(2)}, u32[]{:S(2)}) collective-permute-start(f32[48,128]{1,0:T(8,128)S(1)} %get-tuple-element.46), channel_id=1, source_target_pairs={{0,3},{1,2},{4,7},{5,6},{3,0},{2,1},{7,4},{6,5},{8,11},{9,10},{12,... | collective-permute-start | bytes 73736 | tf_op jit(solution)/shard_map/ppermute | solution.py:535
  41.1 1.8 %shard_map.60.refs_0_.base = f32[2,576,1152]{2,1,0:T(8,128)S(1)} custom-call(f32[2,576,1152]{2,1,0:T(8,128)S(1)} %shard_map.57.refs_0_, f32[48,128]{1,0:T(8,128)S(1)} %get-tuple-element.44.refs_1_.known, f32[2,576,1152]{2,1,0:T(8,128)S(1)} %get-tuple-element.32.refs_1_.refs_2_.refs_3_.y, ...), custom_call_target="tpu_custom_call", output_to_operand_aliasing={{}: (0, {})} | custom-call | flops 1000 | bytes 1000 | tf_op jit(solution)/shard_map/pallas_call | solution.py:516
  43.0 4.9 %shard_map.63 = (f32[2,576,1152]{2,1,0:T(8,128)S(1)}, f32[432,128]{1,0:T(8,128)S(1)}, f32[432,128]{1,0:T(8,128)S(1)}, f32[288,128]{1,0:T(8,128)S(1)}, f32[2,24,1...) custom-call(f32[2,576,1152]{2,1,0:T(8,128)S(1)} %shard_map.60.refs_0_.ba, ...), custom_call_target="tpu_custom_call" | custom-call | flops 1000 | bytes 1000 | tf_op jit(solution)/shard_map/pallas_call | solution.py:516
  48.3 4.4 %collective-permute-start.16 = (f32[432,128]{1,0:T(8,128)S(1)}, f32[432,128]{1,0:T(8,128)S(1)}, u32[]{:S(2)}, u32[]{:S(2)}) collective-permute-start(f32[432,128]{1,0:T(8,128)S(1)} %get-tuple-element.50), channel_id=1, source_target_pairs={{0,2},{1,3},{4,6},{5,7},{2,0},{3,1},{6,4},{7,5},{8,10},{9,11},{12,... | collective-permute-start | bytes 663560 | tf_op jit(solution)/shard_map/ppermute | solution.py:535
  53.6 1.2 %shard_map.64.refs_0_.refs_1_ = f32[2,576,1152]{2,1,0:T(8,128)S(1)} custom-call(f32[2,576,1152]{2,1,0:T(8,128)S(1)} %get-tuple-element.47.refs_0_.refs_2_.refs_1_.y1, f32[2,576,1152]{2,1,0:T(8,128)S(1)} %get-tuple-element.32.refs_1_.refs_2_.refs_3_.y, f32[9,576,128]{2,1,0:T(8,128)S(1)} %shard_map.47.refs_0_.refs_3_.refs_4_.refs_8_.refs_2_, ...), custom_call_target="tpu_custom_call" | custom-call | flops 1000 | bytes 1000 | tf_op jit(solution)/shard_map/pallas_call | solution.py:516
  54.8 1.2 %collective-permute-start.18 = (f32[2,24,1152]{2,1,0:T(8,128)S(1)}, f32[2,24,1152]{2,1,0:T(8,128)S(1)}, u32[]{:S(2)}, u32[]{:S(2)}) collective-permute-start(f32[2,24,1152]{2,1,0:T(8,128)S(1)} %shard_map.70), channel_id=1, source_target_pairs={{0,32},{8,40},{16,48},{24,56},{64,96},{72,104},{80,112},{88,120},{... | collective-permute-start | bytes 663560 | tf_op jit(solution)/shard_map/ppermute | solution.py:535
  56.0 1.2 %shard_map.65.refs_0_.refs_1_ = f32[2,576,1152]{2,1,0:T(8,128)S(1)} custom-call(f32[2,576,1152]{2,1,0:T(8,128)S(1)} %shard_map.64.refs_0_.refs_1_, f32[2,24,1152]{2,1,0:T(8,128)S(1)} %collective-permute-done.14.refs_1_.refs_5_, f32[2,576,1152]{2,1,0:T(8,128)S(1)} %get-tuple-element.47.refs_0_.refs_2_.refs_1_.y1, ...), custom_call_target="tpu_custom_call", output_to_operand_aliasing={{}: (0, {})} | custom-call | flops 1000 | bytes 1000 | tf_op jit(solution)/shard_map/pallas_call | solution.py:516
  57.2 3.2 %collective-permute-start.19 = (f32[2,24,1152]{2,1,0:T(8,128)S(1)}, f32[2,24,1152]{2,1,0:T(8,128)S(1)}, u32[]{:S(2)}, u32[]{:S(2)}) collective-permute-start(f32[2,24,1152]{2,1,0:T(8,128)S(1)} %shard_map.71), channel_id=1, source_target_pairs={{0,96},{8,104},{16,112},{24,120},{32,64},{40,72},{48,80},{56,88},{... | collective-permute-start | bytes 663560 | tf_op jit(solution)/shard_map/ppermute | solution.py:535
  60.5 1.2 %shard_map.66.refs_0_ = f32[2,576,1152]{2,1,0:T(8,128)S(1)} custom-call(f32[2,576,1152]{2,1,0:T(8,128)S(1)} %shard_map.65.refs_0_.refs_1_, f32[288,128]{1,0:T(8,128)S(1)} %collective-permute-done.15.refs_1_.refs_2_, f32[2,576,1152]{2,1,0:T(8,128)S(1)} %get-tuple-element.47.refs_0_.refs_2_.refs_1_.y1, ...), custom_call_target="tpu_custom_call", output_to_operand_aliasing={{}: (0, {})} | custom-call | flops 1000 | bytes 1000 | tf_op jit(solution)/shard_map/pallas_call | solution.py:516
  61.6 1.2 %shard_map.67.refs_0_ = f32[2,576,1152]{2,1,0:T(8,128)S(1)} custom-call(f32[2,576,1152]{2,1,0:T(8,128)S(1)} %shard_map.66.refs_0_, f32[2,576,1152]{2,1,0:T(8,128)S(1)} %get-tuple-element.47.refs_0_.refs_2_.refs_1_.y1, f32[2,576,1152]{2,1,0:T(8,128)S(1)} %get-tuple-element.32.refs_1_.refs_2_.refs_3_.y, ...), custom_call_target="tpu_custom_call", output_to_operand_aliasing={{}: (0, {})} | custom-call | flops 1000 | bytes 1000 | tf_op jit(solution)/shard_map/pallas_call | solution.py:516
  62.8 1.2 %shard_map.68.refs_0_ = f32[2,576,1152]{2,1,0:T(8,128)S(1)} custom-call(f32[2,576,1152]{2,1,0:T(8,128)S(1)} %shard_map.67.refs_0_, f32[2,576,1152]{2,1,0:T(8,128)S(1)} %get-tuple-element.47.refs_0_.refs_2_.refs_1_.y1, f32[2,576,1152]{2,1,0:T(8,128)S(1)} %get-tuple-element.32.refs_1_.refs_2_.refs_3_.y, ...), custom_call_target="tpu_custom_call", output_to_operand_aliasing={{}: (0, {})} | custom-call | flops 1000 | bytes 1000 | tf_op jit(solution)/shard_map/pallas_call | solution.py:516
  64.0 1.2 %shard_map.69.base = f32[2,576,1152]{2,1,0:T(8,128)S(1)} custom-call(f32[2,576,1152]{2,1,0:T(8,128)S(1)} %shard_map.68.refs_0_, f32[2,576,1152]{2,1,0:T(8,128)S(1)} %get-tuple-element.47.refs_0_.refs_2_.refs_1_.y1, f32[2,576,1152]{2,1,0:T(8,128)S(1)} %get-tuple-element.32.refs_1_.refs_2_.refs_3_.y, ...), custom_call_target="tpu_custom_call", output_to_operand_aliasing={{}: (0, {})} | custom-call | flops 1000 | bytes 1000 | tf_op jit(solution)/shard_map/pallas_call | solution.py:516
  65.3 4.4 %shard_map.72 = f32[2,576,1152]{2,1,0:T(8,128)} custom-call(f32[2,576,1152]{2,1,0:T(8,128)S(1)} %shard_map.69.base, f32[2,576,1152]{2,1,0:T(8,128)S(1)} %get-tuple-element.47.refs_0_.refs_2_.refs_1_.y1, f32[432,128]{1,0:T(8,128)S(1)} %collective-permute-done.16.refs_0_, f32[432,128]{1,0:T(8,128)S(1)} %collective-permute-done.17.refs_1_, ...), custom_call_target="tpu_custom_call" | custom-call | flops 1000 | bytes 1000 | tf_op jit(solution)/shard_map/pallas_call | solution.py:516
  (45 shorter events, 7.8 us)
Async XLA Ops:
  5.6 15.0 %collective-permute-start.3 = (f32[288,128]{1,0:T(8,128)S(1)}, f32[288,128]{1,0:T(8,128)S(1)}, u32[]{:S(2)}, u32[]{:S(2)}) collective-permute-start(f32[288,128]{1,0:T(8,128)S(1)} %get-tuple-element.34), channel_id=1, source_target_pairs={{0,1},{2,3},{4,5},{6,7},{1,0},{3,2},{5,4},{7,6},{8,9},{10,11},{12,... | collective-permute-start | bytes 442376 | tf_op jit(solution)/shard_map/ppermute | solution.py:535
  6.5 3.9 %collective-permute-start = (f32[48,128]{1,0:T(8,128)S(1)}, f32[48,128]{1,0:T(8,128)S(1)}, u32[]{:S(2)}, u32[]{:S(2)}) collective-permute-start(f32[48,128]{1,0:T(8,128)S(1)} %get-tuple-element.30.known), channel_id=1, source_target_pairs={{0,32},{8,40},{16,48},{24,56},{64,96},{72,104},{80,112},{88,120},{... | collective-permute-start | bytes 73736 | tf_op jit(solution)/shard_map/ppermute | solution.py:535
  10.3 8.7 %collective-permute-start.1 = (f32[72,128]{1,0:T(8,128)S(1)}, f32[72,128]{1,0:T(8,128)S(1)}, u32[]{:S(2)}, u32[]{:S(2)}) collective-permute-start(f32[72,128]{1,0:T(8,128)S(1)} %shard_map.48.refs_0_.known), channel_id=1, source_target_pairs={{0,96},{8,104},{16,112},{24,120},{32,64},{40,72},{48,80},{56,88},{... | collective-permute-start | bytes 110600 | tf_op jit(solution)/shard_map/ppermute | solution.py:535
  13.1 13.2 %collective-permute-start.5 = (f32[432,128]{1,0:T(8,128)S(1)}, f32[432,128]{1,0:T(8,128)S(1)}, u32[]{:S(2)}, u32[]{:S(2)}) collective-permute-start(f32[432,128]{1,0:T(8,128)S(1)} %get-tuple-element.35), channel_id=1, source_target_pairs={{0,2},{1,3},{4,6},{5,7},{2,0},{3,1},{6,4},{7,5},{8,10},{9,11},{12,... | collective-permute-start | bytes 663560 | tf_op jit(solution)/shard_map/ppermute | solution.py:535
  16.6 9.6 %collective-permute-start.6 = (f32[432,128]{1,0:T(8,128)S(1)}, f32[432,128]{1,0:T(8,128)S(1)}, u32[]{:S(2)}, u32[]{:S(2)}) collective-permute-start(f32[432,128]{1,0:T(8,128)S(1)} %get-tuple-element.36), channel_id=1, source_target_pairs={{0,8},{1,9},{2,4},{3,5},{4,2},{5,3},{6,14},{7,15},{8,0},{9,1},{10,... | collective-permute-start | bytes 663560 | tf_op jit(solution)/shard_map/ppermute | solution.py:630
  19.1 1.5 %collective-permute-start.2 = (f32[120,128]{1,0:T(8,128)S(1)}, f32[120,128]{1,0:T(8,128)S(1)}, u32[]{:S(2)}, u32[]{:S(2)}) collective-permute-start(f32[120,128]{1,0:T(8,128)S(1)} %shard_map.50.known.refs_1_), channel_id=1, source_target_pairs={{0,8},{16,24},{32,40},{48,56},{64,72},{80,88},{96,104},{112,120},{... | collective-permute-start | bytes 184328 | tf_op jit(solution)/shard_map/ppermute | solution.py:535
  19.7 13.3 %collective-permute-start.8 = (f32[2,24,1152]{2,1,0:T(8,128)S(1)}, f32[2,24,1152]{2,1,0:T(8,128)S(1)}, u32[]{:S(2)}, u32[]{:S(2)}) collective-permute-start(f32[2,24,1152]{2,1,0:T(8,128)S(1)} %shard_map.54), channel_id=1, source_target_pairs={{0,32},{8,40},{16,48},{24,56},{64,96},{72,104},{80,112},{88,120},{... | collective-permute-start | bytes 663560 | tf_op jit(solution)/shard_map/ppermute | solution.py:535
  20.6 12.4 %collective-permute-start.9 = (f32[2,24,1152]{2,1,0:T(8,128)S(1)}, f32[2,24,1152]{2,1,0:T(8,128)S(1)}, u32[]{:S(2)}, u32[]{:S(2)}) collective-permute-start(f32[2,24,1152]{2,1,0:T(8,128)S(1)} %shard_map.55), channel_id=1, source_target_pairs={{0,96},{8,104},{16,112},{24,120},{32,64},{40,72},{48,80},{56,88},{... | collective-permute-start | bytes 663560 | tf_op jit(solution)/shard_map/ppermute | solution.py:535
  21.3 4.9 %collective-permute-start.4 = (f32[120,128]{1,0:T(8,128)S(1)}, f32[120,128]{1,0:T(8,128)S(1)}, u32[]{:S(2)}, u32[]{:S(2)}) collective-permute-start(f32[120,128]{1,0:T(8,128)S(1)} %shard_map.51.known.refs_1_), channel_id=1, source_target_pairs={{0,16},{8,24},{32,48},{40,56},{64,80},{72,88},{96,112},{104,120},{... | collective-permute-start | bytes 184328 | tf_op jit(solution)/shard_map/ppermute | solution.py:535
  26.3 6.7 %collective-permute-start.7 = (f32[120,128]{1,0:T(8,128)S(1)}, f32[120,128]{1,0:T(8,128)S(1)}, u32[]{:S(2)}, u32[]{:S(2)}) collective-permute-start(f32[120,128]{1,0:T(8,128)S(1)} %get-tuple-element.38), channel_id=1, source_target_pairs={{0,20},{1,21},{2,22},{3,23},{4,16},{5,17},{6,18},{7,19},{8,28},{9,... | collective-permute-start | bytes 184328 | tf_op jit(solution)/shard_map/ppermute | solution.py:630
  30.8 6.4 %collective-permute-start.11 = (f32[2,24,1152]{2,1,0:T(8,128)S(1)}, f32[2,24,1152]{2,1,0:T(8,128)S(1)}, u32[]{:S(2)}, u32[]{:S(2)}) collective-permute-start(f32[2,24,1152]{2,1,0:T(8,128)S(1)} %shard_map.58), channel_id=1, source_target_pairs={{0,32},{1,33},{2,34},{3,35},{4,36},{5,37},{6,38},{7,39},{8,16},{9,... | collective-permute-start | bytes 663560 | tf_op jit(solution)/shard_map/ppermute | solution.py:630
  33.0 10.0 %collective-permute-start.12 = (f32[2,24,1152]{2,1,0:T(8,128)S(1)}, f32[2,24,1152]{2,1,0:T(8,128)S(1)}, u32[]{:S(2)}, u32[]{:S(2)}) collective-permute-start(f32[2,24,1152]{2,1,0:T(8,128)S(1)} %shard_map.61), channel_id=1, source_target_pairs={{0,8},{16,24},{32,40},{48,56},{64,72},{80,88},{96,104},{112,120},{... | collective-permute-start | bytes 663560 | tf_op jit(solution)/shard_map/ppermute | solution.py:535
  33.1 4.0 %collective-permute-start.10 = (f32[72,128]{1,0:T(8,128)S(1)}, f32[72,128]{1,0:T(8,128)S(1)}, u32[]{:S(2)}, u32[]{:S(2)}) collective-permute-start(f32[72,128]{1,0:T(8,128)S(1)} %get-tuple-element.42), channel_id=1, source_target_pairs={{0,1},{2,3},{4,5},{6,7},{1,0},{3,2},{5,4},{7,6},{8,9},{10,11},{12,... | collective-permute-start | bytes 110600 | tf_op jit(solution)/shard_map/ppermute | solution.py:535
  37.2 5.8 %collective-permute-start.13 = (f32[48,128]{1,0:T(8,128)S(1)}, f32[48,128]{1,0:T(8,128)S(1)}, u32[]{:S(2)}, u32[]{:S(2)}) collective-permute-start(f32[48,128]{1,0:T(8,128)S(1)} %get-tuple-element.46), channel_id=1, source_target_pairs={{0,3},{1,2},{4,7},{5,6},{3,0},{2,1},{7,4},{6,5},{8,11},{9,10},{12,... | collective-permute-start | bytes 73736 | tf_op jit(solution)/shard_map/ppermute | solution.py:535
  47.9 6.9 %collective-permute-start.14 = (f32[2,24,1152]{2,1,0:T(8,128)S(1)}, f32[2,24,1152]{2,1,0:T(8,128)S(1)}, u32[]{:S(2)}, u32[]{:S(2)}) collective-permute-start(f32[2,24,1152]{2,1,0:T(8,128)S(1)} %get-tuple-element.48), channel_id=1, source_target_pairs={{0,8},{16,24},{32,40},{48,56},{64,72},{80,88},{96,104},{112,120},{... | collective-permute-start | bytes 663560 | tf_op jit(solution)/shard_map/ppermute | solution.py:535
  48.0 9.2 %collective-permute-start.15 = (f32[288,128]{1,0:T(8,128)S(1)}, f32[288,128]{1,0:T(8,128)S(1)}, u32[]{:S(2)}, u32[]{:S(2)}) collective-permute-start(f32[288,128]{1,0:T(8,128)S(1)} %get-tuple-element.49), channel_id=1, source_target_pairs={{0,1},{2,3},{4,5},{6,7},{1,0},{3,2},{5,4},{7,6},{8,9},{10,11},{12,... | collective-permute-start | bytes 442376 | tf_op jit(solution)/shard_map/ppermute | solution.py:535
  48.3 16.9 %collective-permute-start.16 = (f32[432,128]{1,0:T(8,128)S(1)}, f32[432,128]{1,0:T(8,128)S(1)}, u32[]{:S(2)}, u32[]{:S(2)}) collective-permute-start(f32[432,128]{1,0:T(8,128)S(1)} %get-tuple-element.50), channel_id=1, source_target_pairs={{0,2},{1,3},{4,6},{5,7},{2,0},{3,1},{6,4},{7,5},{8,10},{9,11},{12,... | collective-permute-start | bytes 663560 | tf_op jit(solution)/shard_map/ppermute | solution.py:535
  52.7 12.5 %collective-permute-start.17 = (f32[432,128]{1,0:T(8,128)S(1)}, f32[432,128]{1,0:T(8,128)S(1)}, u32[]{:S(2)}, u32[]{:S(2)}) collective-permute-start(f32[432,128]{1,0:T(8,128)S(1)} %get-tuple-element.51), channel_id=1, source_target_pairs={{0,8},{1,9},{2,4},{3,5},{4,2},{5,3},{6,14},{7,15},{8,0},{9,1},{10,... | collective-permute-start | bytes 663560 | tf_op jit(solution)/shard_map/ppermute | solution.py:630
  52.7 12.5 %collective-permute-start.20 = (f32[2,24,1152]{2,1,0:T(8,128)S(1)}, f32[2,24,1152]{2,1,0:T(8,128)S(1)}, u32[]{:S(2)}, u32[]{:S(2)}) collective-permute-start(f32[2,24,1152]{2,1,0:T(8,128)S(1)} %get-tuple-element.54), channel_id=1, source_target_pairs={{0,32},{1,33},{2,34},{3,35},{4,36},{5,37},{6,38},{7,39},{8,16},{9,... | collective-permute-start | bytes 663560 | tf_op jit(solution)/shard_map/ppermute | solution.py:630
  54.8 10.4 %collective-permute-start.18 = (f32[2,24,1152]{2,1,0:T(8,128)S(1)}, f32[2,24,1152]{2,1,0:T(8,128)S(1)}, u32[]{:S(2)}, u32[]{:S(2)}) collective-permute-start(f32[2,24,1152]{2,1,0:T(8,128)S(1)} %shard_map.70), channel_id=1, source_target_pairs={{0,32},{8,40},{16,48},{24,56},{64,96},{72,104},{80,112},{88,120},{... | collective-permute-start | bytes 663560 | tf_op jit(solution)/shard_map/ppermute | solution.py:535
  57.2 8.0 %collective-permute-start.19 = (f32[2,24,1152]{2,1,0:T(8,128)S(1)}, f32[2,24,1152]{2,1,0:T(8,128)S(1)}, u32[]{:S(2)}, u32[]{:S(2)}) collective-permute-start(f32[2,24,1152]{2,1,0:T(8,128)S(1)} %shard_map.71), channel_id=1, source_target_pairs={{0,96},{8,104},{16,112},{24,120},{32,64},{40,72},{48,80},{56,88},{... | collective-permute-start | bytes 663560 | tf_op jit(solution)/shard_map/ppermute | solution.py:535

commit v4 on v3

--- a/solution.py
+++ b/solution.py
@@ -86,7 +86,7 @@
 
 def col_weights(bonds, colw):
     _, col_id = place()
-    down, across, rep, dot = tables(bonds)
+    down, across, rep, _ = tables(bonds)
     last = PATCH - 1
     wide = (LATTICE, COLUMNS)
     j = iota(wide, 1)
@@ -99,17 +99,29 @@
     ga = PATCH * (col_id // 2) + a
     gb = PATCH * (2 * parity + g) + b
 
-    def pick_cols(table, da, db):
-        cols = dot(table, on(sub == gb + db))
-        return jnp.sum(jnp.where(sub == ga + da, cols, 0.0), axis=0, keepdims=True)
-
+    def columns_of(tables, db):
+        stacked = jnp.concatenate(tables, 0)
+        parts = []
+        for _ in range(3):
+            parts.append(stacked.astype(jnp.bfloat16))
+            stacked = stacked - parts[-1].astype(F32)
+        hot = on(sub == gb + db).astype(jnp.bfloat16)
+        high, mid, low = [jnp.dot(v, hot, preferred_element_type=F32) for v in parts]
+        return (high + mid) + low
+
+    def pick(columns, n, da):
+        rows = columns[n * LATTICE : (n + 1) * LATTICE]
+        return jnp.sum(jnp.where(sub == ga + da, rows, 0.0), axis=0, keepdims=True)
+
+    here = columns_of([down, across, rep], 0)
+    before = columns_of([across], -1)
     a = a[0:1]
     b = b[0:1]
     g = g[0:1]
-    dn = TIME_STEP * pick_cols(down, 0, 0)
-    up = TIME_STEP * pick_cols(down, -1, 0)
-    rt = TIME_STEP * pick_cols(across, 0, 0)
-    lf = TIME_STEP * pick_cols(across, 0, -1)
+    dn = TIME_STEP * pick(here, 0, 0)
+    up = TIME_STEP * pick(here, 0, -1)
+    rt = TIME_STEP * pick(here, 1, 0)
+    lf = TIME_STEP * pick(before, 0, 0)
     tails0 = rt * on(b == last) * on(g == 0)
     heads1 = lf * on(b == 0) * on(g == 1)
     tails1 = rt * on(b == last) * on(g == 1)
@@ -127,7 +139,7 @@
         C_RT_E: tails0 * rt_e, C_RT_F: tails0 * (1.0 - rt_e),
         C_LF_E: heads1 * lf_e, C_LF_F: heads1 * (1.0 - lf_e),
         C_X_E: x_even * xe_e + x_odd * xo_e, C_X_F: x_even * (1.0 - xe_e) + x_odd * (1.0 - xo_e),
-        COL_U: TIME_STEP * pick_cols(rep, 0, 0),
+        COL_U: TIME_STEP * pick(here, 2, 0),
         C_DN_ALL: dn, C_UP_ALL: up, C_RT_ALL: rt, C_LF_ALL: lf,
     }
     for k, v in values.items():
@@ -205,11 +217,11 @@
 
     steps = PATCH // 4
     if ready is None:
-        lax.fori_loop(0, steps, step, 0)
+        lax.fori_loop(0, steps, step, 0, unroll=2)
     else:
         for i in range(CHUNKS):
             ready(i)
-            lax.fori_loop(i * steps // CHUNKS, (i + 1) * steps // CHUNKS, step, 0)
+            lax.fori_loop(i * steps // CHUNKS, (i + 1) * steps // CHUNKS, step, 0, unroll=2)
     for p in range(2):
         for out, flip in ((down_a, row_up_first), (down_b, jnp.logical_not(row_up_first))):
             out[p] = src[p, pl.ds(pl.multiple_of(jnp.where(flip, SQUARE - PATCH, 0), 8), PATCH), :]
@@ -275,7 +287,7 @@
                 share(a, [start + d for start in starts for d in range(2)])
                 return carry
 
-            lax.fori_loop(0, PATCH, step, 0)
+            lax.fori_loop(0, PATCH, step, 0, unroll=3)
 
         @pl.when(over)
         def _():
@@ -472,7 +484,7 @@
     fold = 3 * PATCH // 4
     stops = (0, fold, PATCH) if chunk_done is None else (0, fold // 3, 2 * fold // 3, fold, PATCH - 2, PATCH)
     for start, stop in zip(stops, stops[1:]):
-        lax.fori_loop(start, stop, lambda a, c, f=start >= fold: (strip(a, f), c)[1], 0, unroll=2)
+        lax.fori_loop(start, stop, lambda a, c, f=start >= fold: (strip(a, f), c)[1], 0, unroll=3 if (stop - start) % 3 == 0 else 2)
         if start == 0:
             rim(0, UP_RIM, down_b, down_a)
         if stop == PATCH:
@@ -664,12 +676,12 @@
     face_b = swap_face_b(face_b)
     face_a = swap_face_a(face_a)
     known = grow(share, flipped(share, "row", 4), first_work)
-    part = piece(0, None, known)
-    known = grow(known, flipped(known, "row", 12), part)
+    known = grow(known, flipped(known, "row", 12))
     down_a = swap_down_a(tie(down_a, known))
     known = added(known, flipped(known, "row", 1), side)
     down_b = swap_down_b(tie(down_b, known))
-    known, send = halve_all(known, flipped(known, "row", 2), face_a, face_b)
+    part = piece(0, None, known)
+    known, send = halve_all(known, flipped(known, "row", 2), part, face_b, face_a)
     across_b = swap_across_b(tie(across_b, known))
     part = piece(1, part, known)
     known, send = halve_four(known, swap_bits(send, 2, 4), part, down_a, down_b)

time: 69.9 us -> 67.9 us (0.971); the launches traced: 69.8 us -> 67 us
  starting transfers between devices: 31.9 us -> 29.1 us
  waiting for transfers between devices: 6.76 us -> 8.34 us
  Pallas kernels: 30.7 us -> 29.2 us
    ppermute x16, starting transfers between devices: 26.3 us -> 23.7 us  [traded(): return lax.ppermute(block, axis, pairs(axis, linked))]
    ppermute x16, waiting for transfers between devices: 5.82 us -> 8.32 us  [traded(): return lax.ppermute(block, axis, pairs(axis, linked))]
    pallas_call x27, Pallas kernels: 30.7 us -> 29.2 us  [call(): pl.pallas_call(kernel, out_shape=out_shapes, in_specs=[pl.BlockSpec(memor...]
    ppermute x5, waiting for transfers between devices: 0.95 us -> 0.02 us  [swapped(): return lax.ppermute(x, ('row', 'col'), route)]
  transfers between devices with their start and end apart: 21 -> 21, of which waited for: 5 -> 7; matrix products, arithmetic and copies ran while one was open for 0% -> 0% of each run, Pallas kernels for 23% -> 24%
where the time goes in v4:
time: 67.9 us; the launch traced here: 67 us
  Pallas kernels  29.2 us (43%)
  starting transfers between devices  29.1 us (43%)
  waiting for transfers between devices  8.34 us (12%)
    pallas_call x27, Pallas kernels, call(): pl.pallas_call(kernel, out_shape=out_shapes, in_specs=[pl.BlockSpec(memor...  29.2 us
    ppermute x16, starting transfers between devices, traded(): return lax.ppermute(block, axis, pairs(axis, linked))  23.7 us
    ppermute x16, waiting for transfers between devices, traded(): return lax.ppermute(block, axis, pairs(axis, linked))  8.32 us
    ppermute x5, starting transfers between devices, swapped(): return lax.ppermute(x, ('row', 'col'), route)  5.4 us
  transfers between devices with their start and end apart: 21, of which 7 were waited for; matrix products, arithmetic and copies ran while one was open for 0% of the time, Pallas kernels for 24%

profile of v4, /device:TPU:0, one launch (start us, length us, event | category | flops | bytes accessed | tf_op | source)
XLA Modules:
  0.0 67.0 jit_solution(11542645298755096065)
XLA Ops:
  0.0 4.4 %shard_map.46 = (f32[2,576,1152]{2,1,0:T(8,128)S(1)}, f32[3,96,96]{2,1,0:T(8,128)S(1)}, f32[17,8,1152]{2,1,0:T(8,128)S(1)}, f32[432,128]{1,0:T(8,128)S(1)}, f32[...) custom-call(f32[2,576,1152]{2,1,0:T(8,128)} %corr.1, ...), custom_call_target="tpu_custom_call" | custom-call | flops 1000 | bytes 1000 | tf_op jit(solution)/shard_map/pallas_call | solution.py:528
  5.5 1.5 %collective-permute-start = (f32[48,128]{1,0:T(8,128)S(1)}, f32[48,128]{1,0:T(8,128)S(1)}, u32[]{:S(2)}, u32[]{:S(2)}) collective-permute-start(f32[48,128]{1,0:T(8,128)S(1)} %get-tuple-element.30.known), channel_id=1, source_target_pairs={{0,32},{8,40},{16,48},{24,56},{64,96},{72,104},{80,112},{88,120},{... | collective-permute-start | bytes 73736 | tf_op jit(solution)/shard_map/ppermute | solution.py:547
  7.0 1.4 %shard_map.47.refs_0_.refs_3_.refs_4_.refs_8_.refs_2_ = f32[9,576,128]{2,1,0:T(8,128)S(1)} custom-call(f32[3,96,96]{2,1,0:T(8,128)S(1)} %get-tuple-element.31.bonds), custom_call_target="tpu_custom_call" | custom-call | flops 1000 | bytes 1000 | tf_op jit(solution)/shard_map/pallas_call | solution.py:528
  9.3 2.8 %collective-permute-start.1 = (f32[72,128]{1,0:T(8,128)S(1)}, f32[72,128]{1,0:T(8,128)S(1)}, u32[]{:S(2)}, u32[]{:S(2)}) collective-permute-start(f32[72,128]{1,0:T(8,128)S(1)} %shard_map.48.known), channel_id=1, source_target_pairs={{0,96},{8,104},{16,112},{24,120},{32,64},{40,72},{48,80},{56,88},{... | collective-permute-start | bytes 110600 | tf_op jit(solution)/shard_map/ppermute | solution.py:547
  12.1 2.4 %collective-permute-done.1.got = f32[72,128]{1,0:T(8,128)S(1)} collective-permute-done((f32[72,128]{1,0:T(8,128)S(1)}, f32[72,128]{1,0:T(8,128)S(1)}, u32[]{:S(2)}, u32[]{:S(2)}) %collective-permute-start.1) | collective-permute-done | bytes 36896 | tf_op jit(solution)/shard_map/ppermute | solution.py:547
  14.5 3.9 %collective-permute-start.6 = (f32[432,128]{1,0:T(8,128)S(1)}, f32[432,128]{1,0:T(8,128)S(1)}, u32[]{:S(2)}, u32[]{:S(2)}) collective-permute-start(f32[432,128]{1,0:T(8,128)S(1)} %get-tuple-element.36), channel_id=1, source_target_pairs={{0,2},{1,3},{4,6},{5,7},{2,0},{3,1},{6,4},{7,5},{8,10},{9,11},{12,... | collective-permute-start | bytes 663560 | tf_op jit(solution)/shard_map/ppermute | solution.py:547
  18.8 2.4 %collective-permute-start.9 = (f32[2,24,1152]{2,1,0:T(8,128)S(1)}, f32[2,24,1152]{2,1,0:T(8,128)S(1)}, u32[]{:S(2)}, u32[]{:S(2)}) collective-permute-start(f32[2,24,1152]{2,1,0:T(8,128)S(1)} %shard_map.55), channel_id=1, source_target_pairs={{0,96},{8,104},{16,112},{24,120},{32,64},{40,72},{48,80},{56,88},{... | collective-permute-start | bytes 663560 | tf_op jit(solution)/shard_map/ppermute | solution.py:547
  21.2 1.6 %collective-permute-start.4 = (f32[120,128]{1,0:T(8,128)S(1)}, f32[120,128]{1,0:T(8,128)S(1)}, u32[]{:S(2)}, u32[]{:S(2)}) collective-permute-start(f32[120,128]{1,0:T(8,128)S(1)} %shard_map.50.refs_0_.known.refs_1_), channel_id=1, source_target_pairs={{0,16},{8,24},{32,48},{40,56},{64,80},{72,88},{96,112},{104,120},{... | collective-permute-start | bytes 184328 | tf_op jit(solution)/shard_map/ppermute | solution.py:547
  22.8 2.4 %shard_map.51.refs_0_ = f32[2,576,1152]{2,1,0:T(8,128)S(1)} custom-call(f32[120,128]{1,0:T(8,128)S(1)} %shard_map.50.refs_0_.known.refs_1_, f32[2,576,1152]{2,1,0:T(8,128)S(1)} %get-tuple-element.33.refs_1_.refs_2_.refs_3_.y, f32[2,576,1152]{2,1,0:T(8,128)S(1)} %get-tuple-element.33.refs_1_.refs_2_.refs_3_.y, ...), custom_call_target="tpu_custom_call" | custom-call | flops 1000 | bytes 1000 | tf_op jit(solution)/shard_map/pallas_call | solution.py:528
  26.1 3.9 %collective-permute-start.7 = (f32[120,128]{1,0:T(8,128)S(1)}, f32[120,128]{1,0:T(8,128)S(1)}, u32[]{:S(2)}, u32[]{:S(2)}) collective-permute-start(f32[120,128]{1,0:T(8,128)S(1)} %get-tuple-element.38), channel_id=1, source_target_pairs={{0,20},{1,21},{2,22},{3,23},{4,16},{5,17},{6,18},{7,19},{8,28},{9,... | collective-permute-start | bytes 184328 | tf_op jit(solution)/shard_map/ppermute | solution.py:642
  32.6 1.8 %shard_map.57.refs_0_ = f32[2,576,1152]{2,1,0:T(8,128)S(1)} custom-call(f32[2,576,1152]{2,1,0:T(8,128)S(1)} %shard_map.53.refs_0_, f32[72,128]{1,0:T(8,128)S(1)} %get-tuple-element.41.refs_1_.known, f32[2,576,1152]{2,1,0:T(8,128)S(1)} %get-tuple-element.33.refs_1_.refs_2_.refs_3_.y, ...), custom_call_target="tpu_custom_call", output_to_operand_aliasing={{}: (0, {})} | custom-call | flops 1000 | bytes 1000 | tf_op jit(solution)/shard_map/pallas_call | solution.py:528
  34.5 2.0 %collective-permute-done.10.got = f32[72,128]{1,0:T(8,128)S(1)} collective-permute-done((f32[72,128]{1,0:T(8,128)S(1)}, f32[72,128]{1,0:T(8,128)S(1)}, u32[]{:S(2)}, u32[]{:S(2)}) %collective-permute-start.10) | collective-permute-done | bytes 36896 | tf_op jit(solution)/shard_map/ppermute | solution.py:547
  36.5 2.7 %collective-permute-start.13 = (f32[48,128]{1,0:T(8,128)S(1)}, f32[48,128]{1,0:T(8,128)S(1)}, u32[]{:S(2)}, u32[]{:S(2)}) collective-permute-start(f32[48,128]{1,0:T(8,128)S(1)} %get-tuple-element.46), channel_id=1, source_target_pairs={{0,3},{1,2},{4,7},{5,6},{3,0},{2,1},{7,4},{6,5},{8,11},{9,10},{12,... | collective-permute-start | bytes 73736 | tf_op jit(solution)/shard_map/ppermute | solution.py:547
  39.2 1.8 %shard_map.60.refs_0_.base = f32[2,576,1152]{2,1,0:T(8,128)S(1)} custom-call(f32[2,576,1152]{2,1,0:T(8,128)S(1)} %shard_map.57.refs_0_, f32[48,128]{1,0:T(8,128)S(1)} %get-tuple-element.44.refs_1_.known, f32[2,576,1152]{2,1,0:T(8,128)S(1)} %get-tuple-element.33.refs_1_.refs_2_.refs_3_.y, ...), custom_call_target="tpu_custom_call", output_to_operand_aliasing={{}: (0, {})} | custom-call | flops 1000 | bytes 1000 | tf_op jit(solution)/shard_map/pallas_call | solution.py:528
  41.8 4.7 %shard_map.63 = (f32[2,576,1152]{2,1,0:T(8,128)S(1)}, f32[432,128]{1,0:T(8,128)S(1)}, f32[432,128]{1,0:T(8,128)S(1)}, f32[288,128]{1,0:T(8,128)S(1)}, f32[2,24,1...) custom-call(f32[2,576,1152]{2,1,0:T(8,128)S(1)} %shard_map.60.refs_0_.ba, ...), custom_call_target="tpu_custom_call" | custom-call | flops 1000 | bytes 1000 | tf_op jit(solution)/shard_map/pallas_call | solution.py:528
  46.8 3.8 %collective-permute-start.16 = (f32[432,128]{1,0:T(8,128)S(1)}, f32[432,128]{1,0:T(8,128)S(1)}, u32[]{:S(2)}, u32[]{:S(2)}) collective-permute-start(f32[432,128]{1,0:T(8,128)S(1)} %get-tuple-element.50), channel_id=1, source_target_pairs={{0,2},{1,3},{4,6},{5,7},{2,0},{3,1},{6,4},{7,5},{8,10},{9,11},{12,... | collective-permute-start | bytes 663560 | tf_op jit(solution)/shard_map/ppermute | solution.py:547
  52.2 1.7 %collective-permute-start.18 = (f32[2,24,1152]{2,1,0:T(8,128)S(1)}, f32[2,24,1152]{2,1,0:T(8,128)S(1)}, u32[]{:S(2)}, u32[]{:S(2)}) collective-permute-start(f32[2,24,1152]{2,1,0:T(8,128)S(1)} %shard_map.70), channel_id=1, source_target_pairs={{0,32},{8,40},{16,48},{24,56},{64,96},{72,104},{80,112},{88,120},{... | collective-permute-start | bytes 663560 | tf_op jit(solution)/shard_map/ppermute | solution.py:547
  53.9 1.2 %shard_map.65.refs_0_.refs_1_ = f32[2,576,1152]{2,1,0:T(8,128)S(1)} custom-call(f32[2,576,1152]{2,1,0:T(8,128)S(1)} %shard_map.64.refs_0_.refs_1_, f32[2,24,1152]{2,1,0:T(8,128)S(1)} %collective-permute-done.14.refs_1_.refs_5_, f32[2,576,1152]{2,1,0:T(8,128)S(1)} %get-tuple-element.47.refs_0_.refs_2_.refs_1_.y1, ...), custom_call_target="tpu_custom_call", output_to_operand_aliasing={{}: (0, {})} | custom-call | flops 1000 | bytes 1000 | tf_op jit(solution)/shard_map/pallas_call | solution.py:528
  55.1 1.4 %collective-permute-start.19 = (f32[2,24,1152]{2,1,0:T(8,128)S(1)}, f32[2,24,1152]{2,1,0:T(8,128)S(1)}, u32[]{:S(2)}, u32[]{:S(2)}) collective-permute-start(f32[2,24,1152]{2,1,0:T(8,128)S(1)} %shard_map.71), channel_id=1, source_target_pairs={{0,96},{8,104},{16,112},{24,120},{32,64},{40,72},{48,80},{56,88},{... | collective-permute-start | bytes 663560 | tf_op jit(solution)/shard_map/ppermute | solution.py:547
  57.7 1.2 %shard_map.67.refs_0_ = f32[2,576,1152]{2,1,0:T(8,128)S(1)} custom-call(f32[2,576,1152]{2,1,0:T(8,128)S(1)} %shard_map.66.refs_0_, f32[2,576,1152]{2,1,0:T(8,128)S(1)} %get-tuple-element.47.refs_0_.refs_2_.refs_1_.y1, f32[2,576,1152]{2,1,0:T(8,128)S(1)} %get-tuple-element.33.refs_1_.refs_2_.refs_3_.y, ...), custom_call_target="tpu_custom_call", output_to_operand_aliasing={{}: (0, {})} | custom-call | flops 1000 | bytes 1000 | tf_op jit(solution)/shard_map/pallas_call | solution.py:528
  58.8 1.2 %shard_map.68.refs_0_ = f32[2,576,1152]{2,1,0:T(8,128)S(1)} custom-call(f32[2,576,1152]{2,1,0:T(8,128)S(1)} %shard_map.67.refs_0_, f32[2,576,1152]{2,1,0:T(8,128)S(1)} %get-tuple-element.47.refs_0_.refs_2_.refs_1_.y1, f32[2,576,1152]{2,1,0:T(8,128)S(1)} %get-tuple-element.33.refs_1_.refs_2_.refs_3_.y, ...), custom_call_target="tpu_custom_call", output_to_operand_aliasing={{}: (0, {})} | custom-call | flops 1000 | bytes 1000 | tf_op jit(solution)/shard_map/pallas_call | solution.py:528
  60.0 1.2 %shard_map.69.base = f32[2,576,1152]{2,1,0:T(8,128)S(1)} custom-call(f32[2,576,1152]{2,1,0:T(8,128)S(1)} %shard_map.68.refs_0_, f32[2,576,1152]{2,1,0:T(8,128)S(1)} %get-tuple-element.47.refs_0_.refs_2_.refs_1_.y1, f32[2,576,1152]{2,1,0:T(8,128)S(1)} %get-tuple-element.33.refs_1_.refs_2_.refs_3_.y, ...), custom_call_target="tpu_custom_call", output_to_operand_aliasing={{}: (0, {})} | custom-call | flops 1000 | bytes 1000 | tf_op jit(solution)/shard_map/pallas_call | solution.py:528
  61.3 1.4 %collective-permute-done.19.refs_4_ = f32[2,24,1152]{2,1,0:T(8,128)S(1)} collective-permute-done((f32[2,24,1152]{2,1,0:T(8,128)S(1)}, f32[2,24,1152]{2,1,0:T(8,128)S(1)}, u32[]{:S(2)}, u32[]{:S(2)}) %collective-permute-start.19) | collective-permute-done | bytes 221216 | tf_op jit(solution)/shard_map/ppermute | solution.py:547
  62.6 4.2 %shard_map.72 = f32[2,576,1152]{2,1,0:T(8,128)} custom-call(f32[2,576,1152]{2,1,0:T(8,128)S(1)} %shard_map.69.base, f32[2,576,1152]{2,1,0:T(8,128)S(1)} %get-tuple-element.47.refs_0_.refs_2_.refs_1_.y1, f32[432,128]{1,0:T(8,128)S(1)} %collective-permute-done.16.refs_0_, f32[432,128]{1,0:T(8,128)S(1)} %collective-permute-done.17.refs_1_, ...), custom_call_target="tpu_custom_call" | custom-call | flops 1000 | bytes 1000 | tf_op jit(solution)/shard_map/pallas_call | solution.py:528
  (45 shorter events, 9.7 us)
Async XLA Ops:
  4.4 14.4 %collective-permute-start.3 = (f32[288,128]{1,0:T(8,128)S(1)}, f32[288,128]{1,0:T(8,128)S(1)}, u32[]{:S(2)}, u32[]{:S(2)}) collective-permute-start(f32[288,128]{1,0:T(8,128)S(1)} %get-tuple-element.32), channel_id=1, source_target_pairs={{0,1},{2,3},{4,5},{6,7},{1,0},{3,2},{5,4},{7,6},{8,9},{10,11},{12,... | collective-permute-start | bytes 442376 | tf_op jit(solution)/shard_map/ppermute | solution.py:547
  5.5 3.8 %collective-permute-start = (f32[48,128]{1,0:T(8,128)S(1)}, f32[48,128]{1,0:T(8,128)S(1)}, u32[]{:S(2)}, u32[]{:S(2)}) collective-permute-start(f32[48,128]{1,0:T(8,128)S(1)} %get-tuple-element.30.known), channel_id=1, source_target_pairs={{0,32},{8,40},{16,48},{24,56},{64,96},{72,104},{80,112},{88,120},{... | collective-permute-start | bytes 73736 | tf_op jit(solution)/shard_map/ppermute | solution.py:547
  9.3 5.2 %collective-permute-start.1 = (f32[72,128]{1,0:T(8,128)S(1)}, f32[72,128]{1,0:T(8,128)S(1)}, u32[]{:S(2)}, u32[]{:S(2)}) collective-permute-start(f32[72,128]{1,0:T(8,128)S(1)} %shard_map.48.known), channel_id=1, source_target_pairs={{0,96},{8,104},{16,112},{24,120},{32,64},{40,72},{48,80},{56,88},{... | collective-permute-start | bytes 110600 | tf_op jit(solution)/shard_map/ppermute | solution.py:547
  12.1 13.3 %collective-permute-start.5 = (f32[432,128]{1,0:T(8,128)S(1)}, f32[432,128]{1,0:T(8,128)S(1)}, u32[]{:S(2)}, u32[]{:S(2)}) collective-permute-start(f32[432,128]{1,0:T(8,128)S(1)} %get-tuple-element.35), channel_id=1, source_target_pairs={{0,8},{1,9},{2,4},{3,5},{4,2},{5,3},{6,14},{7,15},{8,0},{9,1},{10,... | collective-permute-start | bytes 663560 | tf_op jit(solution)/shard_map/ppermute | solution.py:642
  14.5 4.3 %collective-permute-start.2 = (f32[120,128]{1,0:T(8,128)S(1)}, f32[120,128]{1,0:T(8,128)S(1)}, u32[]{:S(2)}, u32[]{:S(2)}) collective-permute-start(f32[120,128]{1,0:T(8,128)S(1)} %shard_map.49.known.refs_1_), channel_id=1, source_target_pairs={{0,8},{16,24},{32,40},{48,56},{64,72},{80,88},{96,104},{112,120},{... | collective-permute-start | bytes 184328 | tf_op jit(solution)/shard_map/ppermute | solution.py:547
  14.5 11.6 %collective-permute-start.6 = (f32[432,128]{1,0:T(8,128)S(1)}, f32[432,128]{1,0:T(8,128)S(1)}, u32[]{:S(2)}, u32[]{:S(2)}) collective-permute-start(f32[432,128]{1,0:T(8,128)S(1)} %get-tuple-element.36), channel_id=1, source_target_pairs={{0,2},{1,3},{4,6},{5,7},{2,0},{3,1},{6,4},{7,5},{8,10},{9,11},{12,... | collective-permute-start | bytes 663560 | tf_op jit(solution)/shard_map/ppermute | solution.py:547
  18.5 13.8 %collective-permute-start.8 = (f32[2,24,1152]{2,1,0:T(8,128)S(1)}, f32[2,24,1152]{2,1,0:T(8,128)S(1)}, u32[]{:S(2)}, u32[]{:S(2)}) collective-permute-start(f32[2,24,1152]{2,1,0:T(8,128)S(1)} %shard_map.54), channel_id=1, source_target_pairs={{0,32},{8,40},{16,48},{24,56},{64,96},{72,104},{80,112},{88,120},{... | collective-permute-start | bytes 663560 | tf_op jit(solution)/shard_map/ppermute | solution.py:547
  18.8 13.5 %collective-permute-start.9 = (f32[2,24,1152]{2,1,0:T(8,128)S(1)}, f32[2,24,1152]{2,1,0:T(8,128)S(1)}, u32[]{:S(2)}, u32[]{:S(2)}) collective-permute-start(f32[2,24,1152]{2,1,0:T(8,128)S(1)} %shard_map.55), channel_id=1, source_target_pairs={{0,96},{8,104},{16,112},{24,120},{32,64},{40,72},{48,80},{56,88},{... | collective-permute-start | bytes 663560 | tf_op jit(solution)/shard_map/ppermute | solution.py:547
  21.2 4.2 %collective-permute-start.4 = (f32[120,128]{1,0:T(8,128)S(1)}, f32[120,128]{1,0:T(8,128)S(1)}, u32[]{:S(2)}, u32[]{:S(2)}) collective-permute-start(f32[120,128]{1,0:T(8,128)S(1)} %shard_map.50.refs_0_.known.refs_1_), channel_id=1, source_target_pairs={{0,16},{8,24},{32,48},{40,56},{64,80},{72,88},{96,112},{104,120},{... | collective-permute-start | bytes 184328 | tf_op jit(solution)/shard_map/ppermute | solution.py:547
  26.1 6.1 %collective-permute-start.7 = (f32[120,128]{1,0:T(8,128)S(1)}, f32[120,128]{1,0:T(8,128)S(1)}, u32[]{:S(2)}, u32[]{:S(2)}) collective-permute-start(f32[120,128]{1,0:T(8,128)S(1)} %get-tuple-element.38), channel_id=1, source_target_pairs={{0,20},{1,21},{2,22},{3,23},{4,16},{5,17},{6,18},{7,19},{8,28},{9,... | collective-permute-start | bytes 184328 | tf_op jit(solution)/shard_map/ppermute | solution.py:642
  30.1 6.4 %collective-permute-start.11 = (f32[2,24,1152]{2,1,0:T(8,128)S(1)}, f32[2,24,1152]{2,1,0:T(8,128)S(1)}, u32[]{:S(2)}, u32[]{:S(2)}) collective-permute-start(f32[2,24,1152]{2,1,0:T(8,128)S(1)} %shard_map.58), channel_id=1, source_target_pairs={{0,32},{1,33},{2,34},{3,35},{4,36},{5,37},{6,38},{7,39},{8,16},{9,... | collective-permute-start | bytes 663560 | tf_op jit(solution)/shard_map/ppermute | solution.py:642
  32.3 9.4 %collective-permute-start.12 = (f32[2,24,1152]{2,1,0:T(8,128)S(1)}, f32[2,24,1152]{2,1,0:T(8,128)S(1)}, u32[]{:S(2)}, u32[]{:S(2)}) collective-permute-start(f32[2,24,1152]{2,1,0:T(8,128)S(1)} %shard_map.61), channel_id=1, source_target_pairs={{0,8},{16,24},{32,40},{48,56},{64,72},{80,88},{96,104},{112,120},{... | collective-permute-start | bytes 663560 | tf_op jit(solution)/shard_map/ppermute | solution.py:547
  32.4 4.0 %collective-permute-start.10 = (f32[72,128]{1,0:T(8,128)S(1)}, f32[72,128]{1,0:T(8,128)S(1)}, u32[]{:S(2)}, u32[]{:S(2)}) collective-permute-start(f32[72,128]{1,0:T(8,128)S(1)} %get-tuple-element.42), channel_id=1, source_target_pairs={{0,1},{2,3},{4,5},{6,7},{1,0},{3,2},{5,4},{7,6},{8,9},{10,11},{12,... | collective-permute-start | bytes 110600 | tf_op jit(solution)/shard_map/ppermute | solution.py:547
  36.5 5.3 %collective-permute-start.13 = (f32[48,128]{1,0:T(8,128)S(1)}, f32[48,128]{1,0:T(8,128)S(1)}, u32[]{:S(2)}, u32[]{:S(2)}) collective-permute-start(f32[48,128]{1,0:T(8,128)S(1)} %get-tuple-element.46), channel_id=1, source_target_pairs={{0,3},{1,2},{4,7},{5,6},{3,0},{2,1},{7,4},{6,5},{8,11},{9,10},{12,... | collective-permute-start | bytes 73736 | tf_op jit(solution)/shard_map/ppermute | solution.py:547
  46.5 5.7 %collective-permute-start.14 = (f32[2,24,1152]{2,1,0:T(8,128)S(1)}, f32[2,24,1152]{2,1,0:T(8,128)S(1)}, u32[]{:S(2)}, u32[]{:S(2)}) collective-permute-start(f32[2,24,1152]{2,1,0:T(8,128)S(1)} %get-tuple-element.48), channel_id=1, source_target_pairs={{0,8},{16,24},{32,40},{48,56},{64,72},{80,88},{96,104},{112,120},{... | collective-permute-start | bytes 663560 | tf_op jit(solution)/shard_map/ppermute | solution.py:547
  46.6 8.5 %collective-permute-start.15 = (f32[288,128]{1,0:T(8,128)S(1)}, f32[288,128]{1,0:T(8,128)S(1)}, u32[]{:S(2)}, u32[]{:S(2)}) collective-permute-start(f32[288,128]{1,0:T(8,128)S(1)} %get-tuple-element.49), channel_id=1, source_target_pairs={{0,1},{2,3},{4,5},{6,7},{1,0},{3,2},{5,4},{7,6},{8,9},{10,11},{12,... | collective-permute-start | bytes 442376 | tf_op jit(solution)/shard_map/ppermute | solution.py:547
  46.8 14.4 %collective-permute-start.16 = (f32[432,128]{1,0:T(8,128)S(1)}, f32[432,128]{1,0:T(8,128)S(1)}, u32[]{:S(2)}, u32[]{:S(2)}) collective-permute-start(f32[432,128]{1,0:T(8,128)S(1)} %get-tuple-element.50), channel_id=1, source_target_pairs={{0,2},{1,3},{4,6},{5,7},{2,0},{3,1},{6,4},{7,5},{8,10},{9,11},{12,... | collective-permute-start | bytes 663560 | tf_op jit(solution)/shard_map/ppermute | solution.py:547
  50.6 10.6 %collective-permute-start.17 = (f32[432,128]{1,0:T(8,128)S(1)}, f32[432,128]{1,0:T(8,128)S(1)}, u32[]{:S(2)}, u32[]{:S(2)}) collective-permute-start(f32[432,128]{1,0:T(8,128)S(1)} %get-tuple-element.51), channel_id=1, source_target_pairs={{0,8},{1,9},{2,4},{3,5},{4,2},{5,3},{6,14},{7,15},{8,0},{9,1},{10,... | collective-permute-start | bytes 663560 | tf_op jit(solution)/shard_map/ppermute | solution.py:642
  50.6 10.6 %collective-permute-start.20 = (f32[2,24,1152]{2,1,0:T(8,128)S(1)}, f32[2,24,1152]{2,1,0:T(8,128)S(1)}, u32[]{:S(2)}, u32[]{:S(2)}) collective-permute-start(f32[2,24,1152]{2,1,0:T(8,128)S(1)} %get-tuple-element.54), channel_id=1, source_target_pairs={{0,32},{1,33},{2,34},{3,35},{4,36},{5,37},{6,38},{7,39},{8,16},{9,... | collective-permute-start | bytes 663560 | tf_op jit(solution)/shard_map/ppermute | solution.py:642
  52.2 9.0 %collective-permute-start.18 = (f32[2,24,1152]{2,1,0:T(8,128)S(1)}, f32[2,24,1152]{2,1,0:T(8,128)S(1)}, u32[]{:S(2)}, u32[]{:S(2)}) collective-permute-start(f32[2,24,1152]{2,1,0:T(8,128)S(1)} %shard_map.70), channel_id=1, source_target_pairs={{0,32},{8,40},{16,48},{24,56},{64,96},{72,104},{80,112},{88,120},{... | collective-permute-start | bytes 663560 | tf_op jit(solution)/shard_map/ppermute | solution.py:547
  55.1 7.5 %collective-permute-start.19 = (f32[2,24,1152]{2,1,0:T(8,128)S(1)}, f32[2,24,1152]{2,1,0:T(8,128)S(1)}, u32[]{:S(2)}, u32[]{:S(2)}) collective-permute-start(f32[2,24,1152]{2,1,0:T(8,128)S(1)} %shard_map.71), channel_id=1, source_target_pairs={{0,96},{8,104},{16,112},{24,120},{32,64},{40,72},{48,80},{56,88},{... | collective-permute-start | bytes 663560 | tf_op jit(solution)/shard_map/ppermute | solution.py:547

commit v5 on v4

--- a/solution.py
+++ b/solution.py
@@ -676,12 +676,12 @@
     face_b = swap_face_b(face_b)
     face_a = swap_face_a(face_a)
     known = grow(share, flipped(share, "row", 4), first_work)
-    known = grow(known, flipped(known, "row", 12))
+    part = piece(0, None, known)
+    known = grow(known, flipped(known, "row", 12), part)
     down_a = swap_down_a(tie(down_a, known))
     known = added(known, flipped(known, "row", 1), side)
     down_b = swap_down_b(tie(down_b, known))
-    part = piece(0, None, known)
-    known, send = halve_all(known, flipped(known, "row", 2), part, face_b, face_a)
+    known, send = halve_all(known, flipped(known, "row", 2), face_a, face_b)
     across_b = swap_across_b(tie(across_b, known))
     part = piece(1, part, known)
     known, send = halve_four(known, swap_bits(send, 2, 4), part, down_a, down_b)
@@ -702,9 +702,9 @@
     side = swap_side(side)
     part = piece(0, None)
     down_a = swap_down_a(tie(down_a, part))
-    part = piece(1, part, across_a)
     down_b = swap_down_b(tie(down_b, part))
-    part = piece(2, part, side)
+    part = piece(1, part, across_a, side)
+    part = piece(2, part)
     part = piece(3, part)
     part = piece(4, part)
     part = piece(5, part)
@@ -738,7 +738,7 @@
         loads=True,
     )
     weights = (call(row_weights_kernel, (bonds,), on_chip(9, SQUARE, LANES)), colw)
-    part, halos = first_exchange(faces, share, weights[0], interior(False, y, y, weights, (0, 8, 12, 18, 24)))
+    part, halos = first_exchange(faces, share, weights[0], interior(False, y, y, weights, (0, 2, 8, 16, 24)))
     y1, *faces = call(middle_kernel, (part, y, *halos, *weights), [on_chip(*STATE), *faces_out], e_scratch)
     part, halos = second_exchange(faces, halos[-1], interior(True, y1, y, weights, (0, 4, 8, 12, 16, 20, 24)))
     return call(

time: 67.9 us -> 67.1 us (0.988); the launches traced: 67 us -> 67 us
  starting transfers between devices: 29.1 us -> 27.9 us
  waiting for transfers between devices: 8.34 us -> 9.34 us
    ppermute x16, starting transfers between devices: 23.7 us -> 20.7 us  [traded(): return lax.ppermute(block, axis, pairs(axis, linked))]
    ppermute x5, starting transfers between devices: 5.4 us -> 7.24 us  [swapped(): return lax.ppermute(x, ('row', 'col'), route)]
    ppermute x16, waiting for transfers between devices: 8.32 us -> 9.08 us  [traded(): return lax.ppermute(block, axis, pairs(axis, linked))]
  transfers between devices with their start and end apart: 21 -> 21, of which waited for: 7 -> 9; matrix products, arithmetic and copies ran while one was open for 0% -> 0% of each run, Pallas kernels for 24% -> 24%
where the time goes in v5:
time: 67.1 us; the launch traced here: 67 us
  Pallas kernels  29.2 us (44%)
  starting transfers between devices  27.9 us (42%)
  waiting for transfers between devices  9.34 us (14%)
    pallas_call x27, Pallas kernels, call(): pl.pallas_call(kernel, out_shape=out_shapes, in_specs=[pl.BlockSpec(memor...  29.2 us
    ppermute x16, starting transfers between devices, traded(): return lax.ppermute(block, axis, pairs(axis, linked))  20.7 us
    ppermute x16, waiting for transfers between devices, traded(): return lax.ppermute(block, axis, pairs(axis, linked))  9.08 us
    ppermute x5, starting transfers between devices, swapped(): return lax.ppermute(x, ('row', 'col'), route)  7.24 us
  transfers between devices with their start and end apart: 21, of which 9 were waited for; matrix products, arithmetic and copies ran while one was open for 0% of the time, Pallas kernels for 24%

profile of v5, /device:TPU:0, one launch (start us, length us, event | category | flops | bytes accessed | tf_op | source)
XLA Modules:
  0.0 67.0 jit_solution(8462208792756294190)
XLA Ops:
  0.0 4.4 %shard_map.46 = (f32[2,576,1152]{2,1,0:T(8,128)S(1)}, f32[3,96,96]{2,1,0:T(8,128)S(1)}, f32[17,8,1152]{2,1,0:T(8,128)S(1)}, f32[432,128]{1,0:T(8,128)S(1)}, f32[...) custom-call(f32[2,576,1152]{2,1,0:T(8,128)} %corr.1, ...), custom_call_target="tpu_custom_call" | custom-call | flops 1000 | bytes 1000 | tf_op jit(solution)/shard_map/pallas_call | solution.py:528
  5.5 1.5 %collective-permute-start = (f32[48,128]{1,0:T(8,128)S(1)}, f32[48,128]{1,0:T(8,128)S(1)}, u32[]{:S(2)}, u32[]{:S(2)}) collective-permute-start(f32[48,128]{1,0:T(8,128)S(1)} %get-tuple-element.30.known), channel_id=1, source_target_pairs={{0,32},{8,40},{16,48},{24,56},{64,96},{72,104},{80,112},{88,120},{... | collective-permute-start | bytes 73736 | tf_op jit(solution)/shard_map/ppermute | solution.py:547
  7.0 1.4 %shard_map.47.refs_0_.refs_3_.refs_4_.refs_8_.refs_2_.refs_5_ = f32[9,576,128]{2,1,0:T(8,128)S(1)} custom-call(f32[3,96,96]{2,1,0:T(8,128)S(1)} %get-tuple-element.31.bonds), custom_call_target="tpu_custom_call" | custom-call | flops 1000 | bytes 1000 | tf_op jit(solution)/shard_map/pallas_call | solution.py:528
  9.3 2.8 %collective-permute-start.1 = (f32[72,128]{1,0:T(8,128)S(1)}, f32[72,128]{1,0:T(8,128)S(1)}, u32[]{:S(2)}, u32[]{:S(2)}) collective-permute-start(f32[72,128]{1,0:T(8,128)S(1)} %shard_map.48.refs_0_.known), channel_id=1, source_target_pairs={{0,96},{8,104},{16,112},{24,120},{32,64},{40,72},{48,80},{56,88},{... | collective-permute-start | bytes 110600 | tf_op jit(solution)/shard_map/ppermute | solution.py:547
  12.1 3.6 %collective-permute-start.5 = (f32[432,128]{1,0:T(8,128)S(1)}, f32[432,128]{1,0:T(8,128)S(1)}, u32[]{:S(2)}, u32[]{:S(2)}) collective-permute-start(f32[432,128]{1,0:T(8,128)S(1)} %get-tuple-element.35), channel_id=1, source_target_pairs={{0,2},{1,3},{4,6},{5,7},{2,0},{3,1},{6,4},{7,5},{8,10},{9,11},{12,... | collective-permute-start | bytes 663560 | tf_op jit(solution)/shard_map/ppermute | solution.py:547
  18.6 2.4 %collective-permute-start.4 = (f32[120,128]{1,0:T(8,128)S(1)}, f32[120,128]{1,0:T(8,128)S(1)}, u32[]{:S(2)}, u32[]{:S(2)}) collective-permute-start(f32[120,128]{1,0:T(8,128)S(1)} %shard_map.51.known.refs_1_), channel_id=1, source_target_pairs={{0,16},{8,24},{32,48},{40,56},{64,80},{72,88},{96,112},{104,120},{... | collective-permute-start | bytes 184328 | tf_op jit(solution)/shard_map/ppermute | solution.py:547
  21.0 2.2 %collective-permute-done.4.got = f32[120,128]{1,0:T(8,128)S(1)} collective-permute-done((f32[120,128]{1,0:T(8,128)S(1)}, f32[120,128]{1,0:T(8,128)S(1)}, u32[]{:S(2)}, u32[]{:S(2)}) %collective-permute-start.4) | collective-permute-done | bytes 61472 | tf_op jit(solution)/shard_map/ppermute | solution.py:547
  23.9 6.2 %collective-permute-start.7 = (f32[120,128]{1,0:T(8,128)S(1)}, f32[120,128]{1,0:T(8,128)S(1)}, u32[]{:S(2)}, u32[]{:S(2)}) collective-permute-start(f32[120,128]{1,0:T(8,128)S(1)} %get-tuple-element.38), channel_id=1, source_target_pairs={{0,20},{1,21},{2,22},{3,23},{4,16},{5,17},{6,18},{7,19},{8,28},{9,... | collective-permute-start | bytes 184328 | tf_op jit(solution)/shard_map/ppermute | solution.py:642
  30.2 1.8 %shard_map.53.refs_0_ = f32[2,576,1152]{2,1,0:T(8,128)S(1)} custom-call(f32[2,576,1152]{2,1,0:T(8,128)S(1)} %shard_map.49.refs_0_, f32[120,128]{1,0:T(8,128)S(1)} %get-tuple-element.37.refs_1_.known, f32[2,576,1152]{2,1,0:T(8,128)S(1)} %get-tuple-element.32.refs_1_.refs_2_.refs_3_.y.refs_4_, ...), custom_call_target="tpu_custom_call", output_to_operand_aliasing={{}: (0, {})} | custom-call | flops 1000 | bytes 1000 | tf_op jit(solution)/shard_map/pallas_call | solution.py:528
  32.5 2.4 %shard_map.57.refs_0_ = f32[2,576,1152]{2,1,0:T(8,128)S(1)} custom-call(f32[2,576,1152]{2,1,0:T(8,128)S(1)} %shard_map.53.refs_0_, f32[72,128]{1,0:T(8,128)S(1)} %get-tuple-element.41.refs_1_.known, f32[2,576,1152]{2,1,0:T(8,128)S(1)} %get-tuple-element.32.refs_1_.refs_2_.refs_3_.y.refs_4_, ...), custom_call_target="tpu_custom_call", output_to_operand_aliasing={{}: (0, {})} | custom-call | flops 1000 | bytes 1000 | tf_op jit(solution)/shard_map/pallas_call | solution.py:528
  34.9 1.5 %collective-permute-done.10.got = f32[72,128]{1,0:T(8,128)S(1)} collective-permute-done((f32[72,128]{1,0:T(8,128)S(1)}, f32[72,128]{1,0:T(8,128)S(1)}, u32[]{:S(2)}, u32[]{:S(2)}) %collective-permute-start.10) | collective-permute-done | bytes 36896 | tf_op jit(solution)/shard_map/ppermute | solution.py:547
  36.5 1.7 %collective-permute-start.13 = (f32[48,128]{1,0:T(8,128)S(1)}, f32[48,128]{1,0:T(8,128)S(1)}, u32[]{:S(2)}, u32[]{:S(2)}) collective-permute-start(f32[48,128]{1,0:T(8,128)S(1)} %get-tuple-element.46), channel_id=1, source_target_pairs={{0,3},{1,2},{4,7},{5,6},{3,0},{2,1},{7,4},{6,5},{8,11},{9,10},{12,... | collective-permute-start | bytes 73736 | tf_op jit(solution)/shard_map/ppermute | solution.py:547
  38.2 2.4 %shard_map.60.refs_0_.base = f32[2,576,1152]{2,1,0:T(8,128)S(1)} custom-call(f32[2,576,1152]{2,1,0:T(8,128)S(1)} %shard_map.57.refs_0_, f32[48,128]{1,0:T(8,128)S(1)} %get-tuple-element.44.refs_1_.known, f32[2,576,1152]{2,1,0:T(8,128)S(1)} %get-tuple-element.32.refs_1_.refs_2_.refs_3_.y.refs_4_, ...), custom_call_target="tpu_custom_call", output_to_operand_aliasing={{}: (0, {})} | custom-call | flops 1000 | bytes 1000 | tf_op jit(solution)/shard_map/pallas_call | solution.py:528
  40.6 1.2 %collective-permute-done.13.got = f32[48,128]{1,0:T(8,128)S(1)} collective-permute-done((f32[48,128]{1,0:T(8,128)S(1)}, f32[48,128]{1,0:T(8,128)S(1)}, u32[]{:S(2)}, u32[]{:S(2)}) %collective-permute-start.13) | collective-permute-done | bytes 24608 | tf_op jit(solution)/shard_map/ppermute | solution.py:547
  41.8 4.7 %shard_map.63 = (f32[2,576,1152]{2,1,0:T(8,128)S(1)}, f32[432,128]{1,0:T(8,128)S(1)}, f32[432,128]{1,0:T(8,128)S(1)}, f32[288,128]{1,0:T(8,128)S(1)}, f32[2,24,1...) custom-call(f32[2,576,1152]{2,1,0:T(8,128)S(1)} %shard_map.60.refs_0_.ba, ...), custom_call_target="tpu_custom_call" | custom-call | flops 1000 | bytes 1000 | tf_op jit(solution)/shard_map/pallas_call | solution.py:528
  46.7 2.9 %collective-permute-start.16 = (f32[432,128]{1,0:T(8,128)S(1)}, f32[432,128]{1,0:T(8,128)S(1)}, u32[]{:S(2)}, u32[]{:S(2)}) collective-permute-start(f32[432,128]{1,0:T(8,128)S(1)} %get-tuple-element.50), channel_id=1, source_target_pairs={{0,2},{1,3},{4,6},{5,7},{2,0},{3,1},{6,4},{7,5},{8,10},{9,11},{12,... | collective-permute-start | bytes 663560 | tf_op jit(solution)/shard_map/ppermute | solution.py:547
  51.8 1.5 %collective-permute-done.15.refs_2_ = f32[288,128]{1,0:T(8,128)S(1)} collective-permute-done((f32[288,128]{1,0:T(8,128)S(1)}, f32[288,128]{1,0:T(8,128)S(1)}, u32[]{:S(2)}, u32[]{:S(2)}) %collective-permute-start.15) | collective-permute-done | bytes 147488 | tf_op jit(solution)/shard_map/ppermute | solution.py:547
  53.3 1.8 %collective-permute-start.18 = (f32[2,24,1152]{2,1,0:T(8,128)S(1)}, f32[2,24,1152]{2,1,0:T(8,128)S(1)}, u32[]{:S(2)}, u32[]{:S(2)}) collective-permute-start(f32[2,24,1152]{2,1,0:T(8,128)S(1)} %shard_map.70), channel_id=1, source_target_pairs={{0,32},{8,40},{16,48},{24,56},{64,96},{72,104},{80,112},{88,120},{... | collective-permute-start | bytes 663560 | tf_op jit(solution)/shard_map/ppermute | solution.py:547
  56.1 1.2 %shard_map.65.refs_0_ = f32[2,576,1152]{2,1,0:T(8,128)S(1)} custom-call(f32[2,576,1152]{2,1,0:T(8,128)S(1)} %shard_map.64.refs_0_.refs_1_, f32[2,24,1152]{2,1,0:T(8,128)S(1)} %collective-permute-done.14.refs_1_.refs_5_, f32[288,128]{1,0:T(8,128)S(1)} %collective-permute-done.15.refs_2_, ...), custom_call_target="tpu_custom_call", output_to_operand_aliasing={{}: (0, {})} | custom-call | flops 1000 | bytes 1000 | tf_op jit(solution)/shard_map/pallas_call | solution.py:528
  57.3 1.2 %shard_map.66.refs_0_ = f32[2,576,1152]{2,1,0:T(8,128)S(1)} custom-call(f32[2,576,1152]{2,1,0:T(8,128)S(1)} %shard_map.65.refs_0_, f32[2,576,1152]{2,1,0:T(8,128)S(1)} %get-tuple-element.47.refs_0_.refs_3_.refs_1_.y1, f32[2,576,1152]{2,1,0:T(8,128)S(1)} %get-tuple-element.32.refs_1_.refs_2_.refs_3_.y.refs_4_, ...), custom_call_target="tpu_custom_call", output_to_operand_aliasing={{}: (0, {})} | custom-call | flops 1000 | bytes 1000 | tf_op jit(solution)/shard_map/pallas_call | solution.py:528
  58.4 1.2 %shard_map.67.refs_0_ = f32[2,576,1152]{2,1,0:T(8,128)S(1)} custom-call(f32[2,576,1152]{2,1,0:T(8,128)S(1)} %shard_map.66.refs_0_, f32[2,576,1152]{2,1,0:T(8,128)S(1)} %get-tuple-element.47.refs_0_.refs_3_.refs_1_.y1, f32[2,576,1152]{2,1,0:T(8,128)S(1)} %get-tuple-element.32.refs_1_.refs_2_.refs_3_.y.refs_4_, ...), custom_call_target="tpu_custom_call", output_to_operand_aliasing={{}: (0, {})} | custom-call | flops 1000 | bytes 1000 | tf_op jit(solution)/shard_map/pallas_call | solution.py:528
  59.6 1.2 %shard_map.68.refs_0_ = f32[2,576,1152]{2,1,0:T(8,128)S(1)} custom-call(f32[2,576,1152]{2,1,0:T(8,128)S(1)} %shard_map.67.refs_0_, f32[2,576,1152]{2,1,0:T(8,128)S(1)} %get-tuple-element.47.refs_0_.refs_3_.refs_1_.y1, f32[2,576,1152]{2,1,0:T(8,128)S(1)} %get-tuple-element.32.refs_1_.refs_2_.refs_3_.y.refs_4_, ...), custom_call_target="tpu_custom_call", output_to_operand_aliasing={{}: (0, {})} | custom-call | flops 1000 | bytes 1000 | tf_op jit(solution)/shard_map/pallas_call | solution.py:528
  60.8 1.2 %shard_map.69.base = f32[2,576,1152]{2,1,0:T(8,128)S(1)} custom-call(f32[2,576,1152]{2,1,0:T(8,128)S(1)} %shard_map.68.refs_0_, f32[2,576,1152]{2,1,0:T(8,128)S(1)} %get-tuple-element.47.refs_0_.refs_3_.refs_1_.y1, f32[2,576,1152]{2,1,0:T(8,128)S(1)} %get-tuple-element.32.refs_1_.refs_2_.refs_3_.y.refs_4_, ...), custom_call_target="tpu_custom_call", output_to_operand_aliasing={{}: (0, {})} | custom-call | flops 1000 | bytes 1000 | tf_op jit(solution)/shard_map/pallas_call | solution.py:528
  62.6 4.2 %shard_map.72 = f32[2,576,1152]{2,1,0:T(8,128)} custom-call(f32[2,576,1152]{2,1,0:T(8,128)S(1)} %shard_map.69.base, f32[2,576,1152]{2,1,0:T(8,128)S(1)} %get-tuple-element.47.refs_0_.refs_3_.refs_1_.y1, f32[432,128]{1,0:T(8,128)S(1)} %collective-permute-done.16.refs_0_, f32[432,128]{1,0:T(8,128)S(1)} %collective-permute-done.17.refs_1_, ...), custom_call_target="tpu_custom_call" | custom-call | flops 1000 | bytes 1000 | tf_op jit(solution)/shard_map/pallas_call | solution.py:528
  (45 shorter events, 10.0 us)
Async XLA Ops:
  4.4 13.4 %collective-permute-start.3 = (f32[288,128]{1,0:T(8,128)S(1)}, f32[288,128]{1,0:T(8,128)S(1)}, u32[]{:S(2)}, u32[]{:S(2)}) collective-permute-start(f32[288,128]{1,0:T(8,128)S(1)} %get-tuple-element.34), channel_id=1, source_target_pairs={{0,1},{2,3},{4,5},{6,7},{1,0},{3,2},{5,4},{7,6},{8,9},{10,11},{12,... | collective-permute-start | bytes 442376 | tf_op jit(solution)/shard_map/ppermute | solution.py:547
  5.5 3.8 %collective-permute-start = (f32[48,128]{1,0:T(8,128)S(1)}, f32[48,128]{1,0:T(8,128)S(1)}, u32[]{:S(2)}, u32[]{:S(2)}) collective-permute-start(f32[48,128]{1,0:T(8,128)S(1)} %get-tuple-element.30.known), channel_id=1, source_target_pairs={{0,32},{8,40},{16,48},{24,56},{64,96},{72,104},{80,112},{88,120},{... | collective-permute-start | bytes 73736 | tf_op jit(solution)/shard_map/ppermute | solution.py:547
  9.3 7.0 %collective-permute-start.1 = (f32[72,128]{1,0:T(8,128)S(1)}, f32[72,128]{1,0:T(8,128)S(1)}, u32[]{:S(2)}, u32[]{:S(2)}) collective-permute-start(f32[72,128]{1,0:T(8,128)S(1)} %shard_map.48.refs_0_.known), channel_id=1, source_target_pairs={{0,96},{8,104},{16,112},{24,120},{32,64},{40,72},{48,80},{56,88},{... | collective-permute-start | bytes 110600 | tf_op jit(solution)/shard_map/ppermute | solution.py:547
  12.1 11.8 %collective-permute-start.5 = (f32[432,128]{1,0:T(8,128)S(1)}, f32[432,128]{1,0:T(8,128)S(1)}, u32[]{:S(2)}, u32[]{:S(2)}) collective-permute-start(f32[432,128]{1,0:T(8,128)S(1)} %get-tuple-element.35), channel_id=1, source_target_pairs={{0,2},{1,3},{4,6},{5,7},{2,0},{3,1},{6,4},{7,5},{8,10},{9,11},{12,... | collective-permute-start | bytes 663560 | tf_op jit(solution)/shard_map/ppermute | solution.py:547
  15.7 8.2 %collective-permute-start.6 = (f32[432,128]{1,0:T(8,128)S(1)}, f32[432,128]{1,0:T(8,128)S(1)}, u32[]{:S(2)}, u32[]{:S(2)}) collective-permute-start(f32[432,128]{1,0:T(8,128)S(1)} %get-tuple-element.36), channel_id=1, source_target_pairs={{0,8},{1,9},{2,4},{3,5},{4,2},{5,3},{6,14},{7,15},{8,0},{9,1},{10,... | collective-permute-start | bytes 663560 | tf_op jit(solution)/shard_map/ppermute | solution.py:642
  16.3 1.5 %collective-permute-start.2 = (f32[120,128]{1,0:T(8,128)S(1)}, f32[120,128]{1,0:T(8,128)S(1)}, u32[]{:S(2)}, u32[]{:S(2)}) collective-permute-start(f32[120,128]{1,0:T(8,128)S(1)} %shard_map.50.known.refs_1_), channel_id=1, source_target_pairs={{0,8},{16,24},{32,40},{48,56},{64,72},{80,88},{96,104},{112,120},{... | collective-permute-start | bytes 184328 | tf_op jit(solution)/shard_map/ppermute | solution.py:547
  16.9 15.3 %collective-permute-start.8 = (f32[2,24,1152]{2,1,0:T(8,128)S(1)}, f32[2,24,1152]{2,1,0:T(8,128)S(1)}, u32[]{:S(2)}, u32[]{:S(2)}) collective-permute-start(f32[2,24,1152]{2,1,0:T(8,128)S(1)} %shard_map.54), channel_id=1, source_target_pairs={{0,32},{8,40},{16,48},{24,56},{64,96},{72,104},{80,112},{88,120},{... | collective-permute-start | bytes 663560 | tf_op jit(solution)/shard_map/ppermute | solution.py:547
  17.9 14.4 %collective-permute-start.9 = (f32[2,24,1152]{2,1,0:T(8,128)S(1)}, f32[2,24,1152]{2,1,0:T(8,128)S(1)}, u32[]{:S(2)}, u32[]{:S(2)}) collective-permute-start(f32[2,24,1152]{2,1,0:T(8,128)S(1)} %shard_map.55), channel_id=1, source_target_pairs={{0,96},{8,104},{16,112},{24,120},{32,64},{40,72},{48,80},{56,88},{... | collective-permute-start | bytes 663560 | tf_op jit(solution)/shard_map/ppermute | solution.py:547
  18.6 4.6 %collective-permute-start.4 = (f32[120,128]{1,0:T(8,128)S(1)}, f32[120,128]{1,0:T(8,128)S(1)}, u32[]{:S(2)}, u32[]{:S(2)}) collective-permute-start(f32[120,128]{1,0:T(8,128)S(1)} %shard_map.51.known.refs_1_), channel_id=1, source_target_pairs={{0,16},{8,24},{32,48},{40,56},{64,80},{72,88},{96,112},{104,120},{... | collective-permute-start | bytes 184328 | tf_op jit(solution)/shard_map/ppermute | solution.py:547
  23.9 8.4 %collective-permute-start.7 = (f32[120,128]{1,0:T(8,128)S(1)}, f32[120,128]{1,0:T(8,128)S(1)}, u32[]{:S(2)}, u32[]{:S(2)}) collective-permute-start(f32[120,128]{1,0:T(8,128)S(1)} %get-tuple-element.38), channel_id=1, source_target_pairs={{0,20},{1,21},{2,22},{3,23},{4,16},{5,17},{6,18},{7,19},{8,28},{9,... | collective-permute-start | bytes 184328 | tf_op jit(solution)/shard_map/ppermute | solution.py:642
  30.1 6.4 %collective-permute-start.11 = (f32[2,24,1152]{2,1,0:T(8,128)S(1)}, f32[2,24,1152]{2,1,0:T(8,128)S(1)}, u32[]{:S(2)}, u32[]{:S(2)}) collective-permute-start(f32[2,24,1152]{2,1,0:T(8,128)S(1)} %shard_map.58), channel_id=1, source_target_pairs={{0,32},{1,33},{2,34},{3,35},{4,36},{5,37},{6,38},{7,39},{8,16},{9,... | collective-permute-start | bytes 663560 | tf_op jit(solution)/shard_map/ppermute | solution.py:642
  32.3 9.4 %collective-permute-start.12 = (f32[2,24,1152]{2,1,0:T(8,128)S(1)}, f32[2,24,1152]{2,1,0:T(8,128)S(1)}, u32[]{:S(2)}, u32[]{:S(2)}) collective-permute-start(f32[2,24,1152]{2,1,0:T(8,128)S(1)} %shard_map.61), channel_id=1, source_target_pairs={{0,8},{16,24},{32,40},{48,56},{64,72},{80,88},{96,104},{112,120},{... | collective-permute-start | bytes 663560 | tf_op jit(solution)/shard_map/ppermute | solution.py:547
  32.4 4.0 %collective-permute-start.10 = (f32[72,128]{1,0:T(8,128)S(1)}, f32[72,128]{1,0:T(8,128)S(1)}, u32[]{:S(2)}, u32[]{:S(2)}) collective-permute-start(f32[72,128]{1,0:T(8,128)S(1)} %get-tuple-element.42), channel_id=1, source_target_pairs={{0,1},{2,3},{4,5},{6,7},{1,0},{3,2},{5,4},{7,6},{8,9},{10,11},{12,... | collective-permute-start | bytes 110600 | tf_op jit(solution)/shard_map/ppermute | solution.py:547
  36.5 5.3 %collective-permute-start.13 = (f32[48,128]{1,0:T(8,128)S(1)}, f32[48,128]{1,0:T(8,128)S(1)}, u32[]{:S(2)}, u32[]{:S(2)}) collective-permute-start(f32[48,128]{1,0:T(8,128)S(1)} %get-tuple-element.46), channel_id=1, source_target_pairs={{0,3},{1,2},{4,7},{5,6},{3,0},{2,1},{7,4},{6,5},{8,11},{9,10},{12,... | collective-permute-start | bytes 73736 | tf_op jit(solution)/shard_map/ppermute | solution.py:547
  46.5 8.6 %collective-permute-start.14 = (f32[2,24,1152]{2,1,0:T(8,128)S(1)}, f32[2,24,1152]{2,1,0:T(8,128)S(1)}, u32[]{:S(2)}, u32[]{:S(2)}) collective-permute-start(f32[2,24,1152]{2,1,0:T(8,128)S(1)} %get-tuple-element.48), channel_id=1, source_target_pairs={{0,8},{16,24},{32,40},{48,56},{64,72},{80,88},{96,104},{112,120},{... | collective-permute-start | bytes 663560 | tf_op jit(solution)/shard_map/ppermute | solution.py:547
  46.6 6.7 %collective-permute-start.15 = (f32[288,128]{1,0:T(8,128)S(1)}, f32[288,128]{1,0:T(8,128)S(1)}, u32[]{:S(2)}, u32[]{:S(2)}) collective-permute-start(f32[288,128]{1,0:T(8,128)S(1)} %get-tuple-element.49), channel_id=1, source_target_pairs={{0,1},{2,3},{4,5},{6,7},{1,0},{3,2},{5,4},{7,6},{8,9},{10,11},{12,... | collective-permute-start | bytes 442376 | tf_op jit(solution)/shard_map/ppermute | solution.py:547
  46.7 15.3 %collective-permute-start.16 = (f32[432,128]{1,0:T(8,128)S(1)}, f32[432,128]{1,0:T(8,128)S(1)}, u32[]{:S(2)}, u32[]{:S(2)}) collective-permute-start(f32[432,128]{1,0:T(8,128)S(1)} %get-tuple-element.50), channel_id=1, source_target_pairs={{0,2},{1,3},{4,6},{5,7},{2,0},{3,1},{6,4},{7,5},{8,10},{9,11},{12,... | collective-permute-start | bytes 663560 | tf_op jit(solution)/shard_map/ppermute | solution.py:547
  49.6 12.4 %collective-permute-start.17 = (f32[432,128]{1,0:T(8,128)S(1)}, f32[432,128]{1,0:T(8,128)S(1)}, u32[]{:S(2)}, u32[]{:S(2)}) collective-permute-start(f32[432,128]{1,0:T(8,128)S(1)} %get-tuple-element.51), channel_id=1, source_target_pairs={{0,8},{1,9},{2,4},{3,5},{4,2},{5,3},{6,14},{7,15},{8,0},{9,1},{10,... | collective-permute-start | bytes 663560 | tf_op jit(solution)/shard_map/ppermute | solution.py:642
  49.6 12.4 %collective-permute-start.20 = (f32[2,24,1152]{2,1,0:T(8,128)S(1)}, f32[2,24,1152]{2,1,0:T(8,128)S(1)}, u32[]{:S(2)}, u32[]{:S(2)}) collective-permute-start(f32[2,24,1152]{2,1,0:T(8,128)S(1)} %get-tuple-element.54), channel_id=1, source_target_pairs={{0,32},{1,33},{2,34},{3,35},{4,36},{5,37},{6,38},{7,39},{8,16},{9,... | collective-permute-start | bytes 663560 | tf_op jit(solution)/shard_map/ppermute | solution.py:642
  53.3 8.7 %collective-permute-start.18 = (f32[2,24,1152]{2,1,0:T(8,128)S(1)}, f32[2,24,1152]{2,1,0:T(8,128)S(1)}, u32[]{:S(2)}, u32[]{:S(2)}) collective-permute-start(f32[2,24,1152]{2,1,0:T(8,128)S(1)} %shard_map.70), channel_id=1, source_target_pairs={{0,32},{8,40},{16,48},{24,56},{64,96},{72,104},{80,112},{88,120},{... | collective-permute-start | bytes 663560 | tf_op jit(solution)/shard_map/ppermute | solution.py:547
  55.1 7.4 %collective-permute-start.19 = (f32[2,24,1152]{2,1,0:T(8,128)S(1)}, f32[2,24,1152]{2,1,0:T(8,128)S(1)}, u32[]{:S(2)}, u32[]{:S(2)}) collective-permute-start(f32[2,24,1152]{2,1,0:T(8,128)S(1)} %shard_map.71), channel_id=1, source_target_pairs={{0,96},{8,104},{16,112},{24,120},{32,64},{40,72},{48,80},{56,88},{... | collective-permute-start | bytes 663560 | tf_op jit(solution)/shard_map/ppermute | solution.py:547

commit v6 on v5

--- a/solution.py
+++ b/solution.py
@@ -396,7 +396,7 @@
             strip(a, p)
         return carry
 
-    lax.fori_loop(first, last, step, 0, unroll=next(n for n in (4, 3, 2, 1) if (last - first) % n == 0))
+    lax.fori_loop(first, last, step, 0, unroll=next(n for n in (5, 4, 3, 2, 1) if (last - first) % n == 0))
 
 
 def unfolded(msg, at, lane):
@@ -738,7 +738,7 @@
         loads=True,
     )
     weights = (call(row_weights_kernel, (bonds,), on_chip(9, SQUARE, LANES)), colw)
-    part, halos = first_exchange(faces, share, weights[0], interior(False, y, y, weights, (0, 2, 8, 16, 24)))
+    part, halos = first_exchange(faces, share, weights[0], interior(False, y, y, weights, (0, 1, 5, 14, 24)))
     y1, *faces = call(middle_kernel, (part, y, *halos, *weights), [on_chip(*STATE), *faces_out], e_scratch)
     part, halos = second_exchange(faces, halos[-1], interior(True, y1, y, weights, (0, 4, 8, 12, 16, 20, 24)))
     return call(

time: 67.1 us -> 67.9 us (1.012)
  the two profiles are of different devices: /device:TPU:0 before, /device:TPU:24 now
where the time goes in v6:
time: 67.9 us; the launch traced here: 67.8 us
  Pallas kernels  28.2 us (42%)
  waiting for transfers between devices  22.1 us (33%)
  starting transfers between devices  16.9 us (25%)
    pallas_call x27, Pallas kernels, call(): pl.pallas_call(kernel, out_shape=out_shapes, in_specs=[pl.BlockSpec(memor...  28.2 us
    ppermute x16, starting transfers between devices, traded(): return lax.ppermute(block, axis, pairs(axis, linked))  16.1 us
    ppermute x16, waiting for transfers between devices, traded(): return lax.ppermute(block, axis, pairs(axis, linked))  14.6 us
    ppermute x5, waiting for transfers between devices, swapped(): return lax.ppermute(x, ('row', 'col'), route)  7.51 us
  transfers between devices with their start and end apart: 21, of which 9 were waited for; matrix products, arithmetic and copies ran while one was open for 0% of the time, Pallas kernels for 23%

profile of v6, /device:TPU:24, one launch (start us, length us, event | category | flops | bytes accessed | tf_op | source)
XLA Modules:
  0.0 67.8 jit_solution(8531953343261082683)
XLA Ops:
  0.0 3.4 %shard_map.46 = (f32[2,576,1152]{2,1,0:T(8,128)S(1)}, f32[3,96,96]{2,1,0:T(8,128)S(1)}, f32[17,8,1152]{2,1,0:T(8,128)S(1)}, f32[432,128]{1,0:T(8,128)S(1)}, f32[...) custom-call(f32[2,576,1152]{2,1,0:T(8,128)} %corr.1, ...), custom_call_target="tpu_custom_call" | custom-call | flops 1000 | bytes 1000 | tf_op jit(solution)/shard_map/pallas_call | solution.py:528
  3.4 2.0 %collective-permute-start.3 = (f32[288,128]{1,0:T(8,128)S(1)}, f32[288,128]{1,0:T(8,128)S(1)}, u32[]{:S(2)}, u32[]{:S(2)}) collective-permute-start(f32[288,128]{1,0:T(8,128)S(1)} %get-tuple-element.34), channel_id=1, source_target_pairs={{0,1},{2,3},{4,5},{6,7},{1,0},{3,2},{5,4},{7,6},{8,9},{10,11},{12,... | collective-permute-start | bytes 442376 | tf_op jit(solution)/shard_map/ppermute | solution.py:547
  5.4 1.7 %collective-permute-start = (f32[48,128]{1,0:T(8,128)S(1)}, f32[48,128]{1,0:T(8,128)S(1)}, u32[]{:S(2)}, u32[]{:S(2)}) collective-permute-start(f32[48,128]{1,0:T(8,128)S(1)} %get-tuple-element.30.known), channel_id=1, source_target_pairs={{0,32},{8,40},{16,48},{24,56},{64,96},{72,104},{80,112},{88,120},{... | collective-permute-start | bytes 73736 | tf_op jit(solution)/shard_map/ppermute | solution.py:547
  7.1 1.4 %shard_map.47.refs_0_.refs_3_.refs_4_.refs_8_.refs_2_.refs_5_ = f32[9,576,128]{2,1,0:T(8,128)S(1)} custom-call(f32[3,96,96]{2,1,0:T(8,128)S(1)} %get-tuple-element.31.bonds), custom_call_target="tpu_custom_call" | custom-call | flops 1000 | bytes 1000 | tf_op jit(solution)/shard_map/pallas_call | solution.py:528
  9.3 3.0 %collective-permute-start.1 = (f32[72,128]{1,0:T(8,128)S(1)}, f32[72,128]{1,0:T(8,128)S(1)}, u32[]{:S(2)}, u32[]{:S(2)}) collective-permute-start(f32[72,128]{1,0:T(8,128)S(1)} %shard_map.48.refs_0_.known), channel_id=1, source_target_pairs={{0,96},{8,104},{16,112},{24,120},{32,64},{40,72},{48,80},{56,88},{... | collective-permute-start | bytes 110600 | tf_op jit(solution)/shard_map/ppermute | solution.py:547
  12.2 4.3 %collective-permute-start.5 = (f32[432,128]{1,0:T(8,128)S(1)}, f32[432,128]{1,0:T(8,128)S(1)}, u32[]{:S(2)}, u32[]{:S(2)}) collective-permute-start(f32[432,128]{1,0:T(8,128)S(1)} %get-tuple-element.35), channel_id=1, source_target_pairs={{0,2},{1,3},{4,6},{5,7},{2,0},{3,1},{6,4},{7,5},{8,10},{9,11},{12,... | collective-permute-start | bytes 663560 | tf_op jit(solution)/shard_map/ppermute | solution.py:547
  18.3 1.2 %collective-permute-start.9 = (f32[2,24,1152]{2,1,0:T(8,128)S(1)}, f32[2,24,1152]{2,1,0:T(8,128)S(1)}, u32[]{:S(2)}, u32[]{:S(2)}) collective-permute-start(f32[2,24,1152]{2,1,0:T(8,128)S(1)} %shard_map.55), channel_id=1, source_target_pairs={{0,96},{8,104},{16,112},{24,120},{32,64},{40,72},{48,80},{56,88},{... | collective-permute-start | bytes 663560 | tf_op jit(solution)/shard_map/ppermute | solution.py:547
  19.5 4.2 %collective-permute-done.4.got = f32[120,128]{1,0:T(8,128)S(1)} collective-permute-done((f32[120,128]{1,0:T(8,128)S(1)}, f32[120,128]{1,0:T(8,128)S(1)}, u32[]{:S(2)}, u32[]{:S(2)}) %collective-permute-start.4) | collective-permute-done | bytes 61472 | tf_op jit(solution)/shard_map/ppermute | solution.py:547
  23.7 3.4 %collective-permute-done.6.refs_1_ = f32[432,128]{1,0:T(8,128)S(1)} collective-permute-done((f32[432,128]{1,0:T(8,128)S(1)}, f32[432,128]{1,0:T(8,128)S(1)}, u32[]{:S(2)}, u32[]{:S(2)}) %collective-permute-start.6) | collective-permute-done | bytes 221216 | tf_op jit(solution)/shard_map/ppermute | solution.py:642
  28.5 4.1 %collective-permute-done.7.got = f32[120,128]{1,0:T(8,128)S(1)} collective-permute-done((f32[120,128]{1,0:T(8,128)S(1)}, f32[120,128]{1,0:T(8,128)S(1)}, u32[]{:S(2)}, u32[]{:S(2)}) %collective-permute-start.7) | collective-permute-done | bytes 61472 | tf_op jit(solution)/shard_map/ppermute | solution.py:642
  32.9 2.8 %shard_map.57.refs_0_ = f32[2,576,1152]{2,1,0:T(8,128)S(1)} custom-call(f32[2,576,1152]{2,1,0:T(8,128)S(1)} %shard_map.53.refs_0_, f32[72,128]{1,0:T(8,128)S(1)} %get-tuple-element.41.refs_1_.known, f32[2,576,1152]{2,1,0:T(8,128)S(1)} %get-tuple-element.32.refs_1_.refs_2_.refs_3_.y.refs_4_, ...), custom_call_target="tpu_custom_call", output_to_operand_aliasing={{}: (0, {})} | custom-call | flops 1000 | bytes 1000 | tf_op jit(solution)/shard_map/pallas_call | solution.py:528
  35.6 1.2 %collective-permute-done.10.got = f32[72,128]{1,0:T(8,128)S(1)} collective-permute-done((f32[72,128]{1,0:T(8,128)S(1)}, f32[72,128]{1,0:T(8,128)S(1)}, u32[]{:S(2)}, u32[]{:S(2)}) %collective-permute-start.10) | collective-permute-done | bytes 36896 | tf_op jit(solution)/shard_map/ppermute | solution.py:547
  37.1 3.0 %shard_map.60.refs_0_.base = f32[2,576,1152]{2,1,0:T(8,128)S(1)} custom-call(f32[2,576,1152]{2,1,0:T(8,128)S(1)} %shard_map.57.refs_0_, f32[48,128]{1,0:T(8,128)S(1)} %get-tuple-element.44.refs_1_.known, f32[2,576,1152]{2,1,0:T(8,128)S(1)} %get-tuple-element.32.refs_1_.refs_2_.refs_3_.y.refs_4_, ...), custom_call_target="tpu_custom_call", output_to_operand_aliasing={{}: (0, {})} | custom-call | flops 1000 | bytes 1000 | tf_op jit(solution)/shard_map/pallas_call | solution.py:528
  40.1 2.0 %collective-permute-done.13.got = f32[48,128]{1,0:T(8,128)S(1)} collective-permute-done((f32[48,128]{1,0:T(8,128)S(1)}, f32[48,128]{1,0:T(8,128)S(1)}, u32[]{:S(2)}, u32[]{:S(2)}) %collective-permute-start.13) | collective-permute-done | bytes 24608 | tf_op jit(solution)/shard_map/ppermute | solution.py:547
  42.1 4.7 %shard_map.63 = (f32[2,576,1152]{2,1,0:T(8,128)S(1)}, f32[432,128]{1,0:T(8,128)S(1)}, f32[432,128]{1,0:T(8,128)S(1)}, f32[288,128]{1,0:T(8,128)S(1)}, f32[2,24,1...) custom-call(f32[2,576,1152]{2,1,0:T(8,128)S(1)} %shard_map.60.refs_0_.ba, ...), custom_call_target="tpu_custom_call" | custom-call | flops 1000 | bytes 1000 | tf_op jit(solution)/shard_map/pallas_call | solution.py:528
  47.0 2.7 %collective-permute-start.16 = (f32[432,128]{1,0:T(8,128)S(1)}, f32[432,128]{1,0:T(8,128)S(1)}, u32[]{:S(2)}, u32[]{:S(2)}) collective-permute-start(f32[432,128]{1,0:T(8,128)S(1)} %get-tuple-element.50), channel_id=1, source_target_pairs={{0,2},{1,3},{4,6},{5,7},{2,0},{3,1},{6,4},{7,5},{8,10},{9,11},{12,... | collective-permute-start | bytes 663560 | tf_op jit(solution)/shard_map/ppermute | solution.py:547
  51.5 2.1 %collective-permute-done.15.refs_2_ = f32[288,128]{1,0:T(8,128)S(1)} collective-permute-done((f32[288,128]{1,0:T(8,128)S(1)}, f32[288,128]{1,0:T(8,128)S(1)}, u32[]{:S(2)}, u32[]{:S(2)}) %collective-permute-start.15) | collective-permute-done | bytes 147488 | tf_op jit(solution)/shard_map/ppermute | solution.py:547
  54.0 1.2 %shard_map.65.refs_0_ = f32[2,576,1152]{2,1,0:T(8,128)S(1)} custom-call(f32[2,576,1152]{2,1,0:T(8,128)S(1)} %shard_map.64.refs_0_.refs_1_, f32[2,24,1152]{2,1,0:T(8,128)S(1)} %collective-permute-done.14.refs_1_.refs_5_, f32[288,128]{1,0:T(8,128)S(1)} %collective-permute-done.15.refs_2_, ...), custom_call_target="tpu_custom_call", output_to_operand_aliasing={{}: (0, {})} | custom-call | flops 1000 | bytes 1000 | tf_op jit(solution)/shard_map/pallas_call | solution.py:528
  55.2 1.2 %shard_map.66.refs_0_ = f32[2,576,1152]{2,1,0:T(8,128)S(1)} custom-call(f32[2,576,1152]{2,1,0:T(8,128)S(1)} %shard_map.65.refs_0_, f32[2,576,1152]{2,1,0:T(8,128)S(1)} %get-tuple-element.47.refs_0_.refs_3_.refs_1_.y1, f32[2,576,1152]{2,1,0:T(8,128)S(1)} %get-tuple-element.32.refs_1_.refs_2_.refs_3_.y.refs_4_, ...), custom_call_target="tpu_custom_call", output_to_operand_aliasing={{}: (0, {})} | custom-call | flops 1000 | bytes 1000 | tf_op jit(solution)/shard_map/pallas_call | solution.py:528
  56.4 1.2 %shard_map.67.refs_0_ = f32[2,576,1152]{2,1,0:T(8,128)S(1)} custom-call(f32[2,576,1152]{2,1,0:T(8,128)S(1)} %shard_map.66.refs_0_, f32[2,576,1152]{2,1,0:T(8,128)S(1)} %get-tuple-element.47.refs_0_.refs_3_.refs_1_.y1, f32[2,576,1152]{2,1,0:T(8,128)S(1)} %get-tuple-element.32.refs_1_.refs_2_.refs_3_.y.refs_4_, ...), custom_call_target="tpu_custom_call", output_to_operand_aliasing={{}: (0, {})} | custom-call | flops 1000 | bytes 1000 | tf_op jit(solution)/shard_map/pallas_call | solution.py:528
  57.6 1.2 %shard_map.68.refs_0_ = f32[2,576,1152]{2,1,0:T(8,128)S(1)} custom-call(f32[2,576,1152]{2,1,0:T(8,128)S(1)} %shard_map.67.refs_0_, f32[2,576,1152]{2,1,0:T(8,128)S(1)} %get-tuple-element.47.refs_0_.refs_3_.refs_1_.y1, f32[2,576,1152]{2,1,0:T(8,128)S(1)} %get-tuple-element.32.refs_1_.refs_2_.refs_3_.y.refs_4_, ...), custom_call_target="tpu_custom_call", output_to_operand_aliasing={{}: (0, {})} | custom-call | flops 1000 | bytes 1000 | tf_op jit(solution)/shard_map/pallas_call | solution.py:528
  58.8 1.2 %shard_map.69.base = f32[2,576,1152]{2,1,0:T(8,128)S(1)} custom-call(f32[2,576,1152]{2,1,0:T(8,128)S(1)} %shard_map.68.refs_0_, f32[2,576,1152]{2,1,0:T(8,128)S(1)} %get-tuple-element.47.refs_0_.refs_3_.refs_1_.y1, f32[2,576,1152]{2,1,0:T(8,128)S(1)} %get-tuple-element.32.refs_1_.refs_2_.refs_3_.y.refs_4_, ...), custom_call_target="tpu_custom_call", output_to_operand_aliasing={{}: (0, {})} | custom-call | flops 1000 | bytes 1000 | tf_op jit(solution)/shard_map/pallas_call | solution.py:528
  59.9 3.4 %collective-permute-done.16.refs_0_ = f32[432,128]{1,0:T(8,128)S(1)} collective-permute-done((f32[432,128]{1,0:T(8,128)S(1)}, f32[432,128]{1,0:T(8,128)S(1)}, u32[]{:S(2)}, u32[]{:S(2)}) %collective-permute-start.16) | collective-permute-done | bytes 221216 | tf_op jit(solution)/shard_map/ppermute | solution.py:547
  63.4 4.2 %shard_map.72 = f32[2,576,1152]{2,1,0:T(8,128)} custom-call(f32[2,576,1152]{2,1,0:T(8,128)S(1)} %shard_map.69.base, f32[2,576,1152]{2,1,0:T(8,128)S(1)} %get-tuple-element.47.refs_0_.refs_3_.refs_1_.y1, f32[432,128]{1,0:T(8,128)S(1)} %collective-permute-done.16.refs_0_, f32[432,128]{1,0:T(8,128)S(1)} %collective-permute-done.17.refs_1_, ...), custom_call_target="tpu_custom_call" | custom-call | flops 1000 | bytes 1000 | tf_op jit(solution)/shard_map/pallas_call | solution.py:528
  (45 shorter events, 6.6 us)
Async XLA Ops:
  3.4 14.8 %collective-permute-start.3 = (f32[288,128]{1,0:T(8,128)S(1)}, f32[288,128]{1,0:T(8,128)S(1)}, u32[]{:S(2)}, u32[]{:S(2)}) collective-permute-start(f32[288,128]{1,0:T(8,128)S(1)} %get-tuple-element.34), channel_id=1, source_target_pairs={{0,1},{2,3},{4,5},{6,7},{1,0},{3,2},{5,4},{7,6},{8,9},{10,11},{12,... | collective-permute-start | bytes 442376 | tf_op jit(solution)/shard_map/ppermute | solution.py:547
  5.4 3.8 %collective-permute-start = (f32[48,128]{1,0:T(8,128)S(1)}, f32[48,128]{1,0:T(8,128)S(1)}, u32[]{:S(2)}, u32[]{:S(2)}) collective-permute-start(f32[48,128]{1,0:T(8,128)S(1)} %get-tuple-element.30.known), channel_id=1, source_target_pairs={{0,32},{8,40},{16,48},{24,56},{64,96},{72,104},{80,112},{88,120},{... | collective-permute-start | bytes 73736 | tf_op jit(solution)/shard_map/ppermute | solution.py:547
  9.3 7.7 %collective-permute-start.1 = (f32[72,128]{1,0:T(8,128)S(1)}, f32[72,128]{1,0:T(8,128)S(1)}, u32[]{:S(2)}, u32[]{:S(2)}) collective-permute-start(f32[72,128]{1,0:T(8,128)S(1)} %shard_map.48.refs_0_.known), channel_id=1, source_target_pairs={{0,96},{8,104},{16,112},{24,120},{32,64},{40,72},{48,80},{56,88},{... | collective-permute-start | bytes 110600 | tf_op jit(solution)/shard_map/ppermute | solution.py:547
  12.2 11.5 %collective-permute-start.5 = (f32[432,128]{1,0:T(8,128)S(1)}, f32[432,128]{1,0:T(8,128)S(1)}, u32[]{:S(2)}, u32[]{:S(2)}) collective-permute-start(f32[432,128]{1,0:T(8,128)S(1)} %get-tuple-element.35), channel_id=1, source_target_pairs={{0,2},{1,3},{4,6},{5,7},{2,0},{3,1},{6,4},{7,5},{8,10},{9,11},{12,... | collective-permute-start | bytes 663560 | tf_op jit(solution)/shard_map/ppermute | solution.py:547
  16.6 10.5 %collective-permute-start.6 = (f32[432,128]{1,0:T(8,128)S(1)}, f32[432,128]{1,0:T(8,128)S(1)}, u32[]{:S(2)}, u32[]{:S(2)}) collective-permute-start(f32[432,128]{1,0:T(8,128)S(1)} %get-tuple-element.36), channel_id=1, source_target_pairs={{0,8},{1,9},{2,4},{3,5},{4,2},{5,3},{6,14},{7,15},{8,0},{9,1},{10,... | collective-permute-start | bytes 663560 | tf_op jit(solution)/shard_map/ppermute | solution.py:642
  16.9 1.3 %collective-permute-start.2 = (f32[120,128]{1,0:T(8,128)S(1)}, f32[120,128]{1,0:T(8,128)S(1)}, u32[]{:S(2)}, u32[]{:S(2)}) collective-permute-start(f32[120,128]{1,0:T(8,128)S(1)} %shard_map.50.known.refs_1_), channel_id=1, source_target_pairs={{0,8},{16,24},{32,40},{48,56},{64,72},{80,88},{96,104},{112,120},{... | collective-permute-start | bytes 184328 | tf_op jit(solution)/shard_map/ppermute | solution.py:547
  17.1 15.6 %collective-permute-start.8 = (f32[2,24,1152]{2,1,0:T(8,128)S(1)}, f32[2,24,1152]{2,1,0:T(8,128)S(1)}, u32[]{:S(2)}, u32[]{:S(2)}) collective-permute-start(f32[2,24,1152]{2,1,0:T(8,128)S(1)} %shard_map.54), channel_id=1, source_target_pairs={{0,32},{8,40},{16,48},{24,56},{64,96},{72,104},{80,112},{88,120},{... | collective-permute-start | bytes 663560 | tf_op jit(solution)/shard_map/ppermute | solution.py:547
  18.3 14.3 %collective-permute-start.9 = (f32[2,24,1152]{2,1,0:T(8,128)S(1)}, f32[2,24,1152]{2,1,0:T(8,128)S(1)}, u32[]{:S(2)}, u32[]{:S(2)}) collective-permute-start(f32[2,24,1152]{2,1,0:T(8,128)S(1)} %shard_map.55), channel_id=1, source_target_pairs={{0,96},{8,104},{16,112},{24,120},{32,64},{40,72},{48,80},{56,88},{... | collective-permute-start | bytes 663560 | tf_op jit(solution)/shard_map/ppermute | solution.py:547
  19.5 4.2 %collective-permute-start.4 = (f32[120,128]{1,0:T(8,128)S(1)}, f32[120,128]{1,0:T(8,128)S(1)}, u32[]{:S(2)}, u32[]{:S(2)}) collective-permute-start(f32[120,128]{1,0:T(8,128)S(1)} %shard_map.51.known.refs_1_), channel_id=1, source_target_pairs={{0,16},{8,24},{32,48},{40,56},{64,80},{72,88},{96,112},{104,120},{... | collective-permute-start | bytes 184328 | tf_op jit(solution)/shard_map/ppermute | solution.py:547
  27.1 5.5 %collective-permute-start.7 = (f32[120,128]{1,0:T(8,128)S(1)}, f32[120,128]{1,0:T(8,128)S(1)}, u32[]{:S(2)}, u32[]{:S(2)}) collective-permute-start(f32[120,128]{1,0:T(8,128)S(1)} %get-tuple-element.38), channel_id=1, source_target_pairs={{0,20},{1,21},{2,22},{3,23},{4,16},{5,17},{6,18},{7,19},{8,28},{9,... | collective-permute-start | bytes 184328 | tf_op jit(solution)/shard_map/ppermute | solution.py:642
  27.2 9.6 %collective-permute-start.11 = (f32[2,24,1152]{2,1,0:T(8,128)S(1)}, f32[2,24,1152]{2,1,0:T(8,128)S(1)}, u32[]{:S(2)}, u32[]{:S(2)}) collective-permute-start(f32[2,24,1152]{2,1,0:T(8,128)S(1)} %shard_map.58), channel_id=1, source_target_pairs={{0,32},{1,33},{2,34},{3,35},{4,36},{5,37},{6,38},{7,39},{8,16},{9,... | collective-permute-start | bytes 663560 | tf_op jit(solution)/shard_map/ppermute | solution.py:642
  32.7 9.4 %collective-permute-start.12 = (f32[2,24,1152]{2,1,0:T(8,128)S(1)}, f32[2,24,1152]{2,1,0:T(8,128)S(1)}, u32[]{:S(2)}, u32[]{:S(2)}) collective-permute-start(f32[2,24,1152]{2,1,0:T(8,128)S(1)} %shard_map.61), channel_id=1, source_target_pairs={{0,8},{16,24},{32,40},{48,56},{64,72},{80,88},{96,104},{112,120},{... | collective-permute-start | bytes 663560 | tf_op jit(solution)/shard_map/ppermute | solution.py:547
  32.8 4.0 %collective-permute-start.10 = (f32[72,128]{1,0:T(8,128)S(1)}, f32[72,128]{1,0:T(8,128)S(1)}, u32[]{:S(2)}, u32[]{:S(2)}) collective-permute-start(f32[72,128]{1,0:T(8,128)S(1)} %get-tuple-element.42), channel_id=1, source_target_pairs={{0,1},{2,3},{4,5},{6,7},{1,0},{3,2},{5,4},{7,6},{8,9},{10,11},{12,... | collective-permute-start | bytes 110600 | tf_op jit(solution)/shard_map/ppermute | solution.py:547
  36.8 5.3 %collective-permute-start.13 = (f32[48,128]{1,0:T(8,128)S(1)}, f32[48,128]{1,0:T(8,128)S(1)}, u32[]{:S(2)}, u32[]{:S(2)}) collective-permute-start(f32[48,128]{1,0:T(8,128)S(1)} %get-tuple-element.46), channel_id=1, source_target_pairs={{0,3},{1,2},{4,7},{5,6},{3,0},{2,1},{7,4},{6,5},{8,11},{9,10},{12,... | collective-permute-start | bytes 73736 | tf_op jit(solution)/shard_map/ppermute | solution.py:547
  46.8 6.8 %collective-permute-start.14 = (f32[2,24,1152]{2,1,0:T(8,128)S(1)}, f32[2,24,1152]{2,1,0:T(8,128)S(1)}, u32[]{:S(2)}, u32[]{:S(2)}) collective-permute-start(f32[2,24,1152]{2,1,0:T(8,128)S(1)} %get-tuple-element.48), channel_id=1, source_target_pairs={{0,8},{16,24},{32,40},{48,56},{64,72},{80,88},{96,104},{112,120},{... | collective-permute-start | bytes 663560 | tf_op jit(solution)/shard_map/ppermute | solution.py:547
  46.9 6.7 %collective-permute-start.15 = (f32[288,128]{1,0:T(8,128)S(1)}, f32[288,128]{1,0:T(8,128)S(1)}, u32[]{:S(2)}, u32[]{:S(2)}) collective-permute-start(f32[288,128]{1,0:T(8,128)S(1)} %get-tuple-element.49), channel_id=1, source_target_pairs={{0,1},{2,3},{4,5},{6,7},{1,0},{3,2},{5,4},{7,6},{8,9},{10,11},{12,... | collective-permute-start | bytes 442376 | tf_op jit(solution)/shard_map/ppermute | solution.py:547
  47.0 16.3 %collective-permute-start.16 = (f32[432,128]{1,0:T(8,128)S(1)}, f32[432,128]{1,0:T(8,128)S(1)}, u32[]{:S(2)}, u32[]{:S(2)}) collective-permute-start(f32[432,128]{1,0:T(8,128)S(1)} %get-tuple-element.50), channel_id=1, source_target_pairs={{0,2},{1,3},{4,6},{5,7},{2,0},{3,1},{6,4},{7,5},{8,10},{9,11},{12,... | collective-permute-start | bytes 663560 | tf_op jit(solution)/shard_map/ppermute | solution.py:547
  49.7 13.6 %collective-permute-start.17 = (f32[432,128]{1,0:T(8,128)S(1)}, f32[432,128]{1,0:T(8,128)S(1)}, u32[]{:S(2)}, u32[]{:S(2)}) collective-permute-start(f32[432,128]{1,0:T(8,128)S(1)} %get-tuple-element.51), channel_id=1, source_target_pairs={{0,8},{1,9},{2,4},{3,5},{4,2},{5,3},{6,14},{7,15},{8,0},{9,1},{10,... | collective-permute-start | bytes 663560 | tf_op jit(solution)/shard_map/ppermute | solution.py:642
  49.7 13.6 %collective-permute-start.20 = (f32[2,24,1152]{2,1,0:T(8,128)S(1)}, f32[2,24,1152]{2,1,0:T(8,128)S(1)}, u32[]{:S(2)}, u32[]{:S(2)}) collective-permute-start(f32[2,24,1152]{2,1,0:T(8,128)S(1)} %get-tuple-element.54), channel_id=1, source_target_pairs={{0,32},{1,33},{2,34},{3,35},{4,36},{5,37},{6,38},{7,39},{8,16},{9,... | collective-permute-start | bytes 663560 | tf_op jit(solution)/shard_map/ppermute | solution.py:642
  53.7 9.7 %collective-permute-start.18 = (f32[2,24,1152]{2,1,0:T(8,128)S(1)}, f32[2,24,1152]{2,1,0:T(8,128)S(1)}, u32[]{:S(2)}, u32[]{:S(2)}) collective-permute-start(f32[2,24,1152]{2,1,0:T(8,128)S(1)} %shard_map.70), channel_id=1, source_target_pairs={{0,32},{8,40},{16,48},{24,56},{64,96},{72,104},{80,112},{88,120},{... | collective-permute-start | bytes 663560 | tf_op jit(solution)/shard_map/ppermute | solution.py:547
  53.7 9.7 %collective-permute-start.19 = (f32[2,24,1152]{2,1,0:T(8,128)S(1)}, f32[2,24,1152]{2,1,0:T(8,128)S(1)}, u32[]{:S(2)}, u32[]{:S(2)}) collective-permute-start(f32[2,24,1152]{2,1,0:T(8,128)S(1)} %shard_map.71), channel_id=1, source_target_pairs={{0,96},{8,104},{16,112},{24,120},{32,64},{40,72},{48,80},{56,88},{... | collective-permute-start | bytes 663560 | tf_op jit(solution)/shard_map/ppermute | solution.py:547
